TPU v7x, 32 devices: a whole 2x2x4 slice. The times are simulated.
32 devices in a mesh: mem: 8 (over z, x), fsdp: 4 (over y, core).
Axes of the slice: x: 2, y: 2, z: 4, core: 2. Of those that a mesh axis runs over, the one named last changes fastest.
Arguments:
- queries: bfloat16 [8192, 1024], P(('mem', 'fsdp')), may hold values from -10 to 10
- keys: bfloat16 [8192, 1024], P(('mem', 'fsdp')), may hold values from -7 to 7
- values: bfloat16 [8192, 1024], P(('mem', 'fsdp')), may hold values from -6 to 6
- mem_keys: bfloat16 [32768, 1024], P('mem', 'fsdp'), may hold values from -7 to 7
- mem_values: bfloat16 [32768, 1024], P('mem', 'fsdp'), may hold values from -6 to 6
- block_ids: int32 [16, 4, 8], replicated, may hold values from 0 to 255, as said below
- gate_bias: float32 [16], replicated, may hold values from -2 to 2
- out_weight: bfloat16 [1024, 2048], P('fsdp'), may hold values from -0.59765625 to 0.59765625
- cotangent: bfloat16 [8192, 2048], P(('mem', 'fsdp')), may hold values from -6 to 6
Outputs:
- projected: bfloat16 [8192, 2048], P(('mem', 'fsdp'))
- query_grad: bfloat16 [8192, 1024], P(('mem', 'fsdp'))
- key_grad: bfloat16 [8192, 1024], P(('mem', 'fsdp'))
- value_grad: bfloat16 [8192, 1024], P(('mem', 'fsdp'))
- weight_grad: float32 [1024, 2048], P('fsdp', 'mem')
Inputs may be any that keep to these rules, and one draw needn't show every extreme that they name: `block_ids`: within one segment the 32 ids are distinct, at most 8 of them lie in the blocks of one index of mem (id // 32), and some index of mem has exactly 8 of them in every segment.
All inputs are finite; a program needn't handle non-finite values.
Results may differ from a plain program's by a relative error of at most 0.022.
Values may be sent and summed in bfloat16 or wider, within the bound.
No kernel may reach another device: no remote copies, remote signals or barrier semaphores. Data moves between devices by JAX's collectives and lax.ppermute only.
A program may use at most 192 MiB of HBM per device.

v0:
```python
import functools

import jax
import jax.numpy as jnp
from jax import lax
from jax.experimental import pallas as pl
from jax.experimental.pallas import tpu as pltpu
from jax.sharding import PartitionSpec as P

DH = 64
QBLK = 128
MBLK = 128
LOW = -1e30
UNROLL = 4
HALVES = 1
ORDER = True
VMEM = 58 * 2**20
SCALE = DH ** (-0.5)
BF = jnp.bfloat16
F32 = jnp.float32
NT = (((1,), (1,)), ((), ()))
NN = (((1,), (0,)), ((), ()))
TN = (((0,), (0,)), ((), ()))


def dot(a, b, dims):
    return lax.dot_general(a, b, dims, preferred_element_type=F32)


def spread(x):
    zero = jnp.zeros((DH, QBLK), x.dtype)
    upper = jnp.concatenate([x[:DH], zero], axis=1)
    lower = jnp.concatenate([zero, x[DH:]], axis=1)
    return jnp.concatenate([upper, lower], axis=0)


def query_block(ref, b, t):
    per = ref.shape[2] // QBLK
    return ref[b // per, t * 128 : (t + 1) * 128, (b % per) * QBLK : (b % per + 1) * QBLK]


def folded(x, op):
    return op(x.reshape(x.shape[0] // 8, 8, x.shape[1]), axis=0)


def own_blocks(parts):
    rows = []
    for part in parts:
        rows.append(part[:DH, :QBLK])
        rows.append(part[DH:, QBLK:])
    return rows


def at_slot(slot, last, column=0):
    def index(s, b, *_):
        return (jnp.where(s == slot, b, jnp.where(s > slot, last, 0)), column, 0)

    return index


def start_step(group, half, slot, memory, buffers, sems, sides):
    rows, width = buffers[0].shape
    rows = rows // 2

    @pl.when((slot == 0) & (pl.program_id(1) == 0))
    def _():
        own = pl.ds(half * width, width)
        sources = [memory[0].at[:, own], memory[1], memory[2].at[:, own], memory[3]]
        targets = [buffers[i].at[pl.ds(j * rows, rows)] for i in range(2) for j in range(2)]
        copies = [
            pltpu.make_async_copy(source, target, sems.at[i])
            for i, (source, target) in enumerate(zip(sources, targets))
        ]
        for copy in copies:
            copy.start()
        for _, out in sides:
            out[...] = jnp.zeros_like(out)
        for copy in copies:
            copy.wait()

    for i in range(group):

        @pl.when(slot == i)
        def _():
            for refs, out in sides:
                for b in range(out.shape[0] - 1):
                    for t in range(out.shape[1]):
                        x = query_block(refs[i], b, t)
                        out[b, t, :DH, :QBLK] = x[:DH]
                        out[b, t, DH:, QBLK:] = x[DH:]


def memory_forward(
    group, pairs, half, counts, places, homes, k_own, k_par, v_own, v_par, *rest
):
    q_refs = rest[:group]
    o_refs = rest[group : 2 * group]
    exact_refs = rest[2 * group : 3 * group]
    lse_ref = rest[3 * group]
    kbuf, vbuf, q_t, scores, tops, norms, acc, sems = rest[3 * group + 1 :]
    slot = pl.program_id(0)
    number = slot * pl.num_programs(1) + pl.program_id(1)
    cap = scores.shape[0]
    blocks = q_t.shape[0] - 1
    start_step(
        group, half, slot, (k_own, k_par, v_own, v_par), (kbuf, vbuf), sems, [(q_refs, q_t)]
    )
    tops[...] = jnp.full(tops.shape, LOW, F32)
    norms[...] = jnp.zeros_like(norms)
    acc[...] = jnp.zeros_like(acc)
    turns = (counts[number] + UNROLL - 1) // UNROLL

    def first(turn, carry):
        found = []
        for u in range(UNROLL):
            j = turn * UNROLL + u
            row = pl.multiple_of(places[number * cap + j] * MBLK, MBLK)
            b = homes[number * cap + j]
            for t in range(pairs):
                cols = slice(t * 128, (t + 1) * 128)
                s = dot(kbuf[pl.ds(row, MBLK), cols], q_t[b, t], NN)
                scores[j, t] = s
                found.append((b, t, folded(s, jnp.max)))
        for b, t, top in found:
            tops[b, t] = jnp.maximum(tops[b, t], top)
        return carry

    lax.fori_loop(0, turns, first, 0)
    tops[...] = jnp.broadcast_to(jnp.max(tops[...], axis=2, keepdims=True), tops.shape)

    def second(turn, carry):
        found = []
        for u in range(UNROLL):
            j = turn * UNROLL + u
            row = pl.multiple_of(places[number * cap + j] * MBLK, MBLK)
            b = homes[number * cap + j]
            for t in range(pairs):
                cols = slice(t * 128, (t + 1) * 128)
                p = jnp.exp(scores[j, t] - tops[b, t, 0:1, :])
                o = dot(vbuf[pl.ds(row, MBLK), cols], p.astype(BF), TN)
                found.append((b, t, folded(p, jnp.sum), o))
        for b, t, norm, o in found:
            norms[b, t] += norm
            acc[b, t] += o
        return carry

    lax.fori_loop(0, turns, second, 0)
    results = []
    for b in range(blocks):
        parts = []
        for t in range(pairs):
            wide = slice(t * 256, (t + 1) * 256)
            norm = jnp.sum(norms[b, t], axis=0, keepdims=True)
            some = norm > 0.0
            safe = jnp.where(some, norm, 1.0)
            lse_ref[0, b, :, wide] = jnp.where(some, tops[b, t, 0:1, :] + jnp.log(safe), LOW)
            parts.append(acc[b, t] * (1.0 / safe))
        results.append(jnp.concatenate(own_blocks(parts), axis=0))
    for i in range(group):

        @pl.when(slot == i)
        def _():
            for b in range(blocks):
                exact_refs[i][b] = results[b]
                o_refs[i][b] = results[b].astype(BF)


def statistics_kernel(group, heads, lse_ref, *rest):
    do_refs, o_refs, stat_ref = rest[:group], rest[group : 2 * group], rest[2 * group]
    for i in range(group):
        for b in range(lse_ref.shape[1]):
            stat_ref[i, b, 0:1, :] = lse_ref[i, b]
            for t in range(heads // 2):
                do = query_block(do_refs[i], b, t).astype(F32)
                product = do * o_refs[i][b, t * 128 : (t + 1) * 128, :]
                for h in range(2):
                    at = slice((2 * t + h) * QBLK, (2 * t + h + 1) * QBLK)
                    stat_ref[i, b, 1:2, at] = jnp.sum(
                        product[h * DH : (h + 1) * DH], axis=0, keepdims=True
                    )


def merged(stat_refs, b):
    lses = [ref[0, b, 0:1, :] for ref in stat_refs]
    top = functools.reduce(jnp.maximum, lses)
    shares = [jnp.exp(x - top) for x in lses]
    norm = functools.reduce(jnp.add, shares)
    return top, shares, norm


def memory_backward(
    group, pairs, half, counts, places, homes, k_own, k_par, v_own, v_par, *rest
):
    q_refs = rest[:group]
    do_refs = rest[group : 2 * group]
    stat_refs = rest[2 * group : 3 * group]
    dq_refs = rest[3 * group : 4 * group]
    kbuf, vbuf, q_t, do_t, weights, lses, means, acc, sems = rest[4 * group :]
    slot = pl.program_id(0)
    number = slot * pl.num_programs(1) + pl.program_id(1)
    cap = places.shape[0] // counts.shape[0]
    blocks = q_t.shape[0] - 1
    start_step(
        group, half, slot, (k_own, k_par, v_own, v_par), (kbuf, vbuf), sems,
        [(q_refs, q_t), (do_refs, do_t)],
    )
    lses[...] = jnp.zeros_like(lses)
    means[...] = jnp.zeros_like(means)
    for b in range(blocks):
        top, shares, norm = merged(stat_refs, b)
        lse = top + jnp.log(norm)
        mean = functools.reduce(
            jnp.add, [x * ref[0, b, 1:2, :] for x, ref in zip(shares, stat_refs)]
        ) / norm
        for t in range(pairs):
            wide = slice(t * 256, (t + 1) * 256)
            lses[b, t] = lse[:, wide]
            means[b, t] = mean[:, wide]
    acc[...] = jnp.zeros_like(acc)

    turns = (counts[number] + UNROLL - 1) // UNROLL

    def first(turn, carry):
        for u in range(UNROLL):
            j = turn * UNROLL + u
            row = pl.multiple_of(places[number * cap + j] * MBLK, MBLK)
            b = homes[number * cap + j]
            for t in range(pairs):
                cols = slice(t * 128, (t + 1) * 128)
                s = dot(kbuf[pl.ds(row, MBLK), cols], q_t[b, t], NN)
                weights[j, t] = jnp.exp(s - lses[b, t])
        return carry

    lax.fori_loop(0, turns, first, 0)

    def second(turn, carry):
        found = []
        for u in range(UNROLL):
            j = turn * UNROLL + u
            row = pl.multiple_of(places[number * cap + j] * MBLK, MBLK)
            b = homes[number * cap + j]
            for t in range(pairs):
                cols = slice(t * 128, (t + 1) * 128)
                slope = dot(vbuf[pl.ds(row, MBLK), cols], do_t[b, t], NN)
                delta = weights[j, t] * (slope - means[b, t])
                found.append((b, t, dot(kbuf[pl.ds(row, MBLK), cols], delta.astype(BF), TN)))
        for b, t, dq in found:
            acc[b, t] += dq
        return carry

    lax.fori_loop(0, turns, second, 0)
    results = [
        jnp.concatenate(own_blocks([acc[b, t] for t in range(pairs)]), axis=0).astype(BF)
        for b in range(blocks)
    ]
    for i in range(group):

        @pl.when(slot == i)
        def _():
            for b in range(blocks):
                dq_refs[i][b] = results[b]


def local_kernel(pairs, blocks, halves, gate, q_ref, k_ref, v_ref, *rest):
    do_refs = rest[:halves]
    o_ref, dq_ref, dk_ref, dv_ref, dk_acc, dv_acc = rest[halves:]
    per_half = pairs // halves
    dk_acc[...] = jnp.zeros_like(dk_acc)
    dv_acc[...] = jnp.zeros_like(dv_acc)
    key_at = lax.broadcasted_iota(jnp.int32, (MBLK, 2 * QBLK), 0)
    query_at = lax.broadcasted_iota(jnp.int32, (MBLK, 2 * QBLK), 1) % QBLK
    causal = key_at <= query_at
    lane = lax.broadcasted_iota(jnp.int32, (1, 128), 1)
    shares = []
    for t in range(pairs):
        shares.append(jnp.where(lane < DH, 1.0 - gate[2 * t], 1.0 - gate[2 * t + 1]))
    for t in range(pairs):
        cols = slice(t * 128, (t + 1) * 128)
        for b in range(blocks):
            q = spread(query_block(q_ref, b, t))
            do = spread(query_block(do_refs[t // per_half], b, t % per_half))
            scores, slopes = [], []
            for n in range(b + 1):
                rows = slice(n * MBLK, (n + 1) * MBLK)
                s = dot(k_ref[rows, cols], q, NN)
                scores.append(jnp.where(causal, s, LOW) if n == b else s)
                slopes.append(dot(v_ref[rows, cols], do, NN))
            largest = functools.reduce(jnp.maximum, [folded(s, jnp.max) for s in scores])
            largest = jnp.max(largest, axis=0, keepdims=True)
            weights = [jnp.exp(s - largest) for s in scores]
            norm = functools.reduce(jnp.add, [folded(p, jnp.sum) for p in weights])
            inverse = 1.0 / jnp.sum(norm, axis=0, keepdims=True)
            weights = [p * inverse for p in weights]
            mean = functools.reduce(
                jnp.add, [folded(p * x, jnp.sum) for p, x in zip(weights, slopes)]
            )
            mean = jnp.sum(mean, axis=0, keepdims=True)
            o = jnp.zeros((128, 256), F32)
            dq = jnp.zeros((128, 256), F32)
            for n in range(b + 1):
                rows = slice(n * MBLK, (n + 1) * MBLK)
                w = weights[n].astype(BF)
                delta = (weights[n] * (slopes[n] - mean)).astype(BF)
                o += dot(v_ref[rows, cols], w, TN)
                dq += dot(k_ref[rows, cols], delta, TN)
                dv_acc[rows, cols] += dot(w, do, NT)
                dk_acc[rows, cols] += dot(delta, q, NT)
            o_pair, dq_pair = own_blocks([o]), own_blocks([dq])
            for i in range(2):
                share = 1.0 - gate[2 * t + i]
                at = slice((2 * t + i) * DH, (2 * t + i + 1) * DH)
                o_ref[b, at, :] = o_pair[i] * share
                dq_ref[b, at, :] = dq_pair[i] * (share * SCALE)
        dk_ref[:, cols] = (dk_acc[:, cols] * shares[t]).astype(BF)
        dv_ref[:, cols] = (dv_acc[:, cols] * shares[t]).astype(BF)


def attention_kernel(group, heads, first, gate, local_ref, *rest):
    o_refs = rest[:group]
    stat_refs = rest[group : 2 * group]
    out_ref, out_t_ref = rest[2 * group :]
    for b in range(local_ref.shape[0]):
        _, shares, norm = merged(stat_refs, b)
        rows = []
        for h in range(heads):
            at = slice(h * DH, (h + 1) * DH)
            wide = slice(h * QBLK, (h + 1) * QBLK)
            total = functools.reduce(
                jnp.add,
                [x[:, wide] * ref[b, at, :].astype(F32) for x, ref in zip(shares, o_refs)],
            )
            rows.append(total * (gate[first + h] / norm[:, wide]) + local_ref[b, at, :])
        result = jnp.concatenate(rows, axis=0).astype(BF)
        out_t_ref[:, b * QBLK : (b + 1) * QBLK] = result
        out_ref[b * QBLK : (b + 1) * QBLK, :] = result.T


def query_grad_kernel(group, heads, first, gate, local_ref, *rest):
    dq_refs = rest[:group]
    out_ref = rest[group]
    for b in range(local_ref.shape[0]):
        rows = []
        for h in range(heads):
            at = slice(h * DH, (h + 1) * DH)
            total = functools.reduce(jnp.add, [ref[b, at, :].astype(F32) for ref in dq_refs])
            rows.append(total * (gate[first + h] * SCALE) + local_ref[b, at, :])
        result = jnp.concatenate(rows, axis=0).astype(BF)
        out_ref[b * QBLK : (b + 1) * QBLK, :] = result.T


def attention_grad_kernel(order, weight_ref, *rest):
    part_refs, out_refs = rest[:4], rest[4:]
    for i in range(4):
        grad = dot(weight_ref[...], part_refs[i][...], NT).astype(BF)
        rows = grad.shape[0] // len(out_refs)
        for j, out_ref in enumerate(out_refs):
            out_ref[order[i]] = grad[j * rows : (j + 1) * rows]


def weight_grad_kernel(order, dests, attention_ref, *rest):
    part_refs, (send_ref, keep_ref) = rest[:4], rest[4:]
    tokens = part_refs[0].shape[0]
    columns = part_refs[0].shape[1] // 2
    total = None
    for i in range(4):
        at = pl.multiple_of(order[i] * tokens, tokens)
        term = dot(attention_ref[:, pl.ds(at, tokens)], part_refs[i][...], NN)
        total = term if total is None else total + term
    total = total.astype(BF)
    side = dests[dests.shape[0] - 1]

    @pl.when(side == 0)
    def _():
        keep_ref[0] = total[:, :columns]
        send_ref[0] = total[:, columns:]

    @pl.when(side == 1)
    def _():
        keep_ref[0] = total[:, columns:]
        send_ref[0] = total[:, :columns]


ANY = pl.BlockSpec(memory_space=pl.ANY)
SMEM = pl.BlockSpec(memory_space=pltpu.SMEM)


def block_lists(block_ids, me, group, seg_dev, per_dev, cap):
    segments, per_seg, retr = block_ids.shape
    asked = per_seg * retr
    z = me // 2
    ids = block_ids.reshape(segments // (2 * seg_dev), 2, seg_dev, asked)
    ids = lax.dynamic_index_in_dim(ids, me % 2, 1, keepdims=False)
    slots = (z - jnp.arange(group, dtype=jnp.int32)) % group
    ids = jnp.take(ids, slots, axis=0).reshape(group * seg_dev, asked)
    owners = ids // per_dev
    here = owners // 2 == z
    place = ids - owners * per_dev + jnp.where(owners == me, 0, per_dev)
    position = jnp.arange(asked, dtype=jnp.int32)
    before = (position[None, :] < position[:, None])[None]
    rank = jnp.sum(jnp.logical_and(before, here[:, None, :]), axis=-1)
    chosen = jnp.logical_and(
        here[:, :, None], rank[:, :, None] == jnp.arange(cap, dtype=jnp.int32)
    )
    places = jnp.sum(jnp.where(chosen, place[:, :, None], 0), axis=1)
    home = position // retr - per_seg
    homes = per_seg + jnp.sum(jnp.where(chosen, home[None, :, None], 0), axis=1)
    counts = jnp.sum(here, axis=-1)
    return (
        counts.astype(jnp.int32),
        places.astype(jnp.int32).reshape(-1),
        homes.astype(jnp.int32).reshape(-1),
    )


def side_by_side(x):
    parts, rows, width = x.shape
    return x.transpose(1, 0, 2).reshape(rows, parts * width)


def gather_tokens(x):
    far = lax.ppermute(x, "fsdp", [(i, i ^ 2) for i in range(4)])
    near = lax.ppermute(x, "fsdp", [(i, i ^ 1) for i in range(4)])
    both = lax.ppermute(far, "fsdp", [(i, i ^ 1) for i in range(4)])
    return [x, near, far, both]


def weight_grad_plain(attention, parts, order):
    n = lax.axis_size("mem")
    rows = parts[0].shape[0]
    total = 0.0
    for i, part in enumerate(parts):
        own = lax.dynamic_slice_in_dim(attention, order[i] * rows, rows, 0)
        total = total + dot(own, part, TN)
    pieces = total.astype(BF).reshape(total.shape[0], n, -1).transpose(1, 0, 2)
    pieces = lax.all_to_all(pieces, "mem", split_axis=0, concat_axis=0, tiled=True)
    return jnp.sum(pieces.astype(F32), axis=0)


def cost(us):
    return pl.CostEstimate(flops=us * 10**9, bytes_accessed=us * 10**6, transcendentals=0)


def after(first, *rest):
    return lax.optimization_barrier((first, *rest))[1:]


def per_device(
    queries, keys, values, mem_keys, mem_values, block_ids, gate_bias, out_weight, cotangent
):
    n = lax.axis_size("mem")
    me = lax.axis_index("mem")
    fs = lax.axis_index("fsdp")
    group = n // 2
    full = mem_keys.shape[1]
    all_heads = full // DH
    width = full // HALVES
    heads = width // DH
    pairs = heads // 2
    segments, per_seg, retr = block_ids.shape
    seg_dev = segments // n
    per_dev = mem_keys.shape[0] // MBLK
    blocks = seg_dev * per_seg
    tokens = blocks * QBLK
    seg_len = per_seg * QBLK
    rows = queries.shape[0]
    seg_rows = seg_len // rows
    gating = jax.nn.sigmoid(lax.dynamic_slice_in_dim(gate_bias, fs * all_heads, all_heads))
    halves = range(HALVES)

    def shifted(x, k):
        return lax.ppermute(x, "mem", [(i, (i + 2 * k) % n) for i in range(n)])

    def exchange(x):
        return lax.all_to_all(x, "fsdp", split_axis=0, concat_axis=0, tiled=True)

    swap = [(i, i ^ 1) for i in range(n)]
    cap = -(-4 * max(1, retr * per_seg // n) // UNROLL) * UNROLL
    lists = block_lists(block_ids, me, group, seg_dev, per_dev, cap)

    par_keys = [lax.ppermute(mem_keys, "mem", swap)]
    par_values = [lax.ppermute(mem_values, "mem", swap)]

    q = exchange((queries * BF(SCALE)).T.reshape(4, full, rows))
    q_slots = [q] + [shifted(q, k) for k in range(1, group)]
    (cotangent,) = after(q, cotangent)
    cot_parts = gather_tokens(cotangent)
    keys, values = after(q, keys, values)
    k, v = (
        exchange(x.reshape(rows, 4, full).transpose(1, 0, 2)).reshape(tokens, full)
        for x in (keys, values)
    )
    cot_parts = after((q_slots, k, v), *cot_parts)
    order = fs ^ jnp.arange(4, dtype=jnp.int32)
    whole = pl.BlockSpec(memory_space=pltpu.VMEM)
    do_parts = pl.pallas_call(
        attention_grad_kernel,
        in_specs=[SMEM] + [whole] * 5,
        out_specs=[whole] * HALVES,
        out_shape=[jax.ShapeDtypeStruct((4, width, rows), BF)] * HALVES,
        compiler_params=pltpu.CompilerParams(vmem_limit_bytes=VMEM),
        cost_estimate=cost(1),
            name="attention_grad",
    )(order, out_weight, *cot_parts)
    do_slots = [[x] + [shifted(x, k) for k in range(1, group)] for x in do_parts]
    (late_weight,) = after(v, out_weight)
    full_weight = lax.all_gather(late_weight, "fsdp", axis=0, tiled=True)

    seg_spec = pl.BlockSpec((seg_len, full), lambda s: (s, 0))
    q_spec = pl.BlockSpec((seg_rows, full, rows), lambda s: (s, 0, 0))
    do_spec = pl.BlockSpec((seg_rows, width, rows), lambda s: (s, 0, 0))
    part_spec = pl.BlockSpec((per_seg, full, QBLK), lambda s: (s, 0, 0))
    part_shape = jax.ShapeDtypeStruct((blocks, full, QBLK), F32)
    head_shape = jax.ShapeDtypeStruct((tokens, full), BF)
    o_local, dq_local, dk, dv = pl.pallas_call(
        functools.partial(local_kernel, all_heads // 2, per_seg, HALVES),
        grid=(seg_dev,),
        in_specs=[SMEM, q_spec, seg_spec, seg_spec] + [do_spec] * HALVES,
        out_specs=[part_spec, part_spec, seg_spec, seg_spec],
        out_shape=[part_shape, part_shape, head_shape, head_shape],
        scratch_shapes=[pltpu.VMEM((seg_len, full), F32)] * 2,
        compiler_params=pltpu.CompilerParams(vmem_limit_bytes=VMEM),
        cost_estimate=cost(1),
            name="local",
    )(gating, q, k, v, *do_parts)

    lists = after((o_local, dk), *lists)
    t_specs = [
        pl.BlockSpec((per_seg, width, QBLK), at_slot(i, seg_dev - 1)) for i in range(group)
    ]
    t_shape = jax.ShapeDtypeStruct((blocks, width, QBLK), BF)
    stat_block = (1, per_seg, 2, heads * QBLK)
    memory_rows = 2 * mem_keys.shape[0]
    scratch = [pltpu.VMEM((memory_rows, width), BF)] * 2
    scratch += [pltpu.VMEM((per_seg + 1, pairs, 128, 256), BF)] * 2
    scratch += [pltpu.VMEM((cap, pairs, MBLK, 256), F32)]
    acc = pltpu.VMEM((per_seg + 1, pairs, 128, 256), F32)
    rows8 = pltpu.VMEM((per_seg + 1, pairs, 8, 256), F32)
    rows1 = pltpu.VMEM((per_seg + 1, pairs, 1, 256), F32)
    sems = pltpu.SemaphoreType.DMA((4,))
    limit = pltpu.CompilerParams(vmem_limit_bytes=VMEM)
    stat_specs = [
        pl.BlockSpec(stat_block, lambda s, b, *_, k=k: ((s - k) % group, b, 0, 0))
        for k in range(group)
    ]

    def slot_specs(half):
        return [
            pl.BlockSpec((seg_rows, width, rows), at_slot(i, seg_dev - 1, half))
            for i in range(group)
        ]

    o_home, stat_slots = [], []
    spreads = [pltpu.VMEM((per_seg + 1, pairs, 128, 256), BF)]
    for i in halves:
        outs = pl.pallas_call(
            functools.partial(memory_forward, group, pairs, i),
            grid_spec=pltpu.PrefetchScalarGridSpec(
                num_scalar_prefetch=3,
                grid=(group, seg_dev),
                in_specs=[ANY] * 4 + slot_specs(i),
                out_specs=t_specs
                + t_specs
                + [
                    pl.BlockSpec(
                        (1, per_seg, 1, heads * QBLK), lambda s, b, *_: (s, b, 0, 0)
                    )
                ],
                scratch_shapes=scratch[:2] + spreads + scratch[-1:] + [rows8, rows8, acc, sems],
            ),
            out_shape=[t_shape] * group
            + [jax.ShapeDtypeStruct(t_shape.shape, F32)] * group
            + [jax.ShapeDtypeStruct((group, blocks, 1, heads * QBLK), F32)],
            compiler_params=limit,
            cost_estimate=cost(30),
            name="memory_forward",
        )(*lists, mem_keys, par_keys[i], mem_values, par_values[i], *q_slots)
        o_slots, exact, lse = list(outs[:group]), outs[group : 2 * group], outs[-1]
        stats = pl.pallas_call(
            functools.partial(statistics_kernel, group, heads),
            grid=(seg_dev,),
            in_specs=[
                pl.BlockSpec((group, per_seg, 1, heads * QBLK), lambda s: (0, s, 0, 0))
            ]
            + [pl.BlockSpec((seg_rows, width, rows), lambda s: (s, 0, 0))] * group
            + [pl.BlockSpec((per_seg, width, QBLK), lambda s: (s, 0, 0))] * group,
            out_specs=pl.BlockSpec(
                (group, per_seg, 2, heads * QBLK), lambda s: (0, s, 0, 0)
            ),
            out_shape=jax.ShapeDtypeStruct((group, blocks, 2, heads * QBLK), F32),
            compiler_params=limit,
            cost_estimate=cost(5),
            name="statistics",
        )(lse, *do_slots[i], *exact)
        stat_slots.append([stats] + [shifted(stats, k) for k in range(1, group)])
        if ORDER:
            middle = range(2, group - 1)
            held = after(stat_slots[-1], *[o_slots[j] for j in middle])
            for j, x in zip(middle, held):
                o_slots[j] = x
        o_home.append([o_slots[0]] + [shifted(o_slots[k], -k) for k in range(1, group)])

    last = stat_slots[-1][0]
    dq_home = []
    for i in halves:
        first_stats = after(last, *stat_slots[i])
        dq_slots = pl.pallas_call(
            functools.partial(memory_backward, group, pairs, i),
            grid_spec=pltpu.PrefetchScalarGridSpec(
                num_scalar_prefetch=3,
                grid=(group, seg_dev),
                in_specs=[ANY] * 4 + slot_specs(i) + slot_specs(0) + stat_specs,
                out_specs=t_specs,
                scratch_shapes=scratch + [rows1, rows1, acc, sems],
            ),
            out_shape=[t_shape] * group,
            compiler_params=limit,
            cost_estimate=cost(30),
            name="memory_backward",
        )(
            *lists, mem_keys, par_keys[i], mem_values, par_values[i],
            *q_slots, *do_slots[i], *first_stats,
        )
        last = dq_slots[0]
        dq_home.append([dq_slots[0]] + [shifted(dq_slots[k], -k) for k in range(1, group)])

    dk, dv = after(last, dk, dv)
    key_grad, value_grad = [side_by_side(exchange(x.reshape(4, rows, full))) for x in (dk, dv)]
    home_spec = pl.BlockSpec((per_seg, width, QBLK), lambda b: (b, 0, 0))
    home_out = pl.BlockSpec((seg_len, width), lambda b: (b, 0))
    home_shape = jax.ShapeDtypeStruct((tokens, width), BF)
    home_specs = [
        pl.BlockSpec(stat_block, lambda b, k=k: (k, b, 0, 0)) for k in range(group)
    ]
    columns = out_weight.shape[1] // n
    steps = jnp.arange(group, dtype=jnp.int32)
    dests = jnp.concatenate([(me // 2 - steps) % group, (me % 2)[None]]).astype(jnp.int32)
    token_attention, weight_rows, token_dq = [], [], []
    for i in halves:
        local_spec = pl.BlockSpec((per_seg, width, QBLK), lambda b, i=i: (b, i, 0))
        home_stats = [stat_slots[i][(group - k) % group] for k in range(group)]
        o_parts = after(last, *o_home[i])
        attention, attention_t = pl.pallas_call(
            functools.partial(attention_kernel, group, heads, i * heads),
            grid=(seg_dev,),
            in_specs=[SMEM, local_spec] + [home_spec] * group + home_specs,
            out_specs=[home_out, pl.BlockSpec((width, seg_len), lambda b: (0, b))],
            out_shape=[home_shape, jax.ShapeDtypeStruct((width, tokens), BF)],
            compiler_params=limit,
            cost_estimate=cost(3),
            name="attention",
        )(gating, o_local, *o_parts, *home_stats)
        token_attention.append(exchange(attention.reshape(4, rows, width)))
        if columns % 128:
            weight_rows.append(weight_grad_plain(attention, cot_parts, order))
            continue
        piece = (1, width, columns)
        send, keep = pl.pallas_call(
            weight_grad_kernel,
            grid_spec=pltpu.PrefetchScalarGridSpec(
                num_scalar_prefetch=2,
                grid=(group,),
                in_specs=[pl.BlockSpec((width, tokens), lambda k, *_: (0, 0))]
                + [pl.BlockSpec((rows, 2 * columns), lambda k, _, to: (0, to[k]))] * 4,
                out_specs=[pl.BlockSpec(piece, lambda k, *_: (k, 0, 0))] * 2,
            ),
            out_shape=[jax.ShapeDtypeStruct((group, width, columns), BF)] * 2,
            compiler_params=limit,
            cost_estimate=cost(5),
            name="weight_grad",
        )(order, dests, attention_t, *cot_parts)
        got = lax.ppermute(send, "mem", swap)
        sums = [
            (keep[k].astype(F32) + got[k].astype(F32)).astype(BF) for k in range(group)
        ]
        sums = [sums[0]] + [shifted(sums[k], -k) for k in range(1, group)]
        weight_rows.append(functools.reduce(jnp.add, [x.astype(F32) for x in sums]))
    projected = jnp.einsum(
        "stc,scd->td",
        jnp.concatenate(token_attention, axis=2),
        full_weight.reshape(4, full, -1),
        preferred_element_type=F32,
    ).astype(BF)
    for i in halves:
        dq_parts = after(projected, *dq_home[i])
        local_spec = pl.BlockSpec((per_seg, width, QBLK), lambda b, i=i: (b, i, 0))
        dq = pl.pallas_call(
            functools.partial(query_grad_kernel, group, heads, i * heads),
            grid=(seg_dev,),
            in_specs=[SMEM, local_spec] + [home_spec] * group,
            out_specs=home_out,
            out_shape=home_shape,
            compiler_params=limit,
            cost_estimate=cost(3),
            name="query_grad",
        )(gating, dq_local, *dq_parts)
        token_dq.append(exchange(dq.reshape(4, rows, width)))

    return (
        projected,
        side_by_side(jnp.concatenate(token_dq, axis=2)),
        key_grad,
        value_grad,
        jnp.concatenate(weight_rows, axis=0),
    )


def solution(mesh):
    in_specs = (
        P(("mem", "fsdp"), None),
        P(("mem", "fsdp"), None),
        P(("mem", "fsdp"), None),
        P("mem", "fsdp"),
        P("mem", "fsdp"),
        P(),
        P(),
        P("fsdp", None),
        P(("mem", "fsdp"), None),
    )
    out_specs = (
        P(("mem", "fsdp"), None),
        P(("mem", "fsdp"), None),
        P(("mem", "fsdp"), None),
        P(("mem", "fsdp"), None),
        P("fsdp", "mem"),
    )
    return jax.shard_map(
        per_device, mesh=mesh, in_specs=in_specs, out_specs=out_specs, check_vma=False
    )
```

profile of v0, /device:TPU:0, one launch (start us, length us, event | category | flops | bytes accessed | tf_op | source)
XLA Modules:
  0.0 281.7 jit_solution(2735456326182688212)
XLA Ops:
  7.2 1.2 multiply_bitcast_fusion
  8.6 13.0 %all_to_all.35.q_ref.rest_0_ = bf16[4,256,256]{2,1,0:T(8,128)(2,1)} all-to-all(bf16[4,256,256]{2,1,0:T(8,128)(2,1)S(1)} %bitcast.59), channel_id=1, replica_groups=mesh['mem'=8,'fsdp'=4] {'fsdp'}, dimensions={0} | all-to-all | bytes 1048576 | tf_op jit(solution)/shard_map/all_to_all | solution.py:474
  21.9 1.9 collective-permute-start.6
  24.3 2.0 collective-permute-start
  27.1 12.7 %collective-permute-done.rest_1_ = bf16[4,256,256]{2,1,0:T(8,128)(2,1)} collective-permute-done((bf16[4,256,256]{2,1,0:T(8,128)(2,1)}, bf16[4,256,256]{2,1,0:T(8,128)(2,1)}, u32[]{:S(2)}, u32[]{:S(2)}) %collective-permute-start) | collective-permute-done | bytes 524320 | tf_op jit(solution)/shard_map/ppermute | solution.py:471
  40.6 5.5 %collective-permute-done.4.rest_2_ = bf16[256,2048]{1,0:T(8,128)(2,1)S(1)} collective-permute-done((bf16[256,2048]{1,0:T(8,128)(2,1)S(1)}, bf16[256,2048]{1,0:T(8,128)(2,1)S(1)}, u32[]{:S(2)}, u32[]{:S(2)}) %collective-permute-start.4) | collective-permute-done | bytes 1048608 | tf_op jit(solution)/shard_map/ppermute | solution.py:421
  46.3 2.0 copy.49
  48.4 4.1 %all-to-all-start.2 = ((bf16[4,256,256]{2,1,0:T(8,128)(2,1)}), bf16[4,256,256]{2,1,0:T(8,128)(2,1)}, u32[]{:S(2)}, u32[]{:S(2)}) async-start(bf16[4,256,256]{2,1,0:T(8,128)(2,1)} %bitcast.53), calls=%async_computation.2 | async-start | bytes 1048576 | tf_op jit(solution)/shard_map/all_to_all | solution.py:474
  52.9 1.9 copy.50
  54.8 6.6 %all-to-all-done.2 = bf16[4,256,256]{2,1,0:T(8,128)(2,1)} async-done(((bf16[4,256,256]{2,1,0:T(8,128)(2,1)}), bf16[4,256,256]{2,1,0:T(8,128)(2,1)}, u32[]{:S(2)}, u32[]{:S(2)}) %all-to-all-start.2) | async-done | bytes 524320 | tf_op jit(solution)/shard_map/all_to_all | solution.py:474
  61.4 4.1 %all-to-all-start.1 = ((bf16[4,256,256]{2,1,0:T(8,128)(2,1)}), bf16[4,256,256]{2,1,0:T(8,128)(2,1)}, u32[]{:S(2)}, u32[]{:S(2)}) async-start(bf16[4,256,256]{2,1,0:T(8,128)(2,1)} %bitcast.55), calls=%async_computation.1 | async-start | bytes 1048576 | tf_op jit(solution)/shard_map/all_to_all | solution.py:474
  65.6 4.0 %collective-permute-start.2 = (bf16[4,256,256]{2,1,0:T(8,128)(2,1)}, bf16[4,256,256]{2,1,0:T(8,128)(2,1)}, u32[]{:S(2)}, u32[]{:S(2)}) collective-permute-start(bf16[4,256,256]{2,1,0:T(8,128)(2,1)} %all_to_all.35.q_ref.rest_0_), channel_id=1, source_target_pairs={{0,24},{4,28},{8,0},{12,4},{16,8},{20,12},{24,16},{28,20},{1,25},{... | collective-permute-start | bytes 1572872 | tf_op jit(solution)/shard_map/ppermute | solution.py:471
  73.0 1.4 all-to-all-done.1
  74.5 7.2 %collective-permute-done.2.rest_3_ = bf16[4,256,256]{2,1,0:T(8,128)(2,1)} collective-permute-done((bf16[4,256,256]{2,1,0:T(8,128)(2,1)}, bf16[4,256,256]{2,1,0:T(8,128)(2,1)}, u32[]{:S(2)}, u32[]{:S(2)}) %collective-permute-start.2) | collective-permute-done | bytes 524320 | tf_op jit(solution)/shard_map/ppermute | solution.py:471
  81.7 1.0 copy-done.2
  82.6 4.6 %attention_grad.1.rest_0_.rest_4_ = bf16[4,256,256]{2,1,0:T(8,128)(2,1)} custom-call(s32[4]{0:T(128)} %iota_xor_fusion.order, bf16[256,2048]{1,0:T(8,128)(2,1)} %weight_ref.1, bf16[256,2048]{1,0:T(8,128)(2,1)} %rest_0_.1, bf16[256,2048]{1,0:T(8,128)(2,1)} %copy-done.2, bf16[256,2048]{1,0:T(8,128)(2,1)} %copy-done.1, ...), custom_call_target="tpu_custom_call" | custom-call | flops 1000000000 | bytes 1000000 | tf_op jit(solution)/shard_map/attention_grad/pallas_call | solution.py:495
  87.2 4.3 %collective-permute-start.10 = (bf16[4,256,256]{2,1,0:T(8,128)(2,1)}, bf16[4,256,256]{2,1,0:T(8,128)(2,1)S(1)}, u32[]{:S(2)}, u32[]{:S(2)}) collective-permute-start(bf16[4,256,256]{2,1,0:T(8,128)(2,1)} %attention_grad.1.rest_0_.rest_4_), channel_id=1, source_target_pairs={{0,24},{4,28},{8,0},{12,4},{16,8},{20,12},{24,16},{28,20},{1,25},{... | collective-permute-start | bytes 1572872 | tf_op jit(solution)/shard_map/ppermute | solution.py:471
  92.1 10.5 %local.1 = (f32[8,256,128]{2,1,0:T(8,128)}, f32[8,256,128]{2,1,0:T(8,128)}, bf16[1024,256]{1,0:T(8,128)(2,1)}, bf16[1024,256]{1,0:T(8,128)(2,1)}) custom-call(f32[4]{0:T(128)} %add_divide_fusion.gate, bf16[4,256,256]{2,1,0:T(8,128)(2,1)} %all_to_all.35.q_ref.rest_0_, bf16[1024,256]{1,0:T(8,128)(2,1)} %bitcast.3.k_ref, bf16[1024,256]{1,0:T(8,128)(2,1)} %bitcast.5.v_ref, ...), custom_call_target="tpu_custom_call" | custom-call | flops 1000000000 | bytes 1000000 | tf_op jit(solution)/shard_map/local/pallas_call | solution.py:514
  102.6 11.9 %collective-permute-done.7.v_par = bf16[4096,256]{1,0:T(8,128)(2,1)} collective-permute-done((bf16[4096,256]{1,0:T(8,128)(2,1)}, bf16[4096,256]{1,0:T(8,128)(2,1)}, u32[]{:S(2)}, u32[]{:S(2)}) %collective-permute-start.7) | collective-permute-done | bytes 2097184 | tf_op jit(solution)/shard_map/ppermute | solution.py:481
  114.5 23.4 %memory_forward.1 = (bf16[8,256,128]{2,1,0:T(8,128)(2,1)}, bf16[8,256,128]{2,1,0:T(8,128)(2,1)}, bf16[8,256,128]{2,1,0:T(8,128)(2,1)}, bf16[8,256,128]{2,1,0:T(8...) custom-call(s32[8]{0:T(128)} %reduce_sum.39.counts, ...), custom_call_target="tpu_custom_call" | custom-call | flops 30000001024 | bytes 30000000 | tf_op jit(solution)/shard_map/memory_forward/pallas_call | solution.py:555
  139.0 3.8 %statistics.1.rest_8_.rest_4_ = f32[4,8,2,512]{3,2,1,0:T(2,128)} custom-call(f32[4,8,1,512]{3,2,1,0:T(1,128)} %get-tuple-element.64.lse_ref, bf16[4,256,256]{2,1,0:T(8,128)(2,1)} %attention_grad.1.rest_0_.rest_4_, bf16[4,256,256]{2,1,0:T(8,128)(2,1)} %copy-done.8, bf16[4,256,256]{2,1,0:T(8,128)(2,1)} %copy-done.10, bf16[4,256,256]{2,1,0:T(8,128)(2,1)} %copy-done.6, ...), custom_call_target="tpu_custom_call" | custom-call | flops 5000000000 | bytes 5000000 | tf_op jit(solution)/shard_map/statistics/pallas_call | solution.py:578
  142.8 5.7 %collective-permute-start.12 = (f32[4,8,2,512]{3,2,1,0:T(2,128)}, f32[4,8,2,512]{3,2,1,0:T(2,128)S(1)}, u32[]{:S(2)}, u32[]{:S(2)}) collective-permute-start(f32[4,8,2,512]{3,2,1,0:T(2,128)} %statistics.1.rest_8_.rest_4_), channel_id=1, source_target_pairs={{0,16},{4,20},{8,24},{12,28},{16,0},{20,4},{24,8},{28,12},{1,17},{... | collective-permute-start | bytes 393224 | tf_op jit(solution)/shard_map/ppermute | solution.py:471
  148.5 1.5 collective-permute-start.14
  150.7 2.0 collective-permute-done.11.rest_9_.rest_7_
  152.7 3.6 %collective-permute-done.12.rest_10_.rest_6_ = f32[4,8,2,512]{3,2,1,0:T(2,128)S(1)} collective-permute-done((f32[4,8,2,512]{3,2,1,0:T(2,128)}, f32[4,8,2,512]{3,2,1,0:T(2,128)S(1)}, u32[]{:S(2)}, u32[]{:S(2)}) %collective-permute-start.12) | collective-permute-done | bytes 131104 | tf_op jit(solution)/shard_map/ppermute | solution.py:471
  156.3 1.4 collective-permute-done.13.rest_11_.rest_5_
  157.7 1.1 collective-permute-start.15
  158.8 27.9 %memory_backward.1 = (bf16[8,256,128]{2,1,0:T(8,128)(2,1)}, bf16[8,256,128]{2,1,0:T(8,128)(2,1)}, bf16[8,256,128]{2,1,0:T(8,128)(2,1)}, bf16[8,256,128]{2,1,0:T(8,128)(2,1)}) custom-call(s32[8]{0:T(128)} %reduce_sum.39.counts, s32[128]{0:T(128)} %reshape.300.places, s32[128]{0:T(128)} %add.136.homes, bf16[4096,256]{1,0:T(8,128)(2,1)} %k_own.3, ...), custom_call_target="tpu_custom_call" | custom-call | flops 30000001024 | bytes 30000000 | tf_op jit(solution)/shard_map/memory_backward/pallas_call | solution.py:606
  186.7 10.5 %all-to-all-start.5 = ((bf16[4,256,256]{2,1,0:T(8,128)(2,1)}), bf16[4,256,256]{2,1,0:T(8,128)(2,1)S(1)}, u32[]{:S(2)}, u32[]{:S(2)}) async-start(bf16[4,256,256]{2,1,0:T(8,128)(2,1)} %bitcast.14), calls=%async_computation.5 | async-start | bytes 1048576 | tf_op jit(solution)/shard_map/all_to_all | solution.py:474
  197.8 8.0 %collective-permute-start.17 = (bf16[8,256,128]{2,1,0:T(8,128)(2,1)}, bf16[8,256,128]{2,1,0:T(8,128)(2,1)S(1)}, u32[]{:S(2)}, u32[]{:S(2)}) collective-permute-start(bf16[8,256,128]{2,1,0:T(8,128)(2,1)} %get-tuple-element.86), channel_id=1, source_target_pairs={{0,24},{4,28},{8,0},{12,4},{16,8},{20,12},{24,16},{28,20},{1,25},{... | collective-permute-start | bytes 1572872 | tf_op jit(solution)/shard_map/ppermute | solution.py:471
  206.4 3.0 %attention.1 = (bf16[1024,256]{1,0:T(8,128)(2,1)}, bf16[256,1024]{1,0:T(8,128)(2,1)}) custom-call(f32[4]{0:T(128)} %add_divide_fusion.gate, f32[8,256,128]{2,1,0:T(8,128)} %get-tuple-element.59.local_ref, bf16[8,256,128]{2,1,0:T(8,128)(2,1)} %get-tuple-element.79.rest_0_, bf16[8,256,128]{2,1,0:T(8,128)(2,1)} %collective-permute-done.14.rest_1_, ...), custom_call_target="tpu_custom_call" | custom-call | flops 3000000000 | bytes 3000000 | tf_op jit(solution)/shard_map/attention/pallas_call | solution.py:642
  209.5 3.5 %all-to-all-start.3 = ((bf16[4,256,256]{2,1,0:T(8,128)(2,1)}), bf16[4,256,256]{2,1,0:T(8,128)(2,1)S(1)}, u32[]{:S(2)}, u32[]{:S(2)}) async-start(bf16[4,256,256]{2,1,0:T(8,128)(2,1)} %bitcast.65), calls=%async_computation.3 | async-start | bytes 1048576 | tf_op jit(solution)/shard_map/all_to_all | solution.py:474
  213.0 5.8 %weight_grad.1 = (bf16[4,256,256]{2,1,0:T(8,128)(2,1)}, bf16[4,256,256]{2,1,0:T(8,128)(2,1)}) custom-call(s32[4]{0:T(128)} %iota_xor_fusion.order, s32[5]{0:T(128)} %pad_add_fusion.dests, bf16[256,1024]{1,0:T(8,128)(2,1)} %get-tuple-element.96.attention_ref, bf16[256,2048]{1,0:T(8,128)(2,1)} %rest_0_.1, bf16[256,2048]{1,0:T(8,128)(2,1)} %copy-done.2, ...), custom_call_target="tpu_custom_call" | custom-call | flops 5000000000 | bytes 5000000 | tf_op jit(solution)/shard_map/weight_grad/pallas_call | solution.py:657
  218.7 1.5 collective-permute-start.20
  220.2 1.5 all-to-all-done.3
  221.8 3.5 %all-to-all-start.6 = ((bf16[4,256,256]{2,1,0:T(8,128)(2,1)}), bf16[4,256,256]{2,1,0:T(8,128)(2,1)S(1)}, u32[]{:S(2)}, u32[]{:S(2)}) async-start(bf16[4,256,256]{2,1,0:T(8,128)(2,1)} %bitcast.16), calls=%async_computation.6 | async-start | bytes 1048576 | tf_op jit(solution)/shard_map/all_to_all | solution.py:474
  225.3 4.4 %fusion = bf16[256,2048]{1,0:T(8,128)(2,1)} fusion(bf16[4,256,256]{2,1,0:T(8,128)(2,1)S(1)} %all-to-all-done.3, bf16[4,256,2048]{2,1,0:T(8,128)(2,1)} %bitcast.69), kind=kOutput, calls=%fused_computation.2 | convolution fusion | flops 1074266112 | bytes 5767168 | tf_op jit(solution)/shard_map/stc,scd->td/dot_general | solution.py:677
  229.7 19.2 %collective-permute-done.18.rest_2_ = bf16[8,256,128]{2,1,0:T(8,128)(2,1)S(1)} collective-permute-done((bf16[8,256,128]{2,1,0:T(8,128)(2,1)}, bf16[8,256,128]{2,1,0:T(8,128)(2,1)S(1)}, u32[]{:S(2)}, u32[]{:S(2)}) %collective-permute-start.18) | collective-permute-done | bytes 524320 | tf_op jit(solution)/shard_map/ppermute | solution.py:471
  248.9 0.8 copy-done.12
  249.7 2.8 query_grad.1
  252.5 3.5 %all-to-all-start.4 = ((bf16[4,256,256]{2,1,0:T(8,128)(2,1)}), bf16[4,256,256]{2,1,0:T(8,128)(2,1)S(1)}, u32[]{:S(2)}, u32[]{:S(2)}) async-start(bf16[4,256,256]{2,1,0:T(8,128)(2,1)} %bitcast.62), calls=%async_computation.4 | async-start | bytes 1048576 | tf_op jit(solution)/shard_map/all_to_all | solution.py:474
  256.2 4.6 %collective-permute-start.22 = (bf16[256,256]{1,0:T(8,128)(2,1)S(1)}, bf16[256,256]{1,0:T(8,128)(2,1)S(1)}, u32[]{:S(2)}, u32[]{:S(2)}) collective-permute-start(bf16[256,256]{1,0:T(8,128)(2,1)S(1)} %get-tuple-element.103), channel_id=1, source_target_pairs={{0,16},{4,20},{8,24},{12,28},{16,0},{20,4},{24,8},{28,12},{1,17},{... | collective-permute-start | bytes 393224 | tf_op jit(solution)/shard_map/ppermute | solution.py:471
  260.8 1.9 collective-permute-start.23
  262.7 0.9 copy.45
  263.6 0.9 copy.46
  264.5 8.8 %collective-permute-done.22 = bf16[256,256]{1,0:T(8,128)(2,1)S(1)} collective-permute-done((bf16[256,256]{1,0:T(8,128)(2,1)S(1)}, bf16[256,256]{1,0:T(8,128)(2,1)S(1)}, u32[]{:S(2)}, u32[]{:S(2)}) %collective-permute-start.22) | collective-permute-done | bytes 131104 | tf_op jit(solution)/shard_map/ppermute | solution.py:471
  273.2 0.8 fusion.2
  274.0 0.9 copy.44
  (92 shorter events, 10.4 us)
Async XLA Ops:
  7.2 14.4 %copy-start = (bf16[256,2048]{1,0:T(8,128)(2,1)S(1)}, bf16[256,2048]{1,0:T(8,128)(2,1)}, u32[]{:S(2)}) copy-start(bf16[256,2048]{1,0:T(8,128)(2,1)} %rest_0_.1) | copy-start | bytes 3145732
  7.2 16.8 %copy-start.4 = (s32[16,4,8]{0,2,1:T(8,128)S(1)}, s32[16,4,8]{0,2,1:T(8,128)}, u32[]{:S(2)}) copy-start(s32[16,4,8]{0,2,1:T(8,128)} %param.14) | copy-start | bytes 6148
  21.6 24.5 %collective-permute-start.4 = (bf16[256,2048]{1,0:T(8,128)(2,1)S(1)}, bf16[256,2048]{1,0:T(8,128)(2,1)S(1)}, u32[]{:S(2)}, u32[]{:S(2)}) collective-permute-start(bf16[256,2048]{1,0:T(8,128)(2,1)S(1)} %copy-done), channel_id=1, source_target_pairs={{0,2},{1,3},{2,0},{3,1},{4,6},{5,7},{6,4},{7,5},{8,10},{9,11},{10,... | collective-permute-start | bytes 3145736 | tf_op jit(solution)/shard_map/ppermute | solution.py:421
  21.9 80.6 %collective-permute-start.6 = (bf16[4096,256]{1,0:T(8,128)(2,1)}, bf16[4096,256]{1,0:T(8,128)(2,1)}, u32[]{:S(2)}, u32[]{:S(2)}) collective-permute-start(bf16[4096,256]{1,0:T(8,128)(2,1)} %k_own.3), channel_id=1, source_target_pairs={{0,4},{4,0},{8,12},{12,8},{16,20},{20,16},{24,28},{28,24},{1,5},{5... | collective-permute-start | bytes 6291464 | tf_op jit(solution)/shard_map/ppermute | solution.py:480
  23.8 90.7 %collective-permute-start.7 = (bf16[4096,256]{1,0:T(8,128)(2,1)}, bf16[4096,256]{1,0:T(8,128)(2,1)}, u32[]{:S(2)}, u32[]{:S(2)}) collective-permute-start(bf16[4096,256]{1,0:T(8,128)(2,1)} %v_own.3), channel_id=1, source_target_pairs={{0,4},{4,0},{8,12},{12,8},{16,20},{20,16},{24,28},{28,24},{1,5},{5... | collective-permute-start | bytes 6291464 | tf_op jit(solution)/shard_map/ppermute | solution.py:481
  24.3 15.5 %collective-permute-start = (bf16[4,256,256]{2,1,0:T(8,128)(2,1)}, bf16[4,256,256]{2,1,0:T(8,128)(2,1)}, u32[]{:S(2)}, u32[]{:S(2)}) collective-permute-start(bf16[4,256,256]{2,1,0:T(8,128)(2,1)} %all_to_all.35.q_ref.rest_0_), channel_id=1, source_target_pairs={{0,8},{4,12},{8,16},{12,20},{16,24},{20,28},{24,0},{28,4},{1,9},{5... | collective-permute-start | bytes 1572872 | tf_op jit(solution)/shard_map/ppermute | solution.py:471
  27.0 54.6 %collective-permute-start.3 = (bf16[256,2048]{1,0:T(8,128)(2,1)S(1)}, bf16[256,2048]{1,0:T(8,128)(2,1)S(1)}, u32[]{:S(2)}, u32[]{:S(2)}) collective-permute-start(bf16[256,2048]{1,0:T(8,128)(2,1)S(1)} %copy-done), channel_id=1, source_target_pairs={{0,1},{1,0},{2,3},{3,2},{4,5},{5,4},{6,7},{7,6},{8,9},{9,8},{10,11... | collective-permute-start | bytes 3145736 | tf_op jit(solution)/shard_map/ppermute | solution.py:422
  39.8 25.8 %collective-permute-start.1 = (bf16[4,256,256]{2,1,0:T(8,128)(2,1)}, bf16[4,256,256]{2,1,0:T(8,128)(2,1)}, u32[]{:S(2)}, u32[]{:S(2)}) collective-permute-start(bf16[4,256,256]{2,1,0:T(8,128)(2,1)} %all_to_all.35.q_ref.rest_0_), channel_id=1, source_target_pairs={{0,16},{4,20},{8,24},{12,28},{16,0},{20,4},{24,8},{28,12},{1,17},{... | collective-permute-start | bytes 1572872 | tf_op jit(solution)/shard_map/ppermute | solution.py:471
  46.1 15.3 %copy-start.1 = (bf16[256,2048]{1,0:T(8,128)(2,1)}, bf16[256,2048]{1,0:T(8,128)(2,1)S(1)}, u32[]{:S(2)}) copy-start(bf16[256,2048]{1,0:T(8,128)(2,1)S(1)} %collective-permute-done.4.rest_2_) | copy-start | bytes 3145732
  46.1 35.6 %collective-permute-start.5 = (bf16[256,2048]{1,0:T(8,128)(2,1)S(1)}, bf16[256,2048]{1,0:T(8,128)(2,1)}, u32[]{:S(2)}, u32[]{:S(2)}) collective-permute-start(bf16[256,2048]{1,0:T(8,128)(2,1)S(1)} %collective-permute-done.4.rest_2_), channel_id=1, source_target_pairs={{0,1},{1,0},{2,3},{3,2},{4,5},{5,4},{6,7},{7,6},{8,9},{9,8},{10,11... | collective-permute-start | bytes 3145736 | tf_op jit(solution)/shard_map/ppermute | solution.py:423
  46.3 26.1 %copy-start.16 = (f32[16]{0:T(128)S(1)}, f32[16]{0:T(128)}, u32[]{:S(2)}) copy-start(f32[16]{0:T(128)} %param.15) | copy-start | bytes 196
  48.4 13.0 %all-to-all-start.2 = ((bf16[4,256,256]{2,1,0:T(8,128)(2,1)}), bf16[4,256,256]{2,1,0:T(8,128)(2,1)}, u32[]{:S(2)}, u32[]{:S(2)}) async-start(bf16[4,256,256]{2,1,0:T(8,128)(2,1)} %bitcast.53), calls=%async_computation.2 | async-start | bytes 1048576 | tf_op jit(solution)/shard_map/all_to_all | solution.py:474
  61.4 13.1 %all-to-all-start.1 = ((bf16[4,256,256]{2,1,0:T(8,128)(2,1)}), bf16[4,256,256]{2,1,0:T(8,128)(2,1)}, u32[]{:S(2)}, u32[]{:S(2)}) async-start(bf16[4,256,256]{2,1,0:T(8,128)(2,1)} %bitcast.55), calls=%async_computation.1 | async-start | bytes 1048576 | tf_op jit(solution)/shard_map/all_to_all | solution.py:474
  65.6 159.7 %all-gather.2.cloned.1.call-start = ((), (), s32[]{:S(2)}) async-start(), calls=%async_computation.7 | async-start | bytes 5242880 | tf_op jit(solution)/shard_map/all_gather | solution.py:506
  65.6 16.1 %collective-permute-start.2 = (bf16[4,256,256]{2,1,0:T(8,128)(2,1)}, bf16[4,256,256]{2,1,0:T(8,128)(2,1)}, u32[]{:S(2)}, u32[]{:S(2)}) collective-permute-start(bf16[4,256,256]{2,1,0:T(8,128)(2,1)} %all_to_all.35.q_ref.rest_0_), channel_id=1, source_target_pairs={{0,24},{4,28},{8,0},{12,4},{16,8},{20,12},{24,16},{28,20},{1,25},{... | collective-permute-start | bytes 1572872 | tf_op jit(solution)/shard_map/ppermute | solution.py:471
  81.7 1.0 copy-start.2
  87.2 50.6 %collective-permute-start.10 = (bf16[4,256,256]{2,1,0:T(8,128)(2,1)}, bf16[4,256,256]{2,1,0:T(8,128)(2,1)S(1)}, u32[]{:S(2)}, u32[]{:S(2)}) collective-permute-start(bf16[4,256,256]{2,1,0:T(8,128)(2,1)} %attention_grad.1.rest_0_.rest_4_), channel_id=1, source_target_pairs={{0,24},{4,28},{8,0},{12,4},{16,8},{20,12},{24,16},{28,20},{1,25},{... | collective-permute-start | bytes 1572872 | tf_op jit(solution)/shard_map/ppermute | solution.py:471
  91.5 46.3 %collective-permute-start.8 = (bf16[4,256,256]{2,1,0:T(8,128)(2,1)}, bf16[4,256,256]{2,1,0:T(8,128)(2,1)S(1)}, u32[]{:S(2)}, u32[]{:S(2)}) collective-permute-start(bf16[4,256,256]{2,1,0:T(8,128)(2,1)} %attention_grad.1.rest_0_.rest_4_), channel_id=1, source_target_pairs={{0,8},{4,12},{8,16},{12,20},{16,24},{20,28},{24,0},{28,4},{1,9},{5... | collective-permute-start | bytes 1572872 | tf_op jit(solution)/shard_map/ppermute | solution.py:471
  91.5 46.4 %collective-permute-start.9 = (bf16[4,256,256]{2,1,0:T(8,128)(2,1)}, bf16[4,256,256]{2,1,0:T(8,128)(2,1)S(1)}, u32[]{:S(2)}, u32[]{:S(2)}) collective-permute-start(bf16[4,256,256]{2,1,0:T(8,128)(2,1)} %attention_grad.1.rest_0_.rest_4_), channel_id=1, source_target_pairs={{0,16},{4,20},{8,24},{12,28},{16,0},{20,4},{24,8},{28,12},{1,17},{... | collective-permute-start | bytes 1572872 | tf_op jit(solution)/shard_map/ppermute | solution.py:471
  137.8 0.8 copy-start.6
  137.9 0.9 copy-start.8
  137.9 1.1 copy-start.10
  139.0 9.5 %copy-start.11 = (bf16[8,256,128]{2,1,0:T(8,128)(2,1)S(1)}, bf16[8,256,128]{2,1,0:T(8,128)(2,1)}, u32[]{:S(2)}) copy-start(bf16[8,256,128]{2,1,0:T(8,128)(2,1)} %get-tuple-element.75) | copy-start | bytes 1572868
  139.0 11.0 %copy-start.7 = (bf16[8,256,128]{2,1,0:T(8,128)(2,1)S(1)}, bf16[8,256,128]{2,1,0:T(8,128)(2,1)}, u32[]{:S(2)}) copy-start(bf16[8,256,128]{2,1,0:T(8,128)(2,1)} %get-tuple-element.78) | copy-start | bytes 1572868
  139.0 18.7 %copy-start.5 = (bf16[8,256,128]{2,1,0:T(8,128)(2,1)S(1)}, bf16[8,256,128]{2,1,0:T(8,128)(2,1)}, u32[]{:S(2)}) copy-start(bf16[8,256,128]{2,1,0:T(8,128)(2,1)} %get-tuple-element.77) | copy-start | bytes 1572868
  142.8 9.8 %collective-permute-start.11 = (f32[4,8,2,512]{3,2,1,0:T(2,128)}, f32[4,8,2,512]{3,2,1,0:T(2,128)S(1)}, u32[]{:S(2)}, u32[]{:S(2)}) collective-permute-start(f32[4,8,2,512]{3,2,1,0:T(2,128)} %statistics.1.rest_8_.rest_4_), channel_id=1, source_target_pairs={{0,8},{4,12},{8,16},{12,20},{16,24},{20,28},{24,0},{28,4},{1,9},{5... | collective-permute-start | bytes 393224 | tf_op jit(solution)/shard_map/ppermute | solution.py:471
  142.8 13.4 %collective-permute-start.12 = (f32[4,8,2,512]{3,2,1,0:T(2,128)}, f32[4,8,2,512]{3,2,1,0:T(2,128)S(1)}, u32[]{:S(2)}, u32[]{:S(2)}) collective-permute-start(f32[4,8,2,512]{3,2,1,0:T(2,128)} %statistics.1.rest_8_.rest_4_), channel_id=1, source_target_pairs={{0,16},{4,20},{8,24},{12,28},{16,0},{20,4},{24,8},{28,12},{1,17},{... | collective-permute-start | bytes 393224 | tf_op jit(solution)/shard_map/ppermute | solution.py:471
  148.5 9.2 %collective-permute-start.13 = (f32[4,8,2,512]{3,2,1,0:T(2,128)}, f32[4,8,2,512]{3,2,1,0:T(2,128)S(1)}, u32[]{:S(2)}, u32[]{:S(2)}) collective-permute-start(f32[4,8,2,512]{3,2,1,0:T(2,128)} %statistics.1.rest_8_.rest_4_), channel_id=1, source_target_pairs={{0,24},{4,28},{8,0},{12,4},{16,8},{20,12},{24,16},{28,20},{1,25},{... | collective-permute-start | bytes 393224 | tf_op jit(solution)/shard_map/ppermute | solution.py:471
  148.5 57.3 %collective-permute-start.14 = (bf16[8,256,128]{2,1,0:T(8,128)(2,1)S(1)}, bf16[8,256,128]{2,1,0:T(8,128)(2,1)}, u32[]{:S(2)}, u32[]{:S(2)}) collective-permute-start(bf16[8,256,128]{2,1,0:T(8,128)(2,1)S(1)} %copy-done.11), channel_id=1, source_target_pairs={{0,24},{4,28},{8,0},{12,4},{16,8},{20,12},{24,16},{28,20},{1,25},{... | collective-permute-start | bytes 1572872 | tf_op jit(solution)/shard_map/ppermute | solution.py:471
  150.1 56.4 %collective-permute-start.16 = (bf16[8,256,128]{2,1,0:T(8,128)(2,1)S(1)}, bf16[8,256,128]{2,1,0:T(8,128)(2,1)}, u32[]{:S(2)}, u32[]{:S(2)}) collective-permute-start(bf16[8,256,128]{2,1,0:T(8,128)(2,1)S(1)} %copy-done.7), channel_id=1, source_target_pairs={{0,8},{4,12},{8,16},{12,20},{16,24},{20,28},{24,0},{28,4},{1,9},{5... | collective-permute-start | bytes 1572872 | tf_op jit(solution)/shard_map/ppermute | solution.py:471
  152.7 6.1 %copy-start.13 = (f32[4,8,2,512]{3,2,1,0:T(2,128)}, f32[4,8,2,512]{3,2,1,0:T(2,128)S(1)}, u32[]{:S(2)}) copy-start(f32[4,8,2,512]{3,2,1,0:T(2,128)S(1)} %collective-permute-done.11.rest_9_.rest_7_) | copy-start | bytes 393220
  156.3 2.5 copy-start.14
  157.7 1.1 copy-start.15
  157.7 48.7 %collective-permute-start.15 = (bf16[8,256,128]{2,1,0:T(8,128)(2,1)S(1)}, bf16[8,256,128]{2,1,0:T(8,128)(2,1)}, u32[]{:S(2)}, u32[]{:S(2)}) collective-permute-start(bf16[8,256,128]{2,1,0:T(8,128)(2,1)S(1)} %copy-done.5), channel_id=1, source_target_pairs={{0,16},{4,20},{8,24},{12,28},{16,0},{20,4},{24,8},{28,12},{1,17},{... | collective-permute-start | bytes 1572872 | tf_op jit(solution)/shard_map/ppermute | solution.py:471
  186.7 22.7 %all-to-all-start.5 = ((bf16[4,256,256]{2,1,0:T(8,128)(2,1)}), bf16[4,256,256]{2,1,0:T(8,128)(2,1)S(1)}, u32[]{:S(2)}, u32[]{:S(2)}) async-start(bf16[4,256,256]{2,1,0:T(8,128)(2,1)} %bitcast.14), calls=%async_computation.5 | async-start | bytes 1048576 | tf_op jit(solution)/shard_map/all_to_all | solution.py:474
  197.8 31.9 %collective-permute-start.17 = (bf16[8,256,128]{2,1,0:T(8,128)(2,1)}, bf16[8,256,128]{2,1,0:T(8,128)(2,1)S(1)}, u32[]{:S(2)}, u32[]{:S(2)}) collective-permute-start(bf16[8,256,128]{2,1,0:T(8,128)(2,1)} %get-tuple-element.86), channel_id=1, source_target_pairs={{0,24},{4,28},{8,0},{12,4},{16,8},{20,12},{24,16},{28,20},{1,25},{... | collective-permute-start | bytes 1572872 | tf_op jit(solution)/shard_map/ppermute | solution.py:471
  205.9 43.1 %collective-permute-start.18 = (bf16[8,256,128]{2,1,0:T(8,128)(2,1)}, bf16[8,256,128]{2,1,0:T(8,128)(2,1)S(1)}, u32[]{:S(2)}, u32[]{:S(2)}) collective-permute-start(bf16[8,256,128]{2,1,0:T(8,128)(2,1)} %get-tuple-element.87), channel_id=1, source_target_pairs={{0,16},{4,20},{8,24},{12,28},{16,0},{20,4},{24,8},{28,12},{1,17},{... | collective-permute-start | bytes 1572872 | tf_op jit(solution)/shard_map/ppermute | solution.py:471
  205.9 43.1 %collective-permute-start.19 = (bf16[8,256,128]{2,1,0:T(8,128)(2,1)}, bf16[8,256,128]{2,1,0:T(8,128)(2,1)}, u32[]{:S(2)}, u32[]{:S(2)}) collective-permute-start(bf16[8,256,128]{2,1,0:T(8,128)(2,1)} %get-tuple-element.88), channel_id=1, source_target_pairs={{0,8},{4,12},{8,16},{12,20},{16,24},{20,28},{24,0},{28,4},{1,9},{5... | collective-permute-start | bytes 1572872 | tf_op jit(solution)/shard_map/ppermute | solution.py:471
  209.5 12.3 %all-to-all-start.3 = ((bf16[4,256,256]{2,1,0:T(8,128)(2,1)}), bf16[4,256,256]{2,1,0:T(8,128)(2,1)S(1)}, u32[]{:S(2)}, u32[]{:S(2)}) async-start(bf16[4,256,256]{2,1,0:T(8,128)(2,1)} %bitcast.65), calls=%async_computation.3 | async-start | bytes 1048576 | tf_op jit(solution)/shard_map/all_to_all | solution.py:474
  218.7 37.3 %collective-permute-start.20 = (bf16[4,256,256]{2,1,0:T(8,128)(2,1)}, bf16[4,256,256]{2,1,0:T(8,128)(2,1)S(1)}, u32[]{:S(2)}, u32[]{:S(2)}) collective-permute-start(bf16[4,256,256]{2,1,0:T(8,128)(2,1)} %get-tuple-element.98), channel_id=1, source_target_pairs={{0,4},{4,0},{8,12},{12,8},{16,20},{20,16},{24,28},{28,24},{1,5},{5... | collective-permute-start | bytes 1572872 | tf_op jit(solution)/shard_map/ppermute | solution.py:671
  221.8 30.7 %all-to-all-start.6 = ((bf16[4,256,256]{2,1,0:T(8,128)(2,1)}), bf16[4,256,256]{2,1,0:T(8,128)(2,1)S(1)}, u32[]{:S(2)}, u32[]{:S(2)}) async-start(bf16[4,256,256]{2,1,0:T(8,128)(2,1)} %bitcast.16), calls=%async_computation.6 | async-start | bytes 1048576 | tf_op jit(solution)/shard_map/all_to_all | solution.py:474
  229.7 19.2 %copy-start.9 = (bf16[8,256,128]{2,1,0:T(8,128)(2,1)}, bf16[8,256,128]{2,1,0:T(8,128)(2,1)S(1)}, u32[]{:S(2)}) copy-start(bf16[8,256,128]{2,1,0:T(8,128)(2,1)S(1)} %collective-permute-done.17.rest_1_) | copy-start | bytes 1572868
  248.9 0.8 copy-start.12
  249.7 6.3 %copy-start.3 = (bf16[4,256,256]{2,1,0:T(8,128)(2,1)S(1)}, bf16[4,256,256]{2,1,0:T(8,128)(2,1)}, u32[]{:S(2)}) copy-start(bf16[4,256,256]{2,1,0:T(8,128)(2,1)} %get-tuple-element.97) | copy-start | bytes 1572868
  252.5 21.5 %all-to-all-start.4 = ((bf16[4,256,256]{2,1,0:T(8,128)(2,1)}), bf16[4,256,256]{2,1,0:T(8,128)(2,1)S(1)}, u32[]{:S(2)}, u32[]{:S(2)}) async-start(bf16[4,256,256]{2,1,0:T(8,128)(2,1)} %bitcast.62), calls=%async_computation.4 | async-start | bytes 1048576 | tf_op jit(solution)/shard_map/all_to_all | solution.py:474
  256.1 8.3 %collective-permute-start.21 = (bf16[256,256]{1,0:T(8,128)(2,1)S(1)}, bf16[256,256]{1,0:T(8,128)(2,1)S(1)}, u32[]{:S(2)}, u32[]{:S(2)}) collective-permute-start(bf16[256,256]{1,0:T(8,128)(2,1)S(1)} %get-tuple-element.101), channel_id=1, source_target_pairs={{0,24},{4,28},{8,0},{12,4},{16,8},{20,12},{24,16},{28,20},{1,25},{... | collective-permute-start | bytes 393224 | tf_op jit(solution)/shard_map/ppermute | solution.py:471
  256.2 17.1 %collective-permute-start.22 = (bf16[256,256]{1,0:T(8,128)(2,1)S(1)}, bf16[256,256]{1,0:T(8,128)(2,1)S(1)}, u32[]{:S(2)}, u32[]{:S(2)}) collective-permute-start(bf16[256,256]{1,0:T(8,128)(2,1)S(1)} %get-tuple-element.103), channel_id=1, source_target_pairs={{0,16},{4,20},{8,24},{12,28},{16,0},{20,4},{24,8},{28,12},{1,17},{... | collective-permute-start | bytes 393224 | tf_op jit(solution)/shard_map/ppermute | solution.py:471
  260.8 12.5 %collective-permute-start.23 = (bf16[256,256]{1,0:T(8,128)(2,1)S(1)}, bf16[256,256]{1,0:T(8,128)(2,1)S(1)}, u32[]{:S(2)}, u32[]{:S(2)}) collective-permute-start(bf16[256,256]{1,0:T(8,128)(2,1)S(1)} %get-tuple-element.102), channel_id=1, source_target_pairs={{0,8},{4,12},{8,16},{12,20},{16,24},{20,28},{24,0},{28,4},{1,9},{5... | collective-permute-start | bytes 393224 | tf_op jit(solution)/shard_map/ppermute | solution.py:471
Sparse Core Ops, SparseCore 0:
  73.1 33.0 all-gather.1
where the time goes:
time: 282 us
  waiting for transfers between devices  82 us (29%)
  Pallas kernels  81.8 us (29%)
  starting transfers between devices  68.9 us (24%)
  between operations  14.3 us (5%)
  blocking collectives  13 us (5%)
  local copies, waits for them, and re-layouts  12.5 us (4%)
  other arithmetic  4.84 us (2%)
  matrix products  4.41 us (2%)
    ppermute x18, waiting for transfers between devices, shifted(): return lax.ppermute(x, 'mem', [(i, (i + 2 * k) % n) for i in range(n)])  55 us
    ppermute x18, starting transfers between devices, shifted(): return lax.ppermute(x, 'mem', [(i, (i + 2 * k) % n) for i in range(n)])  35.7 us
    all_to_all x6, starting transfers between devices, exchange(): return lax.all_to_all(x, 'fsdp', split_axis=0, concat_axis=0, tiled=True)  29.2 us
    pallas_call x1, Pallas kernels, per_device(): pl.pallas_call(functools.partial(memory_backward, group, pairs, i), grid_...  27.9 us
    pallas_call x1, Pallas kernels, per_device(): pl.pallas_call(functools.partial(memory_forward, group, pairs, i), grid_s...  23.4 us
    all_to_all x1, blocking collectives, exchange(): return lax.all_to_all(x, 'fsdp', split_axis=0, concat_axis=0, tiled=True)  13 us
    ppermute x1, waiting for transfers between devices, per_device(): par_values = [lax.ppermute(mem_values, 'mem', swap)]  11.9 us
    pallas_call x1, Pallas kernels, per_device(): pl.pallas_call(functools.partial(local_kernel, all_heads // 2, per_seg, H...  10.5 us
  transfers between devices with their start and end apart: 31, of which 12 were waited for; matrix products, arithmetic and copies ran while one was open for 6% of the time, Pallas kernels for 29%

commit v1 on v0

--- a/solution.py
+++ b/solution.py
@@ -13,7 +13,7 @@
 LOW = -1e30
 UNROLL = 4
 HALVES = 1
-ORDER = True
+ORDER = False
 VMEM = 58 * 2**20
 SCALE = DH ** (-0.5)
 BF = jnp.bfloat16
@@ -61,22 +61,29 @@
 def start_step(group, half, slot, memory, buffers, sems, sides):
     rows, width = buffers[0].shape
     rows = rows // 2
-
-    @pl.when((slot == 0) & (pl.program_id(1) == 0))
+    own = pl.ds(half * width, width)
+    sources = [memory[0].at[:, own], memory[1], memory[2].at[:, own], memory[3]]
+    targets = [buffers[i].at[pl.ds(j * rows, rows)] for i in range(2) for j in range(2)]
+    copies = [
+        pltpu.make_async_copy(source, target, sems.at[i])
+        for i, (source, target) in enumerate(zip(sources, targets))
+    ]
+    begins = (slot == 0) & (pl.program_id(1) == 0)
+
+    @pl.when(begins)
     def _():
-        own = pl.ds(half * width, width)
-        sources = [memory[0].at[:, own], memory[1], memory[2].at[:, own], memory[3]]
-        targets = [buffers[i].at[pl.ds(j * rows, rows)] for i in range(2) for j in range(2)]
-        copies = [
-            pltpu.make_async_copy(source, target, sems.at[i])
-            for i, (source, target) in enumerate(zip(sources, targets))
-        ]
         for copy in copies:
             copy.start()
         for _, out in sides:
             out[...] = jnp.zeros_like(out)
-        for copy in copies:
+        for copy in copies[:2]:
             copy.wait()
+
+    def wait_values():
+        @pl.when(begins)
+        def _():
+            for copy in copies[2:]:
+                copy.wait()
 
     for i in range(group):
 
@@ -88,6 +95,7 @@
                         x = query_block(refs[i], b, t)
                         out[b, t, :DH, :QBLK] = x[:DH]
                         out[b, t, DH:, QBLK:] = x[DH:]
+    return wait_values
 
 
 def memory_forward(
@@ -95,14 +103,13 @@
 ):
     q_refs = rest[:group]
     o_refs = rest[group : 2 * group]
-    exact_refs = rest[2 * group : 3 * group]
-    lse_ref = rest[3 * group]
-    kbuf, vbuf, q_t, scores, tops, norms, acc, sems = rest[3 * group + 1 :]
+    exact_ref, lse_ref = rest[2 * group : 2 * group + 2]
+    kbuf, vbuf, q_t, scores, tops, norms, acc, sems = rest[2 * group + 2 :]
     slot = pl.program_id(0)
     number = slot * pl.num_programs(1) + pl.program_id(1)
     cap = scores.shape[0]
     blocks = q_t.shape[0] - 1
-    start_step(
+    wait_values = start_step(
         group, half, slot, (k_own, k_par, v_own, v_par), (kbuf, vbuf), sems, [(q_refs, q_t)]
     )
     tops[...] = jnp.full(tops.shape, LOW, F32)
@@ -126,6 +133,7 @@
         return carry
 
     lax.fori_loop(0, turns, first, 0)
+    wait_values()
     tops[...] = jnp.broadcast_to(jnp.max(tops[...], axis=2, keepdims=True), tops.shape)
 
     def second(turn, carry):
@@ -156,23 +164,23 @@
             lse_ref[0, b, :, wide] = jnp.where(some, tops[b, t, 0:1, :] + jnp.log(safe), LOW)
             parts.append(acc[b, t] * (1.0 / safe))
         results.append(jnp.concatenate(own_blocks(parts), axis=0))
+        exact_ref[0, b] = results[b]
     for i in range(group):
 
         @pl.when(slot == i)
         def _():
             for b in range(blocks):
-                exact_refs[i][b] = results[b]
                 o_refs[i][b] = results[b].astype(BF)
 
 
 def statistics_kernel(group, heads, lse_ref, *rest):
-    do_refs, o_refs, stat_ref = rest[:group], rest[group : 2 * group], rest[2 * group]
+    do_refs, (o_ref, stat_ref) = rest[:group], rest[group:]
     for i in range(group):
         for b in range(lse_ref.shape[1]):
             stat_ref[i, b, 0:1, :] = lse_ref[i, b]
             for t in range(heads // 2):
                 do = query_block(do_refs[i], b, t).astype(F32)
-                product = do * o_refs[i][b, t * 128 : (t + 1) * 128, :]
+                product = do * o_ref[i, b, t * 128 : (t + 1) * 128, :]
                 for h in range(2):
                     at = slice((2 * t + h) * QBLK, (2 * t + h + 1) * QBLK)
                     stat_ref[i, b, 1:2, at] = jnp.sum(
@@ -193,45 +201,46 @@
 ):
     q_refs = rest[:group]
     do_refs = rest[group : 2 * group]
-    stat_refs = rest[2 * group : 3 * group]
-    dq_refs = rest[3 * group : 4 * group]
-    kbuf, vbuf, q_t, do_t, weights, lses, means, acc, sems = rest[4 * group :]
+    stat_ref = rest[2 * group]
+    delta_ref, key_ref = rest[2 * group + 1 : 2 * group + 3]
+    kbuf, vbuf, q_t, do_t, weights, lses, means, acc, acc_keys, sems = rest[2 * group + 3 :]
     slot = pl.program_id(0)
     number = slot * pl.num_programs(1) + pl.program_id(1)
     cap = places.shape[0] // counts.shape[0]
     blocks = q_t.shape[0] - 1
-    start_step(
+    wait_values = start_step(
         group, half, slot, (k_own, k_par, v_own, v_par), (kbuf, vbuf), sems,
         [(q_refs, q_t), (do_refs, do_t)],
     )
     lses[...] = jnp.zeros_like(lses)
     means[...] = jnp.zeros_like(means)
     for b in range(blocks):
-        top, shares, norm = merged(stat_refs, b)
-        lse = top + jnp.log(norm)
-        mean = functools.reduce(
-            jnp.add, [x * ref[0, b, 1:2, :] for x, ref in zip(shares, stat_refs)]
-        ) / norm
         for t in range(pairs):
             wide = slice(t * 256, (t + 1) * 256)
-            lses[b, t] = lse[:, wide]
-            means[b, t] = mean[:, wide]
+            lses[b, t] = stat_ref[0, b, 0:1, wide]
+            means[b, t] = stat_ref[0, b, 1:2, wide]
     acc[...] = jnp.zeros_like(acc)
-
+    acc_keys[...] = jnp.zeros_like(acc_keys)
     turns = (counts[number] + UNROLL - 1) // UNROLL
 
     def first(turn, carry):
+        found = []
         for u in range(UNROLL):
             j = turn * UNROLL + u
             row = pl.multiple_of(places[number * cap + j] * MBLK, MBLK)
             b = homes[number * cap + j]
             for t in range(pairs):
                 cols = slice(t * 128, (t + 1) * 128)
-                s = dot(kbuf[pl.ds(row, MBLK), cols], q_t[b, t], NN)
-                weights[j, t] = jnp.exp(s - lses[b, t])
+                keys = kbuf[pl.ds(row, MBLK), cols]
+                p = jnp.exp(dot(keys, q_t[b, t], NN) - lses[b, t])
+                weights[j, t] = p
+                found.append((b, t, dot(keys, p.astype(BF), TN)))
+        for b, t, sums in found:
+            acc_keys[b, t] += sums
         return carry
 
     lax.fori_loop(0, turns, first, 0)
+    wait_values()
 
     def second(turn, carry):
         found = []
@@ -244,21 +253,37 @@
                 slope = dot(vbuf[pl.ds(row, MBLK), cols], do_t[b, t], NN)
                 delta = weights[j, t] * (slope - means[b, t])
                 found.append((b, t, dot(kbuf[pl.ds(row, MBLK), cols], delta.astype(BF), TN)))
-        for b, t, dq in found:
-            acc[b, t] += dq
+        for b, t, sums in found:
+            acc[b, t] += sums
         return carry
 
     lax.fori_loop(0, turns, second, 0)
-    results = [
-        jnp.concatenate(own_blocks([acc[b, t] for t in range(pairs)]), axis=0).astype(BF)
-        for b in range(blocks)
-    ]
+    for b in range(blocks):
+        for out_ref, total in ((delta_ref, acc), (key_ref, acc_keys)):
+            parts = own_blocks([total[b, t] for t in range(pairs)])
+            out_ref[0, b] = jnp.concatenate(parts, axis=0)
+
+
+def combine_kernel(group, heads, *rest):
+    stat_refs = rest[:group]
+    delta_ref, key_ref = rest[group : group + 2]
+    dq_refs = rest[group + 2 :]
     for i in range(group):
-
-        @pl.when(slot == i)
-        def _():
-            for b in range(blocks):
-                dq_refs[i][b] = results[b]
+        for b in range(dq_refs[i].shape[0]):
+            rows = [ref[(i - j) % group, b] for j, ref in enumerate(stat_refs)]
+            top = functools.reduce(jnp.maximum, [x[0:1] for x in rows])
+            shares = [jnp.exp(x[0:1] - top) for x in rows]
+            norm = functools.reduce(jnp.add, shares)
+            mean = functools.reduce(jnp.add, [p * x[1:2] for p, x in zip(shares, rows)]) / norm
+            share = shares[0] / norm
+            moved = share * (rows[0][1:2] - mean)
+            for h in range(heads):
+                at = slice(h * DH, (h + 1) * DH)
+                wide = slice(h * QBLK, (h + 1) * QBLK)
+                dq_refs[i][b, at, :] = (
+                    delta_ref[i, b, at, :] * share[:, wide]
+                    + key_ref[i, b, at, :] * moved[:, wide]
+                ).astype(BF)
 
 
 def local_kernel(pairs, blocks, halves, gate, q_ref, k_ref, v_ref, *rest):
@@ -528,6 +553,9 @@
         pl.BlockSpec((per_seg, width, QBLK), at_slot(i, seg_dev - 1)) for i in range(group)
     ]
     t_shape = jax.ShapeDtypeStruct((blocks, width, QBLK), BF)
+    slot_shape = jax.ShapeDtypeStruct((group, blocks, width, QBLK), F32)
+    slot_spec = pl.BlockSpec((1, per_seg, width, QBLK), lambda s, b, *_: (s, b, 0, 0))
+    all_spec = pl.BlockSpec((group, per_seg, width, QBLK), lambda s: (0, s, 0, 0))
     stat_block = (1, per_seg, 2, heads * QBLK)
     memory_rows = 2 * mem_keys.shape[0]
     scratch = [pltpu.VMEM((memory_rows, width), BF)] * 2
@@ -538,11 +566,6 @@
     rows1 = pltpu.VMEM((per_seg + 1, pairs, 1, 256), F32)
     sems = pltpu.SemaphoreType.DMA((4,))
     limit = pltpu.CompilerParams(vmem_limit_bytes=VMEM)
-    stat_specs = [
-        pl.BlockSpec(stat_block, lambda s, b, *_, k=k: ((s - k) % group, b, 0, 0))
-        for k in range(group)
-    ]
-
     def slot_specs(half):
         return [
             pl.BlockSpec((seg_rows, width, rows), at_slot(i, seg_dev - 1, half))
@@ -559,8 +582,8 @@
                 grid=(group, seg_dev),
                 in_specs=[ANY] * 4 + slot_specs(i),
                 out_specs=t_specs
-                + t_specs
                 + [
+                    slot_spec,
                     pl.BlockSpec(
                         (1, per_seg, 1, heads * QBLK), lambda s, b, *_: (s, b, 0, 0)
                     )
@@ -568,13 +591,13 @@
                 scratch_shapes=scratch[:2] + spreads + scratch[-1:] + [rows8, rows8, acc, sems],
             ),
             out_shape=[t_shape] * group
-            + [jax.ShapeDtypeStruct(t_shape.shape, F32)] * group
+            + [slot_shape]
             + [jax.ShapeDtypeStruct((group, blocks, 1, heads * QBLK), F32)],
             compiler_params=limit,
             cost_estimate=cost(30),
             name="memory_forward",
         )(*lists, mem_keys, par_keys[i], mem_values, par_values[i], *q_slots)
-        o_slots, exact, lse = list(outs[:group]), outs[group : 2 * group], outs[-1]
+        o_slots, exact, lse = list(outs[:group]), outs[-2], outs[-1]
         stats = pl.pallas_call(
             functools.partial(statistics_kernel, group, heads),
             grid=(seg_dev,),
@@ -582,7 +605,7 @@
                 pl.BlockSpec((group, per_seg, 1, heads * QBLK), lambda s: (0, s, 0, 0))
             ]
             + [pl.BlockSpec((seg_rows, width, rows), lambda s: (s, 0, 0))] * group
-            + [pl.BlockSpec((per_seg, width, QBLK), lambda s: (s, 0, 0))] * group,
+            + [all_spec],
             out_specs=pl.BlockSpec(
                 (group, per_seg, 2, heads * QBLK), lambda s: (0, s, 0, 0)
             ),
@@ -590,7 +613,7 @@
             compiler_params=limit,
             cost_estimate=cost(5),
             name="statistics",
-        )(lse, *do_slots[i], *exact)
+        )(lse, *do_slots[i], exact)
         stat_slots.append([stats] + [shifted(stats, k) for k in range(1, group)])
         if ORDER:
             middle = range(2, group - 1)
@@ -602,24 +625,42 @@
     last = stat_slots[-1][0]
     dq_home = []
     for i in halves:
-        first_stats = after(last, *stat_slots[i])
-        dq_slots = pl.pallas_call(
+        (own_stats,) = after(last, stat_slots[i][0])
+        sums = pl.pallas_call(
             functools.partial(memory_backward, group, pairs, i),
             grid_spec=pltpu.PrefetchScalarGridSpec(
                 num_scalar_prefetch=3,
                 grid=(group, seg_dev),
-                in_specs=[ANY] * 4 + slot_specs(i) + slot_specs(0) + stat_specs,
-                out_specs=t_specs,
-                scratch_shapes=scratch + [rows1, rows1, acc, sems],
+                in_specs=[ANY] * 4
+                + slot_specs(i)
+                + slot_specs(0)
+                + [pl.BlockSpec(stat_block, lambda s, b, *_: (s, b, 0, 0))],
+                out_specs=[slot_spec] * 2,
+                scratch_shapes=scratch + [rows1, rows1, acc, acc, sems],
             ),
-            out_shape=[t_shape] * group,
+            out_shape=[slot_shape] * 2,
             compiler_params=limit,
             cost_estimate=cost(30),
             name="memory_backward",
         )(
             *lists, mem_keys, par_keys[i], mem_values, par_values[i],
-            *q_slots, *do_slots[i], *first_stats,
+            *q_slots, *do_slots[i], own_stats,
         )
+        wide_spec = pl.BlockSpec((per_seg, width, QBLK), lambda s: (s, 0, 0))
+        dq_slots = pl.pallas_call(
+            functools.partial(combine_kernel, group, heads),
+            grid=(seg_dev,),
+            in_specs=[
+                pl.BlockSpec((group, per_seg, 2, heads * QBLK), lambda s: (0, s, 0, 0))
+            ]
+            * group
+            + [all_spec] * 2,
+            out_specs=[wide_spec] * group,
+            out_shape=[t_shape] * group,
+            compiler_params=limit,
+            cost_estimate=cost(5),
+            name="combine",
+        )(*stat_slots[i], *sums)
         last = dq_slots[0]
         dq_home.append([dq_slots[0]] + [shifted(dq_slots[k], -k) for k in range(1, group)])
 

time: 282 us -> 288 us (1.021); the launches traced: 282 us -> 284 us
  starting transfers between devices: 68.9 us -> 58.3 us
  waiting for transfers between devices: 82 us -> 92.4 us
    ppermute x18, waiting for transfers between devices: 55 us -> 65 us  [shifted(): return lax.ppermute(x, 'mem', [(i, (i + 2 * k) % n) for i in range(n)])]
    all_to_all x6, starting transfers between devices: 29.2 us -> 21.5 us  [exchange(): return lax.all_to_all(x, 'fsdp', split_axis=0, concat_axis=0, tiled=True)]
    pallas_call x0 -> x1, Pallas kernels: none -> 4.99 us  [per_device(): pl.pallas_call(functools.partial(combine_kernel, group, heads), grid=(seg...]
    pallas_call x1, Pallas kernels: 23.4 us -> 19.4 us  [per_device(): pl.pallas_call(functools.partial(memory_forward, group, pairs, i), grid_s...]
  transfers between devices with their start and end apart: 31 -> 31, of which waited for: 12 -> 11; matrix products, arithmetic and copies ran while one was open for 6% -> 6% of each run, Pallas kernels for 29% -> 29%
where the time goes in v1:
time: 288 us; the launch traced here: 284 us
  waiting for transfers between devices  92.4 us (32%)
  Pallas kernels  82.6 us (29%)
  starting transfers between devices  58.3 us (20%)
  between operations  14.4 us (5%)
  local copies, waits for them, and re-layouts  13.6 us (5%)
  blocking collectives  12.9 us (4%)
  other arithmetic  4.94 us (2%)
  matrix products  4.41 us (2%)
    ppermute x18, waiting for transfers between devices, shifted(): return lax.ppermute(x, 'mem', [(i, (i + 2 * k) % n) for i in range(n)])  65 us
    ppermute x18, starting transfers between devices, shifted(): return lax.ppermute(x, 'mem', [(i, (i + 2 * k) % n) for i in range(n)])  34.4 us
    pallas_call x1, Pallas kernels, per_device(): pl.pallas_call(functools.partial(memory_backward, group, pairs, i), grid_...  27.5 us
    all_to_all x6, starting transfers between devices, exchange(): return lax.all_to_all(x, 'fsdp', split_axis=0, concat_axis=0, tiled=True)  21.5 us
    pallas_call x1, Pallas kernels, per_device(): pl.pallas_call(functools.partial(memory_forward, group, pairs, i), grid_s...  19.4 us
    ppermute x1, waiting for transfers between devices, per_device(): par_values = [lax.ppermute(mem_values, 'mem', swap)]  13.8 us
    all_to_all x1, blocking collectives, exchange(): return lax.all_to_all(x, 'fsdp', split_axis=0, concat_axis=0, tiled=True)  12.9 us
    pallas_call x1, Pallas kernels, per_device(): pl.pallas_call(functools.partial(local_kernel, all_heads // 2, per_seg, H...  10.5 us
  transfers between devices with their start and end apart: 31, of which 11 were waited for; matrix products, arithmetic and copies ran while one was open for 6% of the time, Pallas kernels for 29%

profile of v1, /device:TPU:0, one launch (start us, length us, event | category | flops | bytes accessed | tf_op | source)
XLA Modules:
  0.0 283.6 jit_solution(7895207360421066024)
XLA Ops:
  7.2 1.1 multiply_bitcast_fusion
  8.5 12.9 %all_to_all.35.q_ref.rest_0_ = bf16[4,256,256]{2,1,0:T(8,128)(2,1)S(1)} all-to-all(bf16[4,256,256]{2,1,0:T(8,128)(2,1)S(1)} %bitcast.59), channel_id=1, replica_groups=mesh['mem'=8,'fsdp'=4] {'fsdp'}, dimensions={0} | all-to-all | bytes 1048576 | tf_op jit(solution)/shard_map/all_to_all | solution.py:499
  21.8 1.5 collective-permute-start.6
  24.9 1.6 collective-permute-start
  27.2 2.6 collective-permute-start.1
  30.0 11.9 %collective-permute-done.rest_1_ = bf16[4,256,256]{2,1,0:T(8,128)(2,1)} collective-permute-done((bf16[4,256,256]{2,1,0:T(8,128)(2,1)S(1)}, bf16[4,256,256]{2,1,0:T(8,128)(2,1)}, u32[]{:S(2)}, u32[]{:S(2)}) %collective-permute-start) | collective-permute-done | bytes 524320 | tf_op jit(solution)/shard_map/ppermute | solution.py:496
  41.9 4.3 %collective-permute-done.4.rest_2_ = bf16[256,2048]{1,0:T(8,128)(2,1)S(1)} collective-permute-done((bf16[256,2048]{1,0:T(8,128)(2,1)}, bf16[256,2048]{1,0:T(8,128)(2,1)S(1)}, u32[]{:S(2)}, u32[]{:S(2)}) %collective-permute-start.4) | collective-permute-done | bytes 1048608 | tf_op jit(solution)/shard_map/ppermute | solution.py:446
  46.4 2.0 copy.49
  48.4 4.1 %all-to-all-start.2 = ((bf16[4,256,256]{2,1,0:T(8,128)(2,1)}), bf16[4,256,256]{2,1,0:T(8,128)(2,1)}, u32[]{:S(2)}, u32[]{:S(2)}) async-start(bf16[4,256,256]{2,1,0:T(8,128)(2,1)} %bitcast.53), calls=%async_computation.2 | async-start | bytes 1048576 | tf_op jit(solution)/shard_map/all_to_all | solution.py:499
  52.9 9.4 %collective-permute-done.1.rest_2_ = bf16[4,256,256]{2,1,0:T(8,128)(2,1)} collective-permute-done((bf16[4,256,256]{2,1,0:T(8,128)(2,1)S(1)}, bf16[4,256,256]{2,1,0:T(8,128)(2,1)}, u32[]{:S(2)}, u32[]{:S(2)}) %collective-permute-start.1) | collective-permute-done | bytes 524320 | tf_op jit(solution)/shard_map/ppermute | solution.py:496
  62.3 1.6 collective-permute-start.2
  64.8 3.5 %all-to-all-start.1 = ((bf16[4,256,256]{2,1,0:T(8,128)(2,1)}), bf16[4,256,256]{2,1,0:T(8,128)(2,1)S(1)}, u32[]{:S(2)}, u32[]{:S(2)}) async-start(bf16[4,256,256]{2,1,0:T(8,128)(2,1)} %bitcast.55), calls=%async_computation.1 | async-start | bytes 1048576 | tf_op jit(solution)/shard_map/all_to_all | solution.py:499
  71.7 5.3 %all-to-all-done.1 = bf16[4,256,256]{2,1,0:T(8,128)(2,1)S(1)} async-done(((bf16[4,256,256]{2,1,0:T(8,128)(2,1)}), bf16[4,256,256]{2,1,0:T(8,128)(2,1)S(1)}, u32[]{:S(2)}, u32[]{:S(2)}) %all-to-all-start.1) | async-done | bytes 524320 | tf_op jit(solution)/shard_map/all_to_all | solution.py:499
  77.1 1.0 copy-done.1
  78.1 4.7 %attention_grad.1.rest_0_.rest_4_ = bf16[4,256,256]{2,1,0:T(8,128)(2,1)} custom-call(s32[4]{0:T(128)} %iota_xor_fusion.order, bf16[256,2048]{1,0:T(8,128)(2,1)} %weight_ref.1, bf16[256,2048]{1,0:T(8,128)(2,1)} %rest_0_.1, bf16[256,2048]{1,0:T(8,128)(2,1)} %copy-done.1, bf16[256,2048]{1,0:T(8,128)(2,1)} %copy-done, ...), custom_call_target="tpu_custom_call" | custom-call | flops 1000000000 | bytes 1000000 | tf_op jit(solution)/shard_map/attention_grad/pallas_call | solution.py:520
  82.8 1.2 collective-permute-start.10
  83.9 1.7 collective-permute-start.8
  85.7 4.2 %collective-permute-start.9 = (bf16[4,256,256]{2,1,0:T(8,128)(2,1)}, bf16[4,256,256]{2,1,0:T(8,128)(2,1)S(1)}, u32[]{:S(2)}, u32[]{:S(2)}) collective-permute-start(bf16[4,256,256]{2,1,0:T(8,128)(2,1)} %attention_grad.1.rest_0_.rest_4_), channel_id=1, source_target_pairs={{0,16},{4,20},{8,24},{12,28},{16,0},{20,4},{24,8},{28,12},{1,17},{... | collective-permute-start | bytes 1572872 | tf_op jit(solution)/shard_map/ppermute | solution.py:496
  89.9 10.5 %local.1 = (f32[8,256,128]{2,1,0:T(8,128)}, f32[8,256,128]{2,1,0:T(8,128)}, bf16[1024,256]{1,0:T(8,128)(2,1)}, bf16[1024,256]{1,0:T(8,128)(2,1)}) custom-call(f32[4]{0:T(128)} %add_divide_fusion.gate, bf16[4,256,256]{2,1,0:T(8,128)(2,1)} %copy-done.3, bf16[1024,256]{1,0:T(8,128)(2,1)} %bitcast.62, bf16[1024,256]{1,0:T(8,128)(2,1)} %bitcast.5.v_ref, ...), custom_call_target="tpu_custom_call" | custom-call | flops 1000000000 | bytes 1000000 | tf_op jit(solution)/shard_map/local/pallas_call | solution.py:539
  100.4 13.8 %collective-permute-done.7.v_par = bf16[4096,256]{1,0:T(8,128)(2,1)} collective-permute-done((bf16[4096,256]{1,0:T(8,128)(2,1)}, bf16[4096,256]{1,0:T(8,128)(2,1)}, u32[]{:S(2)}, u32[]{:S(2)}) %collective-permute-start.7) | collective-permute-done | bytes 2097184 | tf_op jit(solution)/shard_map/ppermute | solution.py:506
  114.2 19.4 %memory_forward.1 = (bf16[8,256,128]{2,1,0:T(8,128)(2,1)}, bf16[8,256,128]{2,1,0:T(8,128)(2,1)}, bf16[8,256,128]{2,1,0:T(8,128)(2,1)}, bf16[8,256,128]{2,1,0:T(8...) custom-call(s32[8]{0:T(128)} %reduce_sum.39.counts, s32[128]{0:T(128)} %reshape.300.places, ...), custom_call_target="tpu_custom_call" | custom-call | flops 30000001024 | bytes 30000000 | tf_op jit(solution)/shard_map/memory_forward/pallas_call | solution.py:578
  133.7 5.5 %collective-permute-start.14 = (bf16[8,256,128]{2,1,0:T(8,128)(2,1)}, bf16[8,256,128]{2,1,0:T(8,128)(2,1)S(1)}, u32[]{:S(2)}, u32[]{:S(2)}) collective-permute-start(bf16[8,256,128]{2,1,0:T(8,128)(2,1)} %get-tuple-element.66), channel_id=1, source_target_pairs={{0,24},{4,28},{8,0},{12,4},{16,8},{20,12},{24,16},{28,20},{1,25},{... | collective-permute-start | bytes 1572872 | tf_op jit(solution)/shard_map/ppermute | solution.py:496
  139.2 1.3 collective-permute-start.15
  141.7 3.8 %statistics.1.rest_8_.rest_0_.rest_4_ = f32[4,8,2,512]{3,2,1,0:T(2,128)} custom-call(f32[4,8,1,512]{3,2,1,0:T(1,128)} %get-tuple-element.59.lse_ref, bf16[4,256,256]{2,1,0:T(8,128)(2,1)} %attention_grad.1.rest_0_.rest_4_, bf16[4,256,256]{2,1,0:T(8,128)(2,1)} %copy-done.12, bf16[4,256,256]{2,1,0:T(8,128)(2,1)} %copy-done.13, bf16[4,256,256]{2,1,0:T(8,128)(2,1)} %copy-done.11, ...), custom_call_target="tpu_custom_call" | custom-call | flops 5000000000 | bytes 5000000 | tf_op jit(solution)/shard_map/statistics/pallas_call | solution.py:601
  145.5 1.9 collective-permute-start.11
  147.4 2.6 collective-permute-start.13
  150.0 27.5 %memory_backward.1 = (f32[4,8,256,128]{3,2,1,0:T(8,128)}, f32[4,8,256,128]{3,2,1,0:T(8,128)}) custom-call(s32[8]{0:T(128)} %reduce_sum.39.counts, s32[128]{0:T(128)} %reshape.300.places, s32[128]{0:T(128)} %add.136.homes, bf16[4096,256]{1,0:T(8,128)(2,1)} %k_own.3, bf16[4096,256]{1,0:T(8,128)(2,1)} %collective-permute-done.6.k_par, bf16[4096,256]{1,0:T(8,128)(2,1)} %v_own.3, ...), custom_call_target="tpu_custom_call" | custom-call | flops 30000001024 | bytes 30000000 | tf_op jit(solution)/shard_map/memory_backward/pallas_call | solution.py:629
  177.6 4.6 %collective-permute-start.16 = (bf16[8,256,128]{2,1,0:T(8,128)(2,1)S(1)}, bf16[8,256,128]{2,1,0:T(8,128)(2,1)S(1)}, u32[]{:S(2)}, u32[]{:S(2)}) collective-permute-start(bf16[8,256,128]{2,1,0:T(8,128)(2,1)S(1)} %copy-done.8), channel_id=1, source_target_pairs={{0,8},{4,12},{8,16},{12,20},{16,24},{20,28},{24,0},{28,4},{1,9},{5... | collective-permute-start | bytes 1572872 | tf_op jit(solution)/shard_map/ppermute | solution.py:496
  182.1 12.9 %collective-permute-done.12.rest_2_.rest_6_ = f32[4,8,2,512]{3,2,1,0:T(2,128)S(1)} collective-permute-done((f32[4,8,2,512]{3,2,1,0:T(2,128)}, f32[4,8,2,512]{3,2,1,0:T(2,128)S(1)}, u32[]{:S(2)}, u32[]{:S(2)}) %collective-permute-start.12) | collective-permute-done | bytes 131104 | tf_op jit(solution)/shard_map/ppermute | solution.py:496
  195.8 5.0 %combine.1 = (bf16[8,256,128]{2,1,0:T(8,128)(2,1)}, bf16[8,256,128]{2,1,0:T(8,128)(2,1)}, bf16[8,256,128]{2,1,0:T(8,128)(2,1)}, bf16[8,256,128]{2,1,0:T(8,128)(2,1)}) custom-call(f32[4,8,2,512]{3,2,1,0:T(2,128)} %statistics.1.rest_8_.rest_0_.rest_4_, f32[4,8,2,512]{3,2,1,0:T(2,128)} %copy-done.15, f32[4,8,2,512]{3,2,1,0:T(2,128)} %copy-done.16, ...), custom_call_target="tpu_custom_call" | custom-call | flops 5000000000 | bytes 5000000 | tf_op jit(solution)/shard_map/combine/pallas_call | solution.py:650
  200.7 3.5 %all-to-all-start.5 = ((bf16[4,256,256]{2,1,0:T(8,128)(2,1)}), bf16[4,256,256]{2,1,0:T(8,128)(2,1)S(1)}, u32[]{:S(2)}, u32[]{:S(2)}) async-start(bf16[4,256,256]{2,1,0:T(8,128)(2,1)} %bitcast.14), calls=%async_computation.5 | async-start | bytes 1048576 | tf_op jit(solution)/shard_map/all_to_all | solution.py:499
  205.8 3.4 %collective-permute-start.18 = (bf16[8,256,128]{2,1,0:T(8,128)(2,1)}, bf16[8,256,128]{2,1,0:T(8,128)(2,1)S(1)}, u32[]{:S(2)}, u32[]{:S(2)}) collective-permute-start(bf16[8,256,128]{2,1,0:T(8,128)(2,1)} %get-tuple-element.77), channel_id=1, source_target_pairs={{0,16},{4,20},{8,24},{12,28},{16,0},{20,4},{24,8},{28,12},{1,17},{... | collective-permute-start | bytes 1572872 | tf_op jit(solution)/shard_map/ppermute | solution.py:496
  209.2 3.0 %attention.1 = (bf16[1024,256]{1,0:T(8,128)(2,1)}, bf16[256,1024]{1,0:T(8,128)(2,1)}) custom-call(f32[4]{0:T(128)} %add_divide_fusion.gate, f32[8,256,128]{2,1,0:T(8,128)} %get-tuple-element.54.local_ref, bf16[8,256,128]{2,1,0:T(8,128)(2,1)} %get-tuple-element.69.rest_0_, bf16[8,256,128]{2,1,0:T(8,128)(2,1)} %copy-done.6, bf16[8,256,128]{2,1,0:T(8,128)(2,1)} %copy-done.7, ...), custom_call_target="tpu_custom_call" | custom-call | flops 3000000000 | bytes 3000000 | tf_op jit(solution)/shard_map/attention/pallas_call | solution.py:683
  212.2 0.8 all-to-all-done.5
  213.0 3.5 %all-to-all-start.3 = ((bf16[4,256,256]{2,1,0:T(8,128)(2,1)}), bf16[4,256,256]{2,1,0:T(8,128)(2,1)S(1)}, u32[]{:S(2)}, u32[]{:S(2)}) async-start(bf16[4,256,256]{2,1,0:T(8,128)(2,1)} %bitcast.66), calls=%async_computation.3 | async-start | bytes 1048576 | tf_op jit(solution)/shard_map/all_to_all | solution.py:499
  216.5 5.8 %weight_grad.1 = (bf16[4,256,256]{2,1,0:T(8,128)(2,1)}, bf16[4,256,256]{2,1,0:T(8,128)(2,1)}) custom-call(s32[4]{0:T(128)} %iota_xor_fusion.order, s32[5]{0:T(128)} %pad_add_fusion.dests, bf16[256,1024]{1,0:T(8,128)(2,1)} %get-tuple-element.86.attention_ref, bf16[256,2048]{1,0:T(8,128)(2,1)} %rest_0_.1, bf16[256,2048]{1,0:T(8,128)(2,1)} %copy-done.1, ...), custom_call_target="tpu_custom_call" | custom-call | flops 5000000000 | bytes 5000000 | tf_op jit(solution)/shard_map/weight_grad/pallas_call | solution.py:698
  222.3 3.0 %all-to-all-done.3 = bf16[4,256,256]{2,1,0:T(8,128)(2,1)S(1)} async-done(((bf16[4,256,256]{2,1,0:T(8,128)(2,1)}), bf16[4,256,256]{2,1,0:T(8,128)(2,1)S(1)}, u32[]{:S(2)}, u32[]{:S(2)}) %all-to-all-start.3) | async-done | bytes 524320 | tf_op jit(solution)/shard_map/all_to_all | solution.py:499
  225.3 3.5 %all-to-all-start.6 = ((bf16[4,256,256]{2,1,0:T(8,128)(2,1)}), bf16[4,256,256]{2,1,0:T(8,128)(2,1)S(1)}, u32[]{:S(2)}, u32[]{:S(2)}) async-start(bf16[4,256,256]{2,1,0:T(8,128)(2,1)} %bitcast.16), calls=%async_computation.6 | async-start | bytes 1048576 | tf_op jit(solution)/shard_map/all_to_all | solution.py:499
  228.8 4.4 %fusion = bf16[256,2048]{1,0:T(8,128)(2,1)} fusion(bf16[4,256,256]{2,1,0:T(8,128)(2,1)S(1)} %all-to-all-done.3, bf16[4,256,2048]{2,1,0:T(8,128)(2,1)} %bitcast.70), kind=kOutput, calls=%fused_computation.2 | convolution fusion | flops 1074266112 | bytes 5767168 | tf_op jit(solution)/shard_map/stc,scd->td/dot_general | solution.py:718
  233.2 22.1 %collective-permute-done.18.rest_2_ = bf16[8,256,128]{2,1,0:T(8,128)(2,1)S(1)} collective-permute-done((bf16[8,256,128]{2,1,0:T(8,128)(2,1)}, bf16[8,256,128]{2,1,0:T(8,128)(2,1)S(1)}, u32[]{:S(2)}, u32[]{:S(2)}) %collective-permute-start.18) | collective-permute-done | bytes 524320 | tf_op jit(solution)/shard_map/ppermute | solution.py:496
  256.1 2.8 query_grad.1
  258.9 3.5 %all-to-all-start.4 = ((bf16[4,256,256]{2,1,0:T(8,128)(2,1)}), bf16[4,256,256]{2,1,0:T(8,128)(2,1)S(1)}, u32[]{:S(2)}, u32[]{:S(2)}) async-start(bf16[4,256,256]{2,1,0:T(8,128)(2,1)} %bitcast.63), calls=%async_computation.4 | async-start | bytes 1048576 | tf_op jit(solution)/shard_map/all_to_all | solution.py:499
  262.7 1.9 collective-permute-start.23
  264.6 0.9 copy.45
  265.5 0.9 copy.46
  266.3 3.3 %collective-permute-done.21 = bf16[256,256]{1,0:T(8,128)(2,1)S(1)} collective-permute-done((bf16[256,256]{1,0:T(8,128)(2,1)S(1)}, bf16[256,256]{1,0:T(8,128)(2,1)S(1)}, u32[]{:S(2)}, u32[]{:S(2)}) %collective-permute-start.21) | collective-permute-done | bytes 131104 | tf_op jit(solution)/shard_map/ppermute | solution.py:496
  269.6 5.5 %collective-permute-done.22 = bf16[256,256]{1,0:T(8,128)(2,1)S(1)} collective-permute-done((bf16[256,256]{1,0:T(8,128)(2,1)S(1)}, bf16[256,256]{1,0:T(8,128)(2,1)S(1)}, u32[]{:S(2)}, u32[]{:S(2)}) %collective-permute-start.22) | collective-permute-done | bytes 131104 | tf_op jit(solution)/shard_map/ppermute | solution.py:496
  275.9 0.9 copy.44
  (97 shorter events, 13.0 us)
Async XLA Ops:
  7.2 56.8 %copy-start.2 = (bf16[256,1024]{1,0:T(8,128)(2,1)S(1)}, bf16[256,1024]{1,0:T(8,128)(2,1)}, u32[]{:S(2)}) copy-start(bf16[256,1024]{1,0:T(8,128)(2,1)} %param.10) | copy-start | bytes 1572868
  7.2 63.9 %copy-start.18 = (f32[16]{0:T(128)S(1)}, f32[16]{0:T(128)}, u32[]{:S(2)}) copy-start(f32[16]{0:T(128)} %param.15) | copy-start | bytes 196
  21.4 61.3 %copy-start.3 = (bf16[4,256,256]{2,1,0:T(8,128)(2,1)}, bf16[4,256,256]{2,1,0:T(8,128)(2,1)S(1)}, u32[]{:S(2)}) copy-start(bf16[4,256,256]{2,1,0:T(8,128)(2,1)S(1)} %all_to_all.35.q_ref.rest_0_) | copy-start | bytes 1572868
  21.4 24.7 %collective-permute-start.4 = (bf16[256,2048]{1,0:T(8,128)(2,1)}, bf16[256,2048]{1,0:T(8,128)(2,1)S(1)}, u32[]{:S(2)}, u32[]{:S(2)}) collective-permute-start(bf16[256,2048]{1,0:T(8,128)(2,1)} %rest_0_.1), channel_id=1, source_target_pairs={{0,2},{1,3},{2,0},{3,1},{4,6},{5,7},{6,4},{7,5},{8,10},{9,11},{10,... | collective-permute-start | bytes 3145736 | tf_op jit(solution)/shard_map/ppermute | solution.py:446
  21.8 78.6 %collective-permute-start.6 = (bf16[4096,256]{1,0:T(8,128)(2,1)}, bf16[4096,256]{1,0:T(8,128)(2,1)}, u32[]{:S(2)}, u32[]{:S(2)}) collective-permute-start(bf16[4096,256]{1,0:T(8,128)(2,1)} %k_own.3), channel_id=1, source_target_pairs={{0,4},{4,0},{8,12},{12,8},{16,20},{20,16},{24,28},{28,24},{1,5},{5... | collective-permute-start | bytes 6291464 | tf_op jit(solution)/shard_map/ppermute | solution.py:505
  23.3 90.9 %collective-permute-start.7 = (bf16[4096,256]{1,0:T(8,128)(2,1)}, bf16[4096,256]{1,0:T(8,128)(2,1)}, u32[]{:S(2)}, u32[]{:S(2)}) collective-permute-start(bf16[4096,256]{1,0:T(8,128)(2,1)} %v_own.3), channel_id=1, source_target_pairs={{0,4},{4,0},{8,12},{12,8},{16,20},{20,16},{24,28},{28,24},{1,5},{5... | collective-permute-start | bytes 6291464 | tf_op jit(solution)/shard_map/ppermute | solution.py:506
  24.9 16.9 %collective-permute-start = (bf16[4,256,256]{2,1,0:T(8,128)(2,1)S(1)}, bf16[4,256,256]{2,1,0:T(8,128)(2,1)}, u32[]{:S(2)}, u32[]{:S(2)}) collective-permute-start(bf16[4,256,256]{2,1,0:T(8,128)(2,1)S(1)} %all_to_all.35.q_ref.rest_0_), channel_id=1, source_target_pairs={{0,8},{4,12},{8,16},{12,20},{16,24},{20,28},{24,0},{28,4},{1,9},{5... | collective-permute-start | bytes 1572872 | tf_op jit(solution)/shard_map/ppermute | solution.py:496
  27.2 35.1 %collective-permute-start.1 = (bf16[4,256,256]{2,1,0:T(8,128)(2,1)S(1)}, bf16[4,256,256]{2,1,0:T(8,128)(2,1)}, u32[]{:S(2)}, u32[]{:S(2)}) collective-permute-start(bf16[4,256,256]{2,1,0:T(8,128)(2,1)S(1)} %all_to_all.35.q_ref.rest_0_), channel_id=1, source_target_pairs={{0,16},{4,20},{8,24},{12,28},{16,0},{20,4},{24,8},{28,12},{1,17},{... | collective-permute-start | bytes 1572872 | tf_op jit(solution)/shard_map/ppermute | solution.py:496
  41.8 35.3 %collective-permute-start.3 = (bf16[256,2048]{1,0:T(8,128)(2,1)}, bf16[256,2048]{1,0:T(8,128)(2,1)S(1)}, u32[]{:S(2)}, u32[]{:S(2)}) collective-permute-start(bf16[256,2048]{1,0:T(8,128)(2,1)} %rest_0_.1), channel_id=1, source_target_pairs={{0,1},{1,0},{2,3},{3,2},{4,5},{5,4},{6,7},{7,6},{8,9},{9,8},{10,11... | collective-permute-start | bytes 3145736 | tf_op jit(solution)/shard_map/ppermute | solution.py:447
  46.2 31.0 %copy-start = (bf16[256,2048]{1,0:T(8,128)(2,1)}, bf16[256,2048]{1,0:T(8,128)(2,1)S(1)}, u32[]{:S(2)}) copy-start(bf16[256,2048]{1,0:T(8,128)(2,1)S(1)} %collective-permute-done.4.rest_2_) | copy-start | bytes 3145732
  46.2 30.9 %collective-permute-start.5 = (bf16[256,2048]{1,0:T(8,128)(2,1)S(1)}, bf16[256,2048]{1,0:T(8,128)(2,1)}, u32[]{:S(2)}, u32[]{:S(2)}) collective-permute-start(bf16[256,2048]{1,0:T(8,128)(2,1)S(1)} %collective-permute-done.4.rest_2_), channel_id=1, source_target_pairs={{0,1},{1,0},{2,3},{3,2},{4,5},{5,4},{6,7},{7,6},{8,9},{9,8},{10,11... | collective-permute-start | bytes 3145736 | tf_op jit(solution)/shard_map/ppermute | solution.py:448
  48.4 16.4 %all-to-all-start.2 = ((bf16[4,256,256]{2,1,0:T(8,128)(2,1)}), bf16[4,256,256]{2,1,0:T(8,128)(2,1)}, u32[]{:S(2)}, u32[]{:S(2)}) async-start(bf16[4,256,256]{2,1,0:T(8,128)(2,1)} %bitcast.53), calls=%async_computation.2 | async-start | bytes 1048576 | tf_op jit(solution)/shard_map/all_to_all | solution.py:499
  62.3 14.8 %collective-permute-start.2 = (bf16[4,256,256]{2,1,0:T(8,128)(2,1)S(1)}, bf16[4,256,256]{2,1,0:T(8,128)(2,1)}, u32[]{:S(2)}, u32[]{:S(2)}) collective-permute-start(bf16[4,256,256]{2,1,0:T(8,128)(2,1)S(1)} %all_to_all.35.q_ref.rest_0_), channel_id=1, source_target_pairs={{0,24},{4,28},{8,0},{12,4},{16,8},{20,12},{24,16},{28,20},{1,25},{... | collective-permute-start | bytes 1572872 | tf_op jit(solution)/shard_map/ppermute | solution.py:496
  64.8 12.3 %all-to-all-start.1 = ((bf16[4,256,256]{2,1,0:T(8,128)(2,1)}), bf16[4,256,256]{2,1,0:T(8,128)(2,1)S(1)}, u32[]{:S(2)}, u32[]{:S(2)}) async-start(bf16[4,256,256]{2,1,0:T(8,128)(2,1)} %bitcast.55), calls=%async_computation.1 | async-start | bytes 1048576 | tf_op jit(solution)/shard_map/all_to_all | solution.py:499
  68.3 160.5 %all-gather.2.cloned.1.call-start = ((), (), s32[]{:S(2)}) async-start(), calls=%async_computation.7 | async-start | bytes 5242880 | tf_op jit(solution)/shard_map/all_gather | solution.py:531
  77.1 12.8 %copy-start.5 = (bf16[4,256,256]{2,1,0:T(8,128)(2,1)}, bf16[4,256,256]{2,1,0:T(8,128)(2,1)S(1)}, u32[]{:S(2)}) copy-start(bf16[4,256,256]{2,1,0:T(8,128)(2,1)S(1)} %all-to-all-done.1) | copy-start | bytes 1572868
  77.1 1.0 copy-start.1
  82.8 57.8 %collective-permute-start.10 = (bf16[4,256,256]{2,1,0:T(8,128)(2,1)}, bf16[4,256,256]{2,1,0:T(8,128)(2,1)S(1)}, u32[]{:S(2)}, u32[]{:S(2)}) collective-permute-start(bf16[4,256,256]{2,1,0:T(8,128)(2,1)} %attention_grad.1.rest_0_.rest_4_), channel_id=1, source_target_pairs={{0,24},{4,28},{8,0},{12,4},{16,8},{20,12},{24,16},{28,20},{1,25},{... | collective-permute-start | bytes 1572872 | tf_op jit(solution)/shard_map/ppermute | solution.py:496
  83.9 56.6 %collective-permute-start.8 = (bf16[4,256,256]{2,1,0:T(8,128)(2,1)}, bf16[4,256,256]{2,1,0:T(8,128)(2,1)S(1)}, u32[]{:S(2)}, u32[]{:S(2)}) collective-permute-start(bf16[4,256,256]{2,1,0:T(8,128)(2,1)} %attention_grad.1.rest_0_.rest_4_), channel_id=1, source_target_pairs={{0,8},{4,12},{8,16},{12,20},{16,24},{20,28},{24,0},{28,4},{1,9},{5... | collective-permute-start | bytes 1572872 | tf_op jit(solution)/shard_map/ppermute | solution.py:496
  85.7 54.9 %collective-permute-start.9 = (bf16[4,256,256]{2,1,0:T(8,128)(2,1)}, bf16[4,256,256]{2,1,0:T(8,128)(2,1)S(1)}, u32[]{:S(2)}, u32[]{:S(2)}) collective-permute-start(bf16[4,256,256]{2,1,0:T(8,128)(2,1)} %attention_grad.1.rest_0_.rest_4_), channel_id=1, source_target_pairs={{0,16},{4,20},{8,24},{12,28},{16,0},{20,4},{24,8},{28,12},{1,17},{... | collective-permute-start | bytes 1572872 | tf_op jit(solution)/shard_map/ppermute | solution.py:496
  133.7 71.2 %collective-permute-start.14 = (bf16[8,256,128]{2,1,0:T(8,128)(2,1)}, bf16[8,256,128]{2,1,0:T(8,128)(2,1)S(1)}, u32[]{:S(2)}, u32[]{:S(2)}) collective-permute-start(bf16[8,256,128]{2,1,0:T(8,128)(2,1)} %get-tuple-element.66), channel_id=1, source_target_pairs={{0,24},{4,28},{8,0},{12,4},{16,8},{20,12},{24,16},{28,20},{1,25},{... | collective-permute-start | bytes 1572872 | tf_op jit(solution)/shard_map/ppermute | solution.py:496
  139.2 65.7 %collective-permute-start.15 = (bf16[8,256,128]{2,1,0:T(8,128)(2,1)}, bf16[8,256,128]{2,1,0:T(8,128)(2,1)S(1)}, u32[]{:S(2)}, u32[]{:S(2)}) collective-permute-start(bf16[8,256,128]{2,1,0:T(8,128)(2,1)} %get-tuple-element.67), channel_id=1, source_target_pairs={{0,16},{4,20},{8,24},{12,28},{16,0},{20,4},{24,8},{28,12},{1,17},{... | collective-permute-start | bytes 1572872 | tf_op jit(solution)/shard_map/ppermute | solution.py:496
  140.5 0.8 copy-start.11
  140.5 1.0 copy-start.12
  140.6 1.1 copy-start.13
  145.5 32.1 %copy-start.8 = (bf16[8,256,128]{2,1,0:T(8,128)(2,1)S(1)}, bf16[8,256,128]{2,1,0:T(8,128)(2,1)}, u32[]{:S(2)}) copy-start(bf16[8,256,128]{2,1,0:T(8,128)(2,1)} %get-tuple-element.68) | copy-start | bytes 1572868
  145.5 32.1 %collective-permute-start.11 = (f32[4,8,2,512]{3,2,1,0:T(2,128)}, f32[4,8,2,512]{3,2,1,0:T(2,128)S(1)}, u32[]{:S(2)}, u32[]{:S(2)}) collective-permute-start(f32[4,8,2,512]{3,2,1,0:T(2,128)} %statistics.1.rest_8_.rest_0_.rest_4_), channel_id=1, source_target_pairs={{0,8},{4,12},{8,16},{12,20},{16,24},{20,28},{24,0},{28,4},{1,9},{5... | collective-permute-start | bytes 393224 | tf_op jit(solution)/shard_map/ppermute | solution.py:496
  147.4 47.6 %collective-permute-start.12 = (f32[4,8,2,512]{3,2,1,0:T(2,128)}, f32[4,8,2,512]{3,2,1,0:T(2,128)S(1)}, u32[]{:S(2)}, u32[]{:S(2)}) collective-permute-start(f32[4,8,2,512]{3,2,1,0:T(2,128)} %statistics.1.rest_8_.rest_0_.rest_4_), channel_id=1, source_target_pairs={{0,16},{4,20},{8,24},{12,28},{16,0},{20,4},{24,8},{28,12},{1,17},{... | collective-permute-start | bytes 393224 | tf_op jit(solution)/shard_map/ppermute | solution.py:496
  147.4 47.6 %collective-permute-start.13 = (f32[4,8,2,512]{3,2,1,0:T(2,128)}, f32[4,8,2,512]{3,2,1,0:T(2,128)S(1)}, u32[]{:S(2)}, u32[]{:S(2)}) collective-permute-start(f32[4,8,2,512]{3,2,1,0:T(2,128)} %statistics.1.rest_8_.rest_0_.rest_4_), channel_id=1, source_target_pairs={{0,24},{4,28},{8,0},{12,4},{16,8},{20,12},{24,16},{28,20},{1,25},{... | collective-permute-start | bytes 393224 | tf_op jit(solution)/shard_map/ppermute | solution.py:496
  177.6 17.5 %copy-start.15 = (f32[4,8,2,512]{3,2,1,0:T(2,128)}, f32[4,8,2,512]{3,2,1,0:T(2,128)S(1)}, u32[]{:S(2)}) copy-start(f32[4,8,2,512]{3,2,1,0:T(2,128)S(1)} %collective-permute-done.11.rest_1_.rest_7_) | copy-start | bytes 393220
  177.6 27.3 %collective-permute-start.16 = (bf16[8,256,128]{2,1,0:T(8,128)(2,1)S(1)}, bf16[8,256,128]{2,1,0:T(8,128)(2,1)S(1)}, u32[]{:S(2)}, u32[]{:S(2)}) collective-permute-start(bf16[8,256,128]{2,1,0:T(8,128)(2,1)S(1)} %copy-done.8), channel_id=1, source_target_pairs={{0,8},{4,12},{8,16},{12,20},{16,24},{20,28},{24,0},{28,4},{1,9},{5... | collective-permute-start | bytes 1572872 | tf_op jit(solution)/shard_map/ppermute | solution.py:496
  200.7 12.3 %all-to-all-start.5 = ((bf16[4,256,256]{2,1,0:T(8,128)(2,1)}), bf16[4,256,256]{2,1,0:T(8,128)(2,1)S(1)}, u32[]{:S(2)}, u32[]{:S(2)}) async-start(bf16[4,256,256]{2,1,0:T(8,128)(2,1)} %bitcast.14), calls=%async_computation.5 | async-start | bytes 1048576 | tf_op jit(solution)/shard_map/all_to_all | solution.py:499
  204.9 4.3 %copy-start.6 = (bf16[8,256,128]{2,1,0:T(8,128)(2,1)}, bf16[8,256,128]{2,1,0:T(8,128)(2,1)S(1)}, u32[]{:S(2)}) copy-start(bf16[8,256,128]{2,1,0:T(8,128)(2,1)S(1)} %collective-permute-done.14.rest_1_) | copy-start | bytes 1572868
  204.9 4.2 %copy-start.7 = (bf16[8,256,128]{2,1,0:T(8,128)(2,1)}, bf16[8,256,128]{2,1,0:T(8,128)(2,1)S(1)}, u32[]{:S(2)}) copy-start(bf16[8,256,128]{2,1,0:T(8,128)(2,1)S(1)} %collective-permute-done.15.rest_2_) | copy-start | bytes 1572868
  204.9 0.9 copy-start.14
  205.8 27.5 %collective-permute-start.17 = (bf16[8,256,128]{2,1,0:T(8,128)(2,1)}, bf16[8,256,128]{2,1,0:T(8,128)(2,1)S(1)}, u32[]{:S(2)}, u32[]{:S(2)}) collective-permute-start(bf16[8,256,128]{2,1,0:T(8,128)(2,1)} %get-tuple-element.76), channel_id=1, source_target_pairs={{0,24},{4,28},{8,0},{12,4},{16,8},{20,12},{24,16},{28,20},{1,25},{... | collective-permute-start | bytes 1572872 | tf_op jit(solution)/shard_map/ppermute | solution.py:496
  205.8 49.5 %collective-permute-start.18 = (bf16[8,256,128]{2,1,0:T(8,128)(2,1)}, bf16[8,256,128]{2,1,0:T(8,128)(2,1)S(1)}, u32[]{:S(2)}, u32[]{:S(2)}) collective-permute-start(bf16[8,256,128]{2,1,0:T(8,128)(2,1)} %get-tuple-element.77), channel_id=1, source_target_pairs={{0,16},{4,20},{8,24},{12,28},{16,0},{20,4},{24,8},{28,12},{1,17},{... | collective-permute-start | bytes 1572872 | tf_op jit(solution)/shard_map/ppermute | solution.py:496
  209.1 46.2 %collective-permute-start.19 = (bf16[8,256,128]{2,1,0:T(8,128)(2,1)}, bf16[8,256,128]{2,1,0:T(8,128)(2,1)}, u32[]{:S(2)}, u32[]{:S(2)}) collective-permute-start(bf16[8,256,128]{2,1,0:T(8,128)(2,1)} %get-tuple-element.78), channel_id=1, source_target_pairs={{0,8},{4,12},{8,16},{12,20},{16,24},{20,28},{24,0},{28,4},{1,9},{5... | collective-permute-start | bytes 1572872 | tf_op jit(solution)/shard_map/ppermute | solution.py:496
  213.0 12.3 %all-to-all-start.3 = ((bf16[4,256,256]{2,1,0:T(8,128)(2,1)}), bf16[4,256,256]{2,1,0:T(8,128)(2,1)S(1)}, u32[]{:S(2)}, u32[]{:S(2)}) async-start(bf16[4,256,256]{2,1,0:T(8,128)(2,1)} %bitcast.66), calls=%async_computation.3 | async-start | bytes 1048576 | tf_op jit(solution)/shard_map/all_to_all | solution.py:499
  222.3 40.1 %collective-permute-start.20 = (bf16[4,256,256]{2,1,0:T(8,128)(2,1)}, bf16[4,256,256]{2,1,0:T(8,128)(2,1)S(1)}, u32[]{:S(2)}, u32[]{:S(2)}) collective-permute-start(bf16[4,256,256]{2,1,0:T(8,128)(2,1)} %get-tuple-element.88), channel_id=1, source_target_pairs={{0,4},{4,0},{8,12},{12,8},{16,20},{20,16},{24,28},{28,24},{1,5},{5... | collective-permute-start | bytes 1572872 | tf_op jit(solution)/shard_map/ppermute | solution.py:712
  225.3 33.6 %all-to-all-start.6 = ((bf16[4,256,256]{2,1,0:T(8,128)(2,1)}), bf16[4,256,256]{2,1,0:T(8,128)(2,1)S(1)}, u32[]{:S(2)}, u32[]{:S(2)}) async-start(bf16[4,256,256]{2,1,0:T(8,128)(2,1)} %bitcast.16), calls=%async_computation.6 | async-start | bytes 1048576 | tf_op jit(solution)/shard_map/all_to_all | solution.py:499
  233.2 22.1 %copy-start.9 = (bf16[8,256,128]{2,1,0:T(8,128)(2,1)}, bf16[8,256,128]{2,1,0:T(8,128)(2,1)S(1)}, u32[]{:S(2)}) copy-start(bf16[8,256,128]{2,1,0:T(8,128)(2,1)S(1)} %collective-permute-done.17.rest_1_) | copy-start | bytes 1572868
  255.3 0.8 copy-start.10
  256.1 6.3 %copy-start.4 = (bf16[4,256,256]{2,1,0:T(8,128)(2,1)S(1)}, bf16[4,256,256]{2,1,0:T(8,128)(2,1)}, u32[]{:S(2)}) copy-start(bf16[4,256,256]{2,1,0:T(8,128)(2,1)} %get-tuple-element.87) | copy-start | bytes 1572868
  258.9 16.9 %all-to-all-start.4 = ((bf16[4,256,256]{2,1,0:T(8,128)(2,1)}), bf16[4,256,256]{2,1,0:T(8,128)(2,1)S(1)}, u32[]{:S(2)}, u32[]{:S(2)}) async-start(bf16[4,256,256]{2,1,0:T(8,128)(2,1)} %bitcast.63), calls=%async_computation.4 | async-start | bytes 1048576 | tf_op jit(solution)/shard_map/all_to_all | solution.py:499
  262.5 7.1 %collective-permute-start.21 = (bf16[256,256]{1,0:T(8,128)(2,1)S(1)}, bf16[256,256]{1,0:T(8,128)(2,1)S(1)}, u32[]{:S(2)}, u32[]{:S(2)}) collective-permute-start(bf16[256,256]{1,0:T(8,128)(2,1)S(1)} %get-tuple-element.91), channel_id=1, source_target_pairs={{0,24},{4,28},{8,0},{12,4},{16,8},{20,12},{24,16},{28,20},{1,25},{... | collective-permute-start | bytes 393224 | tf_op jit(solution)/shard_map/ppermute | solution.py:496
  262.6 12.5 %collective-permute-start.22 = (bf16[256,256]{1,0:T(8,128)(2,1)S(1)}, bf16[256,256]{1,0:T(8,128)(2,1)S(1)}, u32[]{:S(2)}, u32[]{:S(2)}) collective-permute-start(bf16[256,256]{1,0:T(8,128)(2,1)S(1)} %get-tuple-element.93), channel_id=1, source_target_pairs={{0,16},{4,20},{8,24},{12,28},{16,0},{20,4},{24,8},{28,12},{1,17},{... | collective-permute-start | bytes 393224 | tf_op jit(solution)/shard_map/ppermute | solution.py:496
  262.7 12.4 %collective-permute-start.23 = (bf16[256,256]{1,0:T(8,128)(2,1)S(1)}, bf16[256,256]{1,0:T(8,128)(2,1)S(1)}, u32[]{:S(2)}, u32[]{:S(2)}) collective-permute-start(bf16[256,256]{1,0:T(8,128)(2,1)S(1)} %get-tuple-element.92), channel_id=1, source_target_pairs={{0,8},{4,12},{8,16},{12,20},{16,24},{20,28},{24,0},{28,4},{1,9},{5... | collective-permute-start | bytes 393224 | tf_op jit(solution)/shard_map/ppermute | solution.py:496
  (2 other events, 1.4 us)
Sparse Core Ops, SparseCore 0:
  71.9 37.1 all-gather.1

commit v2 on v1

--- a/solution.py
+++ b/solution.py
@@ -11,7 +11,7 @@
 QBLK = 128
 MBLK = 128
 LOW = -1e30
-UNROLL = 4
+UNROLL = 8
 HALVES = 1
 ORDER = False
 VMEM = 58 * 2**20
@@ -713,6 +713,7 @@
         sums = [
             (keep[k].astype(F32) + got[k].astype(F32)).astype(BF) for k in range(group)
         ]
+        sums = after(dq_home, *sums)
         sums = [sums[0]] + [shifted(sums[k], -k) for k in range(1, group)]
         weight_rows.append(functools.reduce(jnp.add, [x.astype(F32) for x in sums]))
     projected = jnp.einsum(

time: 288 us -> 285 us (0.990)
  Pallas kernels: 82.6 us -> 76.4 us
  starting transfers between devices: 58.3 us -> 64.4 us
    pallas_call x1, Pallas kernels: 27.5 us -> 23.2 us  [per_device(): pl.pallas_call(functools.partial(memory_backward, group, pairs, i), grid_...]
    ppermute x18, starting transfers between devices: 34.4 us -> 38 us  [shifted(): return lax.ppermute(x, 'mem', [(i, (i + 2 * k) % n) for i in range(n)])]
  transfers between devices with their start and end apart: 31 -> 31, of which waited for: 11 -> 11; matrix products, arithmetic and copies ran while one was open for 6% -> 6% of each run, Pallas kernels for 29% -> 27%
where the time goes in v2:
time: 285 us; the launch traced here: 283 us
  waiting for transfers between devices  92.3 us (32%)
  Pallas kernels  76.4 us (27%)
  starting transfers between devices  64.4 us (23%)
  between operations  14.4 us (5%)
  local copies, waits for them, and re-layouts  13.6 us (5%)
  blocking collectives  12.9 us (5%)
  other arithmetic  4.95 us (2%)
  matrix products  4.41 us (2%)
    ppermute x18, waiting for transfers between devices, shifted(): return lax.ppermute(x, 'mem', [(i, (i + 2 * k) % n) for i in range(n)])  66.7 us
    ppermute x18, starting transfers between devices, shifted(): return lax.ppermute(x, 'mem', [(i, (i + 2 * k) % n) for i in range(n)])  38 us
    pallas_call x1, Pallas kernels, per_device(): pl.pallas_call(functools.partial(memory_backward, group, pairs, i), grid_...  23.2 us
    all_to_all x6, starting transfers between devices, exchange(): return lax.all_to_all(x, 'fsdp', split_axis=0, concat_axis=0, tiled=True)  21.5 us
    pallas_call x1, Pallas kernels, per_device(): pl.pallas_call(functools.partial(memory_forward, group, pairs, i), grid_s...  17.5 us
    ppermute x1, waiting for transfers between devices, per_device(): par_values = [lax.ppermute(mem_values, 'mem', swap)]  13.8 us
    all_to_all x1, blocking collectives, exchange(): return lax.all_to_all(x, 'fsdp', split_axis=0, concat_axis=0, tiled=True)  12.9 us
    pallas_call x1, Pallas kernels, per_device(): pl.pallas_call(functools.partial(local_kernel, all_heads // 2, per_seg, H...  10.5 us
  transfers between devices with their start and end apart: 31, of which 11 were waited for; matrix products, arithmetic and copies ran while one was open for 6% of the time, Pallas kernels for 27%

profile of v2, /device:TPU:0, one launch (start us, length us, event | category | flops | bytes accessed | tf_op | source)
XLA Modules:
  0.0 283.4 jit_solution(15143202346027343888)
XLA Ops:
  7.2 1.1 multiply_bitcast_fusion
  8.5 12.9 %all_to_all.35.q_ref.rest_0_ = bf16[4,256,256]{2,1,0:T(8,128)(2,1)S(1)} all-to-all(bf16[4,256,256]{2,1,0:T(8,128)(2,1)S(1)} %bitcast.56), channel_id=1, replica_groups=mesh['mem'=8,'fsdp'=4] {'fsdp'}, dimensions={0} | all-to-all | bytes 1048576 | tf_op jit(solution)/shard_map/all_to_all | solution.py:499
  21.8 1.5 collective-permute-start.6
  24.9 1.6 collective-permute-start
  27.2 2.6 collective-permute-start.1
  30.0 11.9 %collective-permute-done.rest_1_ = bf16[4,256,256]{2,1,0:T(8,128)(2,1)} collective-permute-done((bf16[4,256,256]{2,1,0:T(8,128)(2,1)S(1)}, bf16[4,256,256]{2,1,0:T(8,128)(2,1)}, u32[]{:S(2)}, u32[]{:S(2)}) %collective-permute-start) | collective-permute-done | bytes 524320 | tf_op jit(solution)/shard_map/ppermute | solution.py:496
  41.9 4.3 %collective-permute-done.4.rest_2_ = bf16[256,2048]{1,0:T(8,128)(2,1)S(1)} collective-permute-done((bf16[256,2048]{1,0:T(8,128)(2,1)}, bf16[256,2048]{1,0:T(8,128)(2,1)S(1)}, u32[]{:S(2)}, u32[]{:S(2)}) %collective-permute-start.4) | collective-permute-done | bytes 1048608 | tf_op jit(solution)/shard_map/ppermute | solution.py:446
  46.4 2.0 copy.49
  48.4 4.1 %all-to-all-start.2 = ((bf16[4,256,256]{2,1,0:T(8,128)(2,1)}), bf16[4,256,256]{2,1,0:T(8,128)(2,1)}, u32[]{:S(2)}, u32[]{:S(2)}) async-start(bf16[4,256,256]{2,1,0:T(8,128)(2,1)} %bitcast.50), calls=%async_computation.2 | async-start | bytes 1048576 | tf_op jit(solution)/shard_map/all_to_all | solution.py:499
  52.9 9.4 %collective-permute-done.1.rest_2_ = bf16[4,256,256]{2,1,0:T(8,128)(2,1)} collective-permute-done((bf16[4,256,256]{2,1,0:T(8,128)(2,1)S(1)}, bf16[4,256,256]{2,1,0:T(8,128)(2,1)}, u32[]{:S(2)}, u32[]{:S(2)}) %collective-permute-start.1) | collective-permute-done | bytes 524320 | tf_op jit(solution)/shard_map/ppermute | solution.py:496
  62.3 1.6 collective-permute-start.2
  64.8 3.5 %all-to-all-start.1 = ((bf16[4,256,256]{2,1,0:T(8,128)(2,1)}), bf16[4,256,256]{2,1,0:T(8,128)(2,1)S(1)}, u32[]{:S(2)}, u32[]{:S(2)}) async-start(bf16[4,256,256]{2,1,0:T(8,128)(2,1)} %bitcast.52), calls=%async_computation.1 | async-start | bytes 1048576 | tf_op jit(solution)/shard_map/all_to_all | solution.py:499
  71.7 5.3 %all-to-all-done.1 = bf16[4,256,256]{2,1,0:T(8,128)(2,1)S(1)} async-done(((bf16[4,256,256]{2,1,0:T(8,128)(2,1)}), bf16[4,256,256]{2,1,0:T(8,128)(2,1)S(1)}, u32[]{:S(2)}, u32[]{:S(2)}) %all-to-all-start.1) | async-done | bytes 524320 | tf_op jit(solution)/shard_map/all_to_all | solution.py:499
  77.1 1.0 copy-done.1
  78.1 4.7 %attention_grad.1.rest_0_.rest_4_ = bf16[4,256,256]{2,1,0:T(8,128)(2,1)} custom-call(s32[4]{0:T(128)} %iota_xor_fusion.order, bf16[256,2048]{1,0:T(8,128)(2,1)} %weight_ref.1, bf16[256,2048]{1,0:T(8,128)(2,1)} %rest_0_.1, bf16[256,2048]{1,0:T(8,128)(2,1)} %copy-done.1, bf16[256,2048]{1,0:T(8,128)(2,1)} %copy-done, ...), custom_call_target="tpu_custom_call" | custom-call | flops 1000000000 | bytes 1000000 | tf_op jit(solution)/shard_map/attention_grad/pallas_call | solution.py:520
  82.8 1.2 collective-permute-start.10
  83.9 1.7 collective-permute-start.8
  85.7 4.2 %collective-permute-start.9 = (bf16[4,256,256]{2,1,0:T(8,128)(2,1)}, bf16[4,256,256]{2,1,0:T(8,128)(2,1)S(1)}, u32[]{:S(2)}, u32[]{:S(2)}) collective-permute-start(bf16[4,256,256]{2,1,0:T(8,128)(2,1)} %attention_grad.1.rest_0_.rest_4_), channel_id=1, source_target_pairs={{0,16},{4,20},{8,24},{12,28},{16,0},{20,4},{24,8},{28,12},{1,17},{... | collective-permute-start | bytes 1572872 | tf_op jit(solution)/shard_map/ppermute | solution.py:496
  89.9 10.5 %local.1 = (f32[8,256,128]{2,1,0:T(8,128)}, f32[8,256,128]{2,1,0:T(8,128)}, bf16[1024,256]{1,0:T(8,128)(2,1)}, bf16[1024,256]{1,0:T(8,128)(2,1)}) custom-call(f32[4]{0:T(128)} %add_divide_fusion.gate, bf16[4,256,256]{2,1,0:T(8,128)(2,1)} %copy-done.4, bf16[1024,256]{1,0:T(8,128)(2,1)} %bitcast.59, bf16[1024,256]{1,0:T(8,128)(2,1)} %bitcast.5.v_ref, ...), custom_call_target="tpu_custom_call" | custom-call | flops 1000000000 | bytes 1000000 | tf_op jit(solution)/shard_map/local/pallas_call | solution.py:539
  100.4 13.8 %collective-permute-done.7.v_par = bf16[4096,256]{1,0:T(8,128)(2,1)} collective-permute-done((bf16[4096,256]{1,0:T(8,128)(2,1)}, bf16[4096,256]{1,0:T(8,128)(2,1)}, u32[]{:S(2)}, u32[]{:S(2)}) %collective-permute-start.7) | collective-permute-done | bytes 2097184 | tf_op jit(solution)/shard_map/ppermute | solution.py:506
  114.2 17.5 %memory_forward.1 = (bf16[8,256,128]{2,1,0:T(8,128)(2,1)}, bf16[8,256,128]{2,1,0:T(8,128)(2,1)}, bf16[8,256,128]{2,1,0:T(8,128)(2,1)}, bf16[8,256,128]{2,1,0:T(8...) custom-call(s32[8]{0:T(128)} %reduce_sum.39.counts, s32[128]{0:T(128)} %reshape.298.places, ...), custom_call_target="tpu_custom_call" | custom-call | flops 30000001024 | bytes 30000000 | tf_op jit(solution)/shard_map/memory_forward/pallas_call | solution.py:578
  131.8 5.7 %collective-permute-start.14 = (bf16[8,256,128]{2,1,0:T(8,128)(2,1)}, bf16[8,256,128]{2,1,0:T(8,128)(2,1)S(1)}, u32[]{:S(2)}, u32[]{:S(2)}) collective-permute-start(bf16[8,256,128]{2,1,0:T(8,128)(2,1)} %get-tuple-element.70), channel_id=1, source_target_pairs={{0,24},{4,28},{8,0},{12,4},{16,8},{20,12},{24,16},{28,20},{1,25},{... | collective-permute-start | bytes 1572872 | tf_op jit(solution)/shard_map/ppermute | solution.py:496
  137.4 3.7 %collective-permute-start.15 = (bf16[8,256,128]{2,1,0:T(8,128)(2,1)}, bf16[8,256,128]{2,1,0:T(8,128)(2,1)S(1)}, u32[]{:S(2)}, u32[]{:S(2)}) collective-permute-start(bf16[8,256,128]{2,1,0:T(8,128)(2,1)} %get-tuple-element.71), channel_id=1, source_target_pairs={{0,16},{4,20},{8,24},{12,28},{16,0},{20,4},{24,8},{28,12},{1,17},{... | collective-permute-start | bytes 1572872 | tf_op jit(solution)/shard_map/ppermute | solution.py:496
  142.2 3.8 %statistics.1.rest_8_.rest_0_.rest_4_ = f32[4,8,2,512]{3,2,1,0:T(2,128)} custom-call(f32[4,8,1,512]{3,2,1,0:T(1,128)} %get-tuple-element.63.lse_ref, bf16[4,256,256]{2,1,0:T(8,128)(2,1)} %attention_grad.1.rest_0_.rest_4_, bf16[4,256,256]{2,1,0:T(8,128)(2,1)} %copy-done.12, bf16[4,256,256]{2,1,0:T(8,128)(2,1)} %copy-done.13, bf16[4,256,256]{2,1,0:T(8,128)(2,1)} %copy-done.11, ...), custom_call_target="tpu_custom_call" | custom-call | flops 5000000000 | bytes 5000000 | tf_op jit(solution)/shard_map/statistics/pallas_call | solution.py:601
  146.1 1.9 collective-permute-start.11
  148.0 2.4 collective-permute-start.13
  150.4 23.2 %memory_backward.1 = (f32[4,8,256,128]{3,2,1,0:T(8,128)}, f32[4,8,256,128]{3,2,1,0:T(8,128)}) custom-call(s32[8]{0:T(128)} %reduce_sum.39.counts, s32[128]{0:T(128)} %reshape.298.places, s32[128]{0:T(128)} %add.136.homes, bf16[4096,256]{1,0:T(8,128)(2,1)} %k_own.3, bf16[4096,256]{1,0:T(8,128)(2,1)} %collective-permute-done.6.k_par, bf16[4096,256]{1,0:T(8,128)(2,1)} %v_own.3, ...), custom_call_target="tpu_custom_call" | custom-call | flops 30000001024 | bytes 30000000 | tf_op jit(solution)/shard_map/memory_backward/pallas_call | solution.py:629
  173.7 6.6 %collective-permute-start.16 = (bf16[8,256,128]{2,1,0:T(8,128)(2,1)S(1)}, bf16[8,256,128]{2,1,0:T(8,128)(2,1)S(1)}, u32[]{:S(2)}, u32[]{:S(2)}) collective-permute-start(bf16[8,256,128]{2,1,0:T(8,128)(2,1)S(1)} %copy-done.8), channel_id=1, source_target_pairs={{0,8},{4,12},{8,16},{12,20},{16,24},{20,28},{24,0},{28,4},{1,9},{5... | collective-permute-start | bytes 1572872 | tf_op jit(solution)/shard_map/ppermute | solution.py:496
  180.3 15.3 %collective-permute-done.12.rest_2_.rest_6_ = f32[4,8,2,512]{3,2,1,0:T(2,128)S(1)} collective-permute-done((f32[4,8,2,512]{3,2,1,0:T(2,128)}, f32[4,8,2,512]{3,2,1,0:T(2,128)S(1)}, u32[]{:S(2)}, u32[]{:S(2)}) %collective-permute-start.12) | collective-permute-done | bytes 131104 | tf_op jit(solution)/shard_map/ppermute | solution.py:496
  196.3 5.0 %combine.1 = (bf16[8,256,128]{2,1,0:T(8,128)(2,1)}, bf16[8,256,128]{2,1,0:T(8,128)(2,1)}, bf16[8,256,128]{2,1,0:T(8,128)(2,1)}, bf16[8,256,128]{2,1,0:T(8,128)(2,1)}) custom-call(f32[4,8,2,512]{3,2,1,0:T(2,128)} %statistics.1.rest_8_.rest_0_.rest_4_, f32[4,8,2,512]{3,2,1,0:T(2,128)} %copy-done.15, f32[4,8,2,512]{3,2,1,0:T(2,128)} %copy-done.16, ...), custom_call_target="tpu_custom_call" | custom-call | flops 5000000000 | bytes 5000000 | tf_op jit(solution)/shard_map/combine/pallas_call | solution.py:650
  201.3 3.5 %all-to-all-start.5 = ((bf16[4,256,256]{2,1,0:T(8,128)(2,1)}), bf16[4,256,256]{2,1,0:T(8,128)(2,1)S(1)}, u32[]{:S(2)}, u32[]{:S(2)}) async-start(bf16[4,256,256]{2,1,0:T(8,128)(2,1)} %bitcast.14), calls=%async_computation.5 | async-start | bytes 1048576 | tf_op jit(solution)/shard_map/all_to_all | solution.py:499
  206.4 2.6 collective-permute-start.18
  208.9 3.0 %attention.1 = (bf16[1024,256]{1,0:T(8,128)(2,1)}, bf16[256,1024]{1,0:T(8,128)(2,1)}) custom-call(f32[4]{0:T(128)} %add_divide_fusion.gate, f32[8,256,128]{2,1,0:T(8,128)} %get-tuple-element.58.local_ref, bf16[8,256,128]{2,1,0:T(8,128)(2,1)} %get-tuple-element.73.rest_0_, bf16[8,256,128]{2,1,0:T(8,128)(2,1)} %copy-done.6, bf16[8,256,128]{2,1,0:T(8,128)(2,1)} %copy-done.7, ...), custom_call_target="tpu_custom_call" | custom-call | flops 3000000000 | bytes 3000000 | tf_op jit(solution)/shard_map/attention/pallas_call | solution.py:683
  212.0 1.6 all-to-all-done.5
  213.6 3.5 %all-to-all-start.3 = ((bf16[4,256,256]{2,1,0:T(8,128)(2,1)}), bf16[4,256,256]{2,1,0:T(8,128)(2,1)S(1)}, u32[]{:S(2)}, u32[]{:S(2)}) async-start(bf16[4,256,256]{2,1,0:T(8,128)(2,1)} %bitcast.63), calls=%async_computation.3 | async-start | bytes 1048576 | tf_op jit(solution)/shard_map/all_to_all | solution.py:499
  217.1 5.8 %weight_grad.1 = (bf16[4,256,256]{2,1,0:T(8,128)(2,1)}, bf16[4,256,256]{2,1,0:T(8,128)(2,1)}) custom-call(s32[4]{0:T(128)} %iota_xor_fusion.order, s32[5]{0:T(128)} %pad_add_fusion.dests, bf16[256,1024]{1,0:T(8,128)(2,1)} %get-tuple-element.90.attention_ref, bf16[256,2048]{1,0:T(8,128)(2,1)} %rest_0_.1, bf16[256,2048]{1,0:T(8,128)(2,1)} %copy-done.1, ...), custom_call_target="tpu_custom_call" | custom-call | flops 5000000000 | bytes 5000000 | tf_op jit(solution)/shard_map/weight_grad/pallas_call | solution.py:698
  222.9 2.5 collective-permute-start.20
  225.9 3.5 %all-to-all-start.6 = ((bf16[4,256,256]{2,1,0:T(8,128)(2,1)}), bf16[4,256,256]{2,1,0:T(8,128)(2,1)S(1)}, u32[]{:S(2)}, u32[]{:S(2)}) async-start(bf16[4,256,256]{2,1,0:T(8,128)(2,1)} %bitcast.16), calls=%async_computation.6 | async-start | bytes 1048576 | tf_op jit(solution)/shard_map/all_to_all | solution.py:499
  229.4 4.4 %fusion = bf16[256,2048]{1,0:T(8,128)(2,1)} fusion(bf16[4,256,256]{2,1,0:T(8,128)(2,1)S(1)} %all-to-all-done.3, bf16[4,256,2048]{2,1,0:T(8,128)(2,1)} %bitcast.67), kind=kOutput, calls=%fused_computation.2 | convolution fusion | flops 1074266112 | bytes 5767168 | tf_op jit(solution)/shard_map/stc,scd->td/dot_general | solution.py:719
  233.8 21.3 %collective-permute-done.18.rest_2_ = bf16[8,256,128]{2,1,0:T(8,128)(2,1)S(1)} collective-permute-done((bf16[8,256,128]{2,1,0:T(8,128)(2,1)}, bf16[8,256,128]{2,1,0:T(8,128)(2,1)S(1)}, u32[]{:S(2)}, u32[]{:S(2)}) %collective-permute-start.18) | collective-permute-done | bytes 524320 | tf_op jit(solution)/shard_map/ppermute | solution.py:496
  255.9 2.8 query_grad.1
  258.7 3.5 %all-to-all-start.4 = ((bf16[4,256,256]{2,1,0:T(8,128)(2,1)}), bf16[4,256,256]{2,1,0:T(8,128)(2,1)S(1)}, u32[]{:S(2)}, u32[]{:S(2)}) async-start(bf16[4,256,256]{2,1,0:T(8,128)(2,1)} %bitcast.60), calls=%async_computation.4 | async-start | bytes 1048576 | tf_op jit(solution)/shard_map/all_to_all | solution.py:499
  262.5 1.9 collective-permute-start.23
  264.4 0.9 copy.45
  265.3 0.9 copy.46
  266.2 3.3 %collective-permute-done.21 = bf16[256,256]{1,0:T(8,128)(2,1)S(1)} collective-permute-done((bf16[256,256]{1,0:T(8,128)(2,1)S(1)}, bf16[256,256]{1,0:T(8,128)(2,1)S(1)}, u32[]{:S(2)}, u32[]{:S(2)}) %collective-permute-start.21) | collective-permute-done | bytes 131104 | tf_op jit(solution)/shard_map/ppermute | solution.py:496
  269.4 5.5 %collective-permute-done.22 = bf16[256,256]{1,0:T(8,128)(2,1)S(1)} collective-permute-done((bf16[256,256]{1,0:T(8,128)(2,1)S(1)}, bf16[256,256]{1,0:T(8,128)(2,1)S(1)}, u32[]{:S(2)}, u32[]{:S(2)}) %collective-permute-start.22) | collective-permute-done | bytes 131104 | tf_op jit(solution)/shard_map/ppermute | solution.py:496
  275.7 0.9 copy.44
  (97 shorter events, 13.6 us)
Async XLA Ops:
  7.2 56.8 %copy-start.3 = (bf16[256,1024]{1,0:T(8,128)(2,1)S(1)}, bf16[256,1024]{1,0:T(8,128)(2,1)}, u32[]{:S(2)}) copy-start(bf16[256,1024]{1,0:T(8,128)(2,1)} %param.10) | copy-start | bytes 1572868
  7.2 63.9 %copy-start.18 = (f32[16]{0:T(128)S(1)}, f32[16]{0:T(128)}, u32[]{:S(2)}) copy-start(f32[16]{0:T(128)} %param.15) | copy-start | bytes 196
  21.4 61.3 %copy-start.4 = (bf16[4,256,256]{2,1,0:T(8,128)(2,1)}, bf16[4,256,256]{2,1,0:T(8,128)(2,1)S(1)}, u32[]{:S(2)}) copy-start(bf16[4,256,256]{2,1,0:T(8,128)(2,1)S(1)} %all_to_all.35.q_ref.rest_0_) | copy-start | bytes 1572868
  21.4 24.7 %collective-permute-start.4 = (bf16[256,2048]{1,0:T(8,128)(2,1)}, bf16[256,2048]{1,0:T(8,128)(2,1)S(1)}, u32[]{:S(2)}, u32[]{:S(2)}) collective-permute-start(bf16[256,2048]{1,0:T(8,128)(2,1)} %rest_0_.1), channel_id=1, source_target_pairs={{0,2},{1,3},{2,0},{3,1},{4,6},{5,7},{6,4},{7,5},{8,10},{9,11},{10,... | collective-permute-start | bytes 3145736 | tf_op jit(solution)/shard_map/ppermute | solution.py:446
  21.8 78.6 %collective-permute-start.6 = (bf16[4096,256]{1,0:T(8,128)(2,1)}, bf16[4096,256]{1,0:T(8,128)(2,1)}, u32[]{:S(2)}, u32[]{:S(2)}) collective-permute-start(bf16[4096,256]{1,0:T(8,128)(2,1)} %k_own.3), channel_id=1, source_target_pairs={{0,4},{4,0},{8,12},{12,8},{16,20},{20,16},{24,28},{28,24},{1,5},{5... | collective-permute-start | bytes 6291464 | tf_op jit(solution)/shard_map/ppermute | solution.py:505
  23.3 90.9 %collective-permute-start.7 = (bf16[4096,256]{1,0:T(8,128)(2,1)}, bf16[4096,256]{1,0:T(8,128)(2,1)}, u32[]{:S(2)}, u32[]{:S(2)}) collective-permute-start(bf16[4096,256]{1,0:T(8,128)(2,1)} %v_own.3), channel_id=1, source_target_pairs={{0,4},{4,0},{8,12},{12,8},{16,20},{20,16},{24,28},{28,24},{1,5},{5... | collective-permute-start | bytes 6291464 | tf_op jit(solution)/shard_map/ppermute | solution.py:506
  24.9 16.9 %collective-permute-start = (bf16[4,256,256]{2,1,0:T(8,128)(2,1)S(1)}, bf16[4,256,256]{2,1,0:T(8,128)(2,1)}, u32[]{:S(2)}, u32[]{:S(2)}) collective-permute-start(bf16[4,256,256]{2,1,0:T(8,128)(2,1)S(1)} %all_to_all.35.q_ref.rest_0_), channel_id=1, source_target_pairs={{0,8},{4,12},{8,16},{12,20},{16,24},{20,28},{24,0},{28,4},{1,9},{5... | collective-permute-start | bytes 1572872 | tf_op jit(solution)/shard_map/ppermute | solution.py:496
  27.2 35.1 %collective-permute-start.1 = (bf16[4,256,256]{2,1,0:T(8,128)(2,1)S(1)}, bf16[4,256,256]{2,1,0:T(8,128)(2,1)}, u32[]{:S(2)}, u32[]{:S(2)}) collective-permute-start(bf16[4,256,256]{2,1,0:T(8,128)(2,1)S(1)} %all_to_all.35.q_ref.rest_0_), channel_id=1, source_target_pairs={{0,16},{4,20},{8,24},{12,28},{16,0},{20,4},{24,8},{28,12},{1,17},{... | collective-permute-start | bytes 1572872 | tf_op jit(solution)/shard_map/ppermute | solution.py:496
  41.8 35.3 %collective-permute-start.3 = (bf16[256,2048]{1,0:T(8,128)(2,1)}, bf16[256,2048]{1,0:T(8,128)(2,1)S(1)}, u32[]{:S(2)}, u32[]{:S(2)}) collective-permute-start(bf16[256,2048]{1,0:T(8,128)(2,1)} %rest_0_.1), channel_id=1, source_target_pairs={{0,1},{1,0},{2,3},{3,2},{4,5},{5,4},{6,7},{7,6},{8,9},{9,8},{10,11... | collective-permute-start | bytes 3145736 | tf_op jit(solution)/shard_map/ppermute | solution.py:447
  46.2 31.0 %copy-start = (bf16[256,2048]{1,0:T(8,128)(2,1)}, bf16[256,2048]{1,0:T(8,128)(2,1)S(1)}, u32[]{:S(2)}) copy-start(bf16[256,2048]{1,0:T(8,128)(2,1)S(1)} %collective-permute-done.4.rest_2_) | copy-start | bytes 3145732
  46.2 30.9 %collective-permute-start.5 = (bf16[256,2048]{1,0:T(8,128)(2,1)S(1)}, bf16[256,2048]{1,0:T(8,128)(2,1)}, u32[]{:S(2)}, u32[]{:S(2)}) collective-permute-start(bf16[256,2048]{1,0:T(8,128)(2,1)S(1)} %collective-permute-done.4.rest_2_), channel_id=1, source_target_pairs={{0,1},{1,0},{2,3},{3,2},{4,5},{5,4},{6,7},{7,6},{8,9},{9,8},{10,11... | collective-permute-start | bytes 3145736 | tf_op jit(solution)/shard_map/ppermute | solution.py:448
  48.4 16.4 %all-to-all-start.2 = ((bf16[4,256,256]{2,1,0:T(8,128)(2,1)}), bf16[4,256,256]{2,1,0:T(8,128)(2,1)}, u32[]{:S(2)}, u32[]{:S(2)}) async-start(bf16[4,256,256]{2,1,0:T(8,128)(2,1)} %bitcast.50), calls=%async_computation.2 | async-start | bytes 1048576 | tf_op jit(solution)/shard_map/all_to_all | solution.py:499
  62.3 14.8 %collective-permute-start.2 = (bf16[4,256,256]{2,1,0:T(8,128)(2,1)S(1)}, bf16[4,256,256]{2,1,0:T(8,128)(2,1)}, u32[]{:S(2)}, u32[]{:S(2)}) collective-permute-start(bf16[4,256,256]{2,1,0:T(8,128)(2,1)S(1)} %all_to_all.35.q_ref.rest_0_), channel_id=1, source_target_pairs={{0,24},{4,28},{8,0},{12,4},{16,8},{20,12},{24,16},{28,20},{1,25},{... | collective-permute-start | bytes 1572872 | tf_op jit(solution)/shard_map/ppermute | solution.py:496
  64.8 12.3 %all-to-all-start.1 = ((bf16[4,256,256]{2,1,0:T(8,128)(2,1)}), bf16[4,256,256]{2,1,0:T(8,128)(2,1)S(1)}, u32[]{:S(2)}, u32[]{:S(2)}) async-start(bf16[4,256,256]{2,1,0:T(8,128)(2,1)} %bitcast.52), calls=%async_computation.1 | async-start | bytes 1048576 | tf_op jit(solution)/shard_map/all_to_all | solution.py:499
  68.3 161.1 %all-gather.2.cloned.1.call-start = ((), (), s32[]{:S(2)}) async-start(), calls=%async_computation.7 | async-start | bytes 5242880 | tf_op jit(solution)/shard_map/all_gather | solution.py:531
  77.1 12.8 %copy-start.5 = (bf16[4,256,256]{2,1,0:T(8,128)(2,1)}, bf16[4,256,256]{2,1,0:T(8,128)(2,1)S(1)}, u32[]{:S(2)}) copy-start(bf16[4,256,256]{2,1,0:T(8,128)(2,1)S(1)} %all-to-all-done.1) | copy-start | bytes 1572868
  77.1 1.0 copy-start.1
  82.8 58.3 %collective-permute-start.10 = (bf16[4,256,256]{2,1,0:T(8,128)(2,1)}, bf16[4,256,256]{2,1,0:T(8,128)(2,1)S(1)}, u32[]{:S(2)}, u32[]{:S(2)}) collective-permute-start(bf16[4,256,256]{2,1,0:T(8,128)(2,1)} %attention_grad.1.rest_0_.rest_4_), channel_id=1, source_target_pairs={{0,24},{4,28},{8,0},{12,4},{16,8},{20,12},{24,16},{28,20},{1,25},{... | collective-permute-start | bytes 1572872 | tf_op jit(solution)/shard_map/ppermute | solution.py:496
  83.9 57.2 %collective-permute-start.8 = (bf16[4,256,256]{2,1,0:T(8,128)(2,1)}, bf16[4,256,256]{2,1,0:T(8,128)(2,1)S(1)}, u32[]{:S(2)}, u32[]{:S(2)}) collective-permute-start(bf16[4,256,256]{2,1,0:T(8,128)(2,1)} %attention_grad.1.rest_0_.rest_4_), channel_id=1, source_target_pairs={{0,8},{4,12},{8,16},{12,20},{16,24},{20,28},{24,0},{28,4},{1,9},{5... | collective-permute-start | bytes 1572872 | tf_op jit(solution)/shard_map/ppermute | solution.py:496
  85.7 55.4 %collective-permute-start.9 = (bf16[4,256,256]{2,1,0:T(8,128)(2,1)}, bf16[4,256,256]{2,1,0:T(8,128)(2,1)S(1)}, u32[]{:S(2)}, u32[]{:S(2)}) collective-permute-start(bf16[4,256,256]{2,1,0:T(8,128)(2,1)} %attention_grad.1.rest_0_.rest_4_), channel_id=1, source_target_pairs={{0,16},{4,20},{8,24},{12,28},{16,0},{20,4},{24,8},{28,12},{1,17},{... | collective-permute-start | bytes 1572872 | tf_op jit(solution)/shard_map/ppermute | solution.py:496
  131.8 73.7 %collective-permute-start.14 = (bf16[8,256,128]{2,1,0:T(8,128)(2,1)}, bf16[8,256,128]{2,1,0:T(8,128)(2,1)S(1)}, u32[]{:S(2)}, u32[]{:S(2)}) collective-permute-start(bf16[8,256,128]{2,1,0:T(8,128)(2,1)} %get-tuple-element.70), channel_id=1, source_target_pairs={{0,24},{4,28},{8,0},{12,4},{16,8},{20,12},{24,16},{28,20},{1,25},{... | collective-permute-start | bytes 1572872 | tf_op jit(solution)/shard_map/ppermute | solution.py:496
  137.4 68.0 %collective-permute-start.15 = (bf16[8,256,128]{2,1,0:T(8,128)(2,1)}, bf16[8,256,128]{2,1,0:T(8,128)(2,1)S(1)}, u32[]{:S(2)}, u32[]{:S(2)}) collective-permute-start(bf16[8,256,128]{2,1,0:T(8,128)(2,1)} %get-tuple-element.71), channel_id=1, source_target_pairs={{0,16},{4,20},{8,24},{12,28},{16,0},{20,4},{24,8},{28,12},{1,17},{... | collective-permute-start | bytes 1572872 | tf_op jit(solution)/shard_map/ppermute | solution.py:496
  141.1 0.8 copy-start.11
  141.1 1.0 copy-start.12
  141.1 1.1 copy-start.13
  146.1 27.6 %copy-start.8 = (bf16[8,256,128]{2,1,0:T(8,128)(2,1)S(1)}, bf16[8,256,128]{2,1,0:T(8,128)(2,1)}, u32[]{:S(2)}) copy-start(bf16[8,256,128]{2,1,0:T(8,128)(2,1)} %get-tuple-element.72) | copy-start | bytes 1572868
  146.1 27.6 %collective-permute-start.11 = (f32[4,8,2,512]{3,2,1,0:T(2,128)}, f32[4,8,2,512]{3,2,1,0:T(2,128)S(1)}, u32[]{:S(2)}, u32[]{:S(2)}) collective-permute-start(f32[4,8,2,512]{3,2,1,0:T(2,128)} %statistics.1.rest_8_.rest_0_.rest_4_), channel_id=1, source_target_pairs={{0,8},{4,12},{8,16},{12,20},{16,24},{20,28},{24,0},{28,4},{1,9},{5... | collective-permute-start | bytes 393224 | tf_op jit(solution)/shard_map/ppermute | solution.py:496
  148.0 47.6 %collective-permute-start.12 = (f32[4,8,2,512]{3,2,1,0:T(2,128)}, f32[4,8,2,512]{3,2,1,0:T(2,128)S(1)}, u32[]{:S(2)}, u32[]{:S(2)}) collective-permute-start(f32[4,8,2,512]{3,2,1,0:T(2,128)} %statistics.1.rest_8_.rest_0_.rest_4_), channel_id=1, source_target_pairs={{0,16},{4,20},{8,24},{12,28},{16,0},{20,4},{24,8},{28,12},{1,17},{... | collective-permute-start | bytes 393224 | tf_op jit(solution)/shard_map/ppermute | solution.py:496
  148.0 47.6 %collective-permute-start.13 = (f32[4,8,2,512]{3,2,1,0:T(2,128)}, f32[4,8,2,512]{3,2,1,0:T(2,128)S(1)}, u32[]{:S(2)}, u32[]{:S(2)}) collective-permute-start(f32[4,8,2,512]{3,2,1,0:T(2,128)} %statistics.1.rest_8_.rest_0_.rest_4_), channel_id=1, source_target_pairs={{0,24},{4,28},{8,0},{12,4},{16,8},{20,12},{24,16},{28,20},{1,25},{... | collective-permute-start | bytes 393224 | tf_op jit(solution)/shard_map/ppermute | solution.py:496
  173.7 21.9 %copy-start.15 = (f32[4,8,2,512]{3,2,1,0:T(2,128)}, f32[4,8,2,512]{3,2,1,0:T(2,128)S(1)}, u32[]{:S(2)}) copy-start(f32[4,8,2,512]{3,2,1,0:T(2,128)S(1)} %collective-permute-done.11.rest_1_.rest_7_) | copy-start | bytes 393220
  173.7 31.8 %collective-permute-start.16 = (bf16[8,256,128]{2,1,0:T(8,128)(2,1)S(1)}, bf16[8,256,128]{2,1,0:T(8,128)(2,1)S(1)}, u32[]{:S(2)}, u32[]{:S(2)}) collective-permute-start(bf16[8,256,128]{2,1,0:T(8,128)(2,1)S(1)} %copy-done.8), channel_id=1, source_target_pairs={{0,8},{4,12},{8,16},{12,20},{16,24},{20,28},{24,0},{28,4},{1,9},{5... | collective-permute-start | bytes 1572872 | tf_op jit(solution)/shard_map/ppermute | solution.py:496
  201.3 12.3 %all-to-all-start.5 = ((bf16[4,256,256]{2,1,0:T(8,128)(2,1)}), bf16[4,256,256]{2,1,0:T(8,128)(2,1)S(1)}, u32[]{:S(2)}, u32[]{:S(2)}) async-start(bf16[4,256,256]{2,1,0:T(8,128)(2,1)} %bitcast.14), calls=%async_computation.5 | async-start | bytes 1048576 | tf_op jit(solution)/shard_map/all_to_all | solution.py:499
  205.5 3.5 %copy-start.6 = (bf16[8,256,128]{2,1,0:T(8,128)(2,1)}, bf16[8,256,128]{2,1,0:T(8,128)(2,1)S(1)}, u32[]{:S(2)}) copy-start(bf16[8,256,128]{2,1,0:T(8,128)(2,1)S(1)} %collective-permute-done.14.rest_1_) | copy-start | bytes 1572868
  205.5 3.5 %copy-start.7 = (bf16[8,256,128]{2,1,0:T(8,128)(2,1)}, bf16[8,256,128]{2,1,0:T(8,128)(2,1)S(1)}, u32[]{:S(2)}) copy-start(bf16[8,256,128]{2,1,0:T(8,128)(2,1)S(1)} %collective-permute-done.15.rest_2_) | copy-start | bytes 1572868
  205.5 0.9 copy-start.14
  205.5 28.3 %collective-permute-start.17 = (bf16[8,256,128]{2,1,0:T(8,128)(2,1)}, bf16[8,256,128]{2,1,0:T(8,128)(2,1)S(1)}, u32[]{:S(2)}, u32[]{:S(2)}) collective-permute-start(bf16[8,256,128]{2,1,0:T(8,128)(2,1)} %get-tuple-element.80), channel_id=1, source_target_pairs={{0,24},{4,28},{8,0},{12,4},{16,8},{20,12},{24,16},{28,20},{1,25},{... | collective-permute-start | bytes 1572872 | tf_op jit(solution)/shard_map/ppermute | solution.py:496
  206.4 48.8 %collective-permute-start.18 = (bf16[8,256,128]{2,1,0:T(8,128)(2,1)}, bf16[8,256,128]{2,1,0:T(8,128)(2,1)S(1)}, u32[]{:S(2)}, u32[]{:S(2)}) collective-permute-start(bf16[8,256,128]{2,1,0:T(8,128)(2,1)} %get-tuple-element.81), channel_id=1, source_target_pairs={{0,16},{4,20},{8,24},{12,28},{16,0},{20,4},{24,8},{28,12},{1,17},{... | collective-permute-start | bytes 1572872 | tf_op jit(solution)/shard_map/ppermute | solution.py:496
  208.9 46.2 %collective-permute-start.19 = (bf16[8,256,128]{2,1,0:T(8,128)(2,1)}, bf16[8,256,128]{2,1,0:T(8,128)(2,1)}, u32[]{:S(2)}, u32[]{:S(2)}) collective-permute-start(bf16[8,256,128]{2,1,0:T(8,128)(2,1)} %get-tuple-element.82), channel_id=1, source_target_pairs={{0,8},{4,12},{8,16},{12,20},{16,24},{20,28},{24,0},{28,4},{1,9},{5... | collective-permute-start | bytes 1572872 | tf_op jit(solution)/shard_map/ppermute | solution.py:496
  213.6 12.3 %all-to-all-start.3 = ((bf16[4,256,256]{2,1,0:T(8,128)(2,1)}), bf16[4,256,256]{2,1,0:T(8,128)(2,1)S(1)}, u32[]{:S(2)}, u32[]{:S(2)}) async-start(bf16[4,256,256]{2,1,0:T(8,128)(2,1)} %bitcast.63), calls=%async_computation.3 | async-start | bytes 1048576 | tf_op jit(solution)/shard_map/all_to_all | solution.py:499
  222.9 39.3 %collective-permute-start.20 = (bf16[4,256,256]{2,1,0:T(8,128)(2,1)}, bf16[4,256,256]{2,1,0:T(8,128)(2,1)S(1)}, u32[]{:S(2)}, u32[]{:S(2)}) collective-permute-start(bf16[4,256,256]{2,1,0:T(8,128)(2,1)} %get-tuple-element.92), channel_id=1, source_target_pairs={{0,4},{4,0},{8,12},{12,8},{16,20},{20,16},{24,28},{28,24},{1,5},{5... | collective-permute-start | bytes 1572872 | tf_op jit(solution)/shard_map/ppermute | solution.py:712
  225.9 32.8 %all-to-all-start.6 = ((bf16[4,256,256]{2,1,0:T(8,128)(2,1)}), bf16[4,256,256]{2,1,0:T(8,128)(2,1)S(1)}, u32[]{:S(2)}, u32[]{:S(2)}) async-start(bf16[4,256,256]{2,1,0:T(8,128)(2,1)} %bitcast.16), calls=%async_computation.6 | async-start | bytes 1048576 | tf_op jit(solution)/shard_map/all_to_all | solution.py:499
  233.8 22.1 %copy-start.9 = (bf16[8,256,128]{2,1,0:T(8,128)(2,1)}, bf16[8,256,128]{2,1,0:T(8,128)(2,1)S(1)}, u32[]{:S(2)}) copy-start(bf16[8,256,128]{2,1,0:T(8,128)(2,1)S(1)} %collective-permute-done.17.rest_1_) | copy-start | bytes 1572868
  255.1 0.8 copy-start.10
  255.9 6.3 %copy-start.2 = (bf16[4,256,256]{2,1,0:T(8,128)(2,1)S(1)}, bf16[4,256,256]{2,1,0:T(8,128)(2,1)}, u32[]{:S(2)}) copy-start(bf16[4,256,256]{2,1,0:T(8,128)(2,1)} %get-tuple-element.91) | copy-start | bytes 1572868
  258.7 17.0 %all-to-all-start.4 = ((bf16[4,256,256]{2,1,0:T(8,128)(2,1)}), bf16[4,256,256]{2,1,0:T(8,128)(2,1)S(1)}, u32[]{:S(2)}, u32[]{:S(2)}) async-start(bf16[4,256,256]{2,1,0:T(8,128)(2,1)} %bitcast.60), calls=%async_computation.4 | async-start | bytes 1048576 | tf_op jit(solution)/shard_map/all_to_all | solution.py:499
  262.4 7.1 %collective-permute-start.21 = (bf16[256,256]{1,0:T(8,128)(2,1)S(1)}, bf16[256,256]{1,0:T(8,128)(2,1)S(1)}, u32[]{:S(2)}, u32[]{:S(2)}) collective-permute-start(bf16[256,256]{1,0:T(8,128)(2,1)S(1)} %get-tuple-element.94), channel_id=1, source_target_pairs={{0,24},{4,28},{8,0},{12,4},{16,8},{20,12},{24,16},{28,20},{1,25},{... | collective-permute-start | bytes 393224 | tf_op jit(solution)/shard_map/ppermute | solution.py:496
  262.4 12.5 %collective-permute-start.22 = (bf16[256,256]{1,0:T(8,128)(2,1)S(1)}, bf16[256,256]{1,0:T(8,128)(2,1)S(1)}, u32[]{:S(2)}, u32[]{:S(2)}) collective-permute-start(bf16[256,256]{1,0:T(8,128)(2,1)S(1)} %get-tuple-element.95), channel_id=1, source_target_pairs={{0,16},{4,20},{8,24},{12,28},{16,0},{20,4},{24,8},{28,12},{1,17},{... | collective-permute-start | bytes 393224 | tf_op jit(solution)/shard_map/ppermute | solution.py:496
  262.5 12.4 %collective-permute-start.23 = (bf16[256,256]{1,0:T(8,128)(2,1)S(1)}, bf16[256,256]{1,0:T(8,128)(2,1)S(1)}, u32[]{:S(2)}, u32[]{:S(2)}) collective-permute-start(bf16[256,256]{1,0:T(8,128)(2,1)S(1)} %get-tuple-element.96), channel_id=1, source_target_pairs={{0,8},{4,12},{8,16},{12,20},{16,24},{20,28},{24,0},{28,4},{1,9},{5... | collective-permute-start | bytes 393224 | tf_op jit(solution)/shard_map/ppermute | solution.py:496
  (2 other events, 1.4 us)
Sparse Core Ops, SparseCore 0:
  71.9 37.1 all-gather.1

commit v3 on v2

--- a/solution.py
+++ b/solution.py
@@ -51,6 +51,17 @@
     return rows
 
 
+def own_columns(total):
+    return jnp.concatenate([total[:DH, :QBLK], total[DH:, QBLK:]], axis=1)
+
+
+def stacked(parts):
+    rows = []
+    for part in parts:
+        rows += [part[:, :QBLK], part[:, QBLK:]]
+    return jnp.concatenate(rows, axis=0)
+
+
 def at_slot(slot, last, column=0):
     def index(s, b, *_):
         return (jnp.where(s == slot, b, jnp.where(s > slot, last, 0)), column, 0)
@@ -149,7 +160,7 @@
                 found.append((b, t, folded(p, jnp.sum), o))
         for b, t, norm, o in found:
             norms[b, t] += norm
-            acc[b, t] += o
+            acc[b, t] += own_columns(o)
         return carry
 
     lax.fori_loop(0, turns, second, 0)
@@ -163,7 +174,7 @@
             safe = jnp.where(some, norm, 1.0)
             lse_ref[0, b, :, wide] = jnp.where(some, tops[b, t, 0:1, :] + jnp.log(safe), LOW)
             parts.append(acc[b, t] * (1.0 / safe))
-        results.append(jnp.concatenate(own_blocks(parts), axis=0))
+        results.append(stacked(parts))
         exact_ref[0, b] = results[b]
     for i in range(group):
 
@@ -236,7 +247,7 @@
                 weights[j, t] = p
                 found.append((b, t, dot(keys, p.astype(BF), TN)))
         for b, t, sums in found:
-            acc_keys[b, t] += sums
+            acc_keys[b, t] += own_columns(sums)
         return carry
 
     lax.fori_loop(0, turns, first, 0)
@@ -254,14 +265,13 @@
                 delta = weights[j, t] * (slope - means[b, t])
                 found.append((b, t, dot(kbuf[pl.ds(row, MBLK), cols], delta.astype(BF), TN)))
         for b, t, sums in found:
-            acc[b, t] += sums
+            acc[b, t] += own_columns(sums)
         return carry
 
     lax.fori_loop(0, turns, second, 0)
     for b in range(blocks):
         for out_ref, total in ((delta_ref, acc), (key_ref, acc_keys)):
-            parts = own_blocks([total[b, t] for t in range(pairs)])
-            out_ref[0, b] = jnp.concatenate(parts, axis=0)
+            out_ref[0, b] = stacked([total[b, t] for t in range(pairs)])
 
 
 def combine_kernel(group, heads, *rest):
@@ -561,7 +571,7 @@
     scratch = [pltpu.VMEM((memory_rows, width), BF)] * 2
     scratch += [pltpu.VMEM((per_seg + 1, pairs, 128, 256), BF)] * 2
     scratch += [pltpu.VMEM((cap, pairs, MBLK, 256), F32)]
-    acc = pltpu.VMEM((per_seg + 1, pairs, 128, 256), F32)
+    acc = pltpu.VMEM((per_seg + 1, pairs, DH, 256), F32)
     rows8 = pltpu.VMEM((per_seg + 1, pairs, 8, 256), F32)
     rows1 = pltpu.VMEM((per_seg + 1, pairs, 1, 256), F32)
     sems = pltpu.SemaphoreType.DMA((4,))

time: 285 us -> 284 us (level)
  waiting for transfers between devices: 92.3 us -> 86.9 us
  Pallas kernels: 76.4 us -> 79.8 us
    ppermute x18, waiting for transfers between devices: 66.7 us -> 60.3 us  [shifted(): return lax.ppermute(x, 'mem', [(i, (i + 2 * k) % n) for i in range(n)])]
    ppermute x18, starting transfers between devices: 38 us -> 41.3 us  [shifted(): return lax.ppermute(x, 'mem', [(i, (i + 2 * k) % n) for i in range(n)])]
  transfers between devices with their start and end apart: 31 -> 31, of which waited for: 11 -> 11; matrix products, arithmetic and copies ran while one was open for 6% -> 6% of each run, Pallas kernels for 27% -> 28%
where the time goes in v3:
time: 284 us
  waiting for transfers between devices  86.9 us (31%)
  Pallas kernels  79.8 us (28%)
  starting transfers between devices  66.7 us (23%)
  between operations  14.4 us (5%)
  local copies, waits for them, and re-layouts  13.6 us (5%)
  blocking collectives  12.9 us (5%)
  other arithmetic  4.95 us (2%)
  matrix products  4.41 us (2%)
    ppermute x18, waiting for transfers between devices, shifted(): return lax.ppermute(x, 'mem', [(i, (i + 2 * k) % n) for i in range(n)])  60.3 us
    ppermute x18, starting transfers between devices, shifted(): return lax.ppermute(x, 'mem', [(i, (i + 2 * k) % n) for i in range(n)])  41.3 us
    pallas_call x1, Pallas kernels, per_device(): pl.pallas_call(functools.partial(memory_backward, group, pairs, i), grid_...  25.7 us
    all_to_all x6, starting transfers between devices, exchange(): return lax.all_to_all(x, 'fsdp', split_axis=0, concat_axis=0, tiled=True)  21.5 us
    pallas_call x1, Pallas kernels, per_device(): pl.pallas_call(functools.partial(memory_forward, group, pairs, i), grid_s...  18.4 us
    ppermute x1, waiting for transfers between devices, per_device(): par_values = [lax.ppermute(mem_values, 'mem', swap)]  13.8 us
    all_to_all x1, blocking collectives, exchange(): return lax.all_to_all(x, 'fsdp', split_axis=0, concat_axis=0, tiled=True)  12.9 us
    pallas_call x1, Pallas kernels, per_device(): pl.pallas_call(functools.partial(local_kernel, all_heads // 2, per_seg, H...  10.5 us
  transfers between devices with their start and end apart: 31, of which 11 were waited for; matrix products, arithmetic and copies ran while one was open for 6% of the time, Pallas kernels for 28%

profile of v3, /device:TPU:0, one launch (start us, length us, event | category | flops | bytes accessed | tf_op | source)
XLA Modules:
  0.0 283.6 jit_solution(14558644873772597715)
XLA Ops:
  7.2 1.1 multiply_bitcast_fusion
  8.5 12.9 %all_to_all.35.q_ref.rest_0_ = bf16[4,256,256]{2,1,0:T(8,128)(2,1)S(1)} all-to-all(bf16[4,256,256]{2,1,0:T(8,128)(2,1)S(1)} %bitcast.56), channel_id=1, replica_groups=mesh['mem'=8,'fsdp'=4] {'fsdp'}, dimensions={0} | all-to-all | bytes 1048576 | tf_op jit(solution)/shard_map/all_to_all | solution.py:509
  21.8 1.5 collective-permute-start.6
  24.9 1.6 collective-permute-start
  27.2 2.6 collective-permute-start.1
  30.0 11.9 %collective-permute-done.rest_1_ = bf16[4,256,256]{2,1,0:T(8,128)(2,1)} collective-permute-done((bf16[4,256,256]{2,1,0:T(8,128)(2,1)S(1)}, bf16[4,256,256]{2,1,0:T(8,128)(2,1)}, u32[]{:S(2)}, u32[]{:S(2)}) %collective-permute-start) | collective-permute-done | bytes 524320 | tf_op jit(solution)/shard_map/ppermute | solution.py:506
  41.9 4.3 %collective-permute-done.4.rest_2_ = bf16[256,2048]{1,0:T(8,128)(2,1)S(1)} collective-permute-done((bf16[256,2048]{1,0:T(8,128)(2,1)}, bf16[256,2048]{1,0:T(8,128)(2,1)S(1)}, u32[]{:S(2)}, u32[]{:S(2)}) %collective-permute-start.4) | collective-permute-done | bytes 1048608 | tf_op jit(solution)/shard_map/ppermute | solution.py:456
  46.4 2.0 copy.49
  48.4 4.1 %all-to-all-start.2 = ((bf16[4,256,256]{2,1,0:T(8,128)(2,1)}), bf16[4,256,256]{2,1,0:T(8,128)(2,1)}, u32[]{:S(2)}, u32[]{:S(2)}) async-start(bf16[4,256,256]{2,1,0:T(8,128)(2,1)} %bitcast.50), calls=%async_computation.2 | async-start | bytes 1048576 | tf_op jit(solution)/shard_map/all_to_all | solution.py:509
  52.9 9.4 %collective-permute-done.1.rest_2_ = bf16[4,256,256]{2,1,0:T(8,128)(2,1)} collective-permute-done((bf16[4,256,256]{2,1,0:T(8,128)(2,1)S(1)}, bf16[4,256,256]{2,1,0:T(8,128)(2,1)}, u32[]{:S(2)}, u32[]{:S(2)}) %collective-permute-start.1) | collective-permute-done | bytes 524320 | tf_op jit(solution)/shard_map/ppermute | solution.py:506
  62.3 1.6 collective-permute-start.2
  64.8 3.5 %all-to-all-start.1 = ((bf16[4,256,256]{2,1,0:T(8,128)(2,1)}), bf16[4,256,256]{2,1,0:T(8,128)(2,1)S(1)}, u32[]{:S(2)}, u32[]{:S(2)}) async-start(bf16[4,256,256]{2,1,0:T(8,128)(2,1)} %bitcast.52), calls=%async_computation.1 | async-start | bytes 1048576 | tf_op jit(solution)/shard_map/all_to_all | solution.py:509
  71.7 5.3 %all-to-all-done.1 = bf16[4,256,256]{2,1,0:T(8,128)(2,1)S(1)} async-done(((bf16[4,256,256]{2,1,0:T(8,128)(2,1)}), bf16[4,256,256]{2,1,0:T(8,128)(2,1)S(1)}, u32[]{:S(2)}, u32[]{:S(2)}) %all-to-all-start.1) | async-done | bytes 524320 | tf_op jit(solution)/shard_map/all_to_all | solution.py:509
  77.1 1.0 copy-done.1
  78.1 4.7 %attention_grad.1.rest_0_.rest_4_ = bf16[4,256,256]{2,1,0:T(8,128)(2,1)} custom-call(s32[4]{0:T(128)} %iota_xor_fusion.order, bf16[256,2048]{1,0:T(8,128)(2,1)} %weight_ref.1, bf16[256,2048]{1,0:T(8,128)(2,1)} %rest_0_.1, bf16[256,2048]{1,0:T(8,128)(2,1)} %copy-done.1, bf16[256,2048]{1,0:T(8,128)(2,1)} %copy-done, ...), custom_call_target="tpu_custom_call" | custom-call | flops 1000000000 | bytes 1000000 | tf_op jit(solution)/shard_map/attention_grad/pallas_call | solution.py:530
  82.8 1.2 collective-permute-start.10
  83.9 1.7 collective-permute-start.8
  85.7 4.2 %collective-permute-start.9 = (bf16[4,256,256]{2,1,0:T(8,128)(2,1)}, bf16[4,256,256]{2,1,0:T(8,128)(2,1)S(1)}, u32[]{:S(2)}, u32[]{:S(2)}) collective-permute-start(bf16[4,256,256]{2,1,0:T(8,128)(2,1)} %attention_grad.1.rest_0_.rest_4_), channel_id=1, source_target_pairs={{0,16},{4,20},{8,24},{12,28},{16,0},{20,4},{24,8},{28,12},{1,17},{... | collective-permute-start | bytes 1572872 | tf_op jit(solution)/shard_map/ppermute | solution.py:506
  89.9 10.5 %local.1 = (f32[8,256,128]{2,1,0:T(8,128)}, f32[8,256,128]{2,1,0:T(8,128)}, bf16[1024,256]{1,0:T(8,128)(2,1)}, bf16[1024,256]{1,0:T(8,128)(2,1)}) custom-call(f32[4]{0:T(128)} %add_divide_fusion.gate, bf16[4,256,256]{2,1,0:T(8,128)(2,1)} %copy-done.4, bf16[1024,256]{1,0:T(8,128)(2,1)} %bitcast.59, bf16[1024,256]{1,0:T(8,128)(2,1)} %bitcast.5.v_ref, ...), custom_call_target="tpu_custom_call" | custom-call | flops 1000000000 | bytes 1000000 | tf_op jit(solution)/shard_map/local/pallas_call | solution.py:549
  100.4 13.8 %collective-permute-done.7.v_par = bf16[4096,256]{1,0:T(8,128)(2,1)} collective-permute-done((bf16[4096,256]{1,0:T(8,128)(2,1)}, bf16[4096,256]{1,0:T(8,128)(2,1)}, u32[]{:S(2)}, u32[]{:S(2)}) %collective-permute-start.7) | collective-permute-done | bytes 2097184 | tf_op jit(solution)/shard_map/ppermute | solution.py:516
  114.2 18.4 %memory_forward.1 = (bf16[8,256,128]{2,1,0:T(8,128)(2,1)}, bf16[8,256,128]{2,1,0:T(8,128)(2,1)}, bf16[8,256,128]{2,1,0:T(8,128)(2,1)}, bf16[8,256,128]{2,1,0:T(8...) custom-call(s32[8]{0:T(128)} %reduce_sum.39.counts, s32[128]{0:T(128)} %reshape.298.places, ...), custom_call_target="tpu_custom_call" | custom-call | flops 30000001024 | bytes 30000000 | tf_op jit(solution)/shard_map/memory_forward/pallas_call | solution.py:588
  132.7 3.1 %collective-permute-start.14 = (bf16[8,256,128]{2,1,0:T(8,128)(2,1)}, bf16[8,256,128]{2,1,0:T(8,128)(2,1)S(1)}, u32[]{:S(2)}, u32[]{:S(2)}) collective-permute-start(bf16[8,256,128]{2,1,0:T(8,128)(2,1)} %get-tuple-element.70), channel_id=1, source_target_pairs={{0,24},{4,28},{8,0},{12,4},{16,8},{20,12},{24,16},{28,20},{1,25},{... | collective-permute-start | bytes 1572872 | tf_op jit(solution)/shard_map/ppermute | solution.py:506
  135.8 5.8 %collective-permute-start.15 = (bf16[8,256,128]{2,1,0:T(8,128)(2,1)}, bf16[8,256,128]{2,1,0:T(8,128)(2,1)S(1)}, u32[]{:S(2)}, u32[]{:S(2)}) collective-permute-start(bf16[8,256,128]{2,1,0:T(8,128)(2,1)} %get-tuple-element.71), channel_id=1, source_target_pairs={{0,16},{4,20},{8,24},{12,28},{16,0},{20,4},{24,8},{28,12},{1,17},{... | collective-permute-start | bytes 1572872 | tf_op jit(solution)/shard_map/ppermute | solution.py:506
  142.7 3.8 %statistics.1.rest_8_.rest_0_.rest_4_ = f32[4,8,2,512]{3,2,1,0:T(2,128)} custom-call(f32[4,8,1,512]{3,2,1,0:T(1,128)} %get-tuple-element.63.lse_ref, bf16[4,256,256]{2,1,0:T(8,128)(2,1)} %attention_grad.1.rest_0_.rest_4_, bf16[4,256,256]{2,1,0:T(8,128)(2,1)} %copy-done.12, bf16[4,256,256]{2,1,0:T(8,128)(2,1)} %copy-done.13, bf16[4,256,256]{2,1,0:T(8,128)(2,1)} %copy-done.11, ...), custom_call_target="tpu_custom_call" | custom-call | flops 5000000000 | bytes 5000000 | tf_op jit(solution)/shard_map/statistics/pallas_call | solution.py:611
  146.5 1.5 collective-permute-start.12
  148.0 2.3 collective-permute-start.13
  150.3 25.7 %memory_backward.1 = (f32[4,8,256,128]{3,2,1,0:T(8,128)}, f32[4,8,256,128]{3,2,1,0:T(8,128)}) custom-call(s32[8]{0:T(128)} %reduce_sum.39.counts, s32[128]{0:T(128)} %reshape.298.places, s32[128]{0:T(128)} %add.136.homes, bf16[4096,256]{1,0:T(8,128)(2,1)} %k_own.3, bf16[4096,256]{1,0:T(8,128)(2,1)} %collective-permute-done.6.k_par, bf16[4096,256]{1,0:T(8,128)(2,1)} %v_own.3, ...), custom_call_target="tpu_custom_call" | custom-call | flops 30000001024 | bytes 30000000 | tf_op jit(solution)/shard_map/memory_backward/pallas_call | solution.py:639
  176.1 10.9 %collective-permute-start.16 = (bf16[8,256,128]{2,1,0:T(8,128)(2,1)S(1)}, bf16[8,256,128]{2,1,0:T(8,128)(2,1)S(1)}, u32[]{:S(2)}, u32[]{:S(2)}) collective-permute-start(bf16[8,256,128]{2,1,0:T(8,128)(2,1)S(1)} %copy-done.8), channel_id=1, source_target_pairs={{0,8},{4,12},{8,16},{12,20},{16,24},{20,28},{24,0},{28,4},{1,9},{5... | collective-permute-start | bytes 1572872 | tf_op jit(solution)/shard_map/ppermute | solution.py:506
  186.9 8.9 %collective-permute-done.12.rest_2_.rest_6_ = f32[4,8,2,512]{3,2,1,0:T(2,128)S(1)} collective-permute-done((f32[4,8,2,512]{3,2,1,0:T(2,128)}, f32[4,8,2,512]{3,2,1,0:T(2,128)S(1)}, u32[]{:S(2)}, u32[]{:S(2)}) %collective-permute-start.12) | collective-permute-done | bytes 131104 | tf_op jit(solution)/shard_map/ppermute | solution.py:506
  196.6 5.0 %combine.1 = (bf16[8,256,128]{2,1,0:T(8,128)(2,1)}, bf16[8,256,128]{2,1,0:T(8,128)(2,1)}, bf16[8,256,128]{2,1,0:T(8,128)(2,1)}, bf16[8,256,128]{2,1,0:T(8,128)(2,1)}) custom-call(f32[4,8,2,512]{3,2,1,0:T(2,128)} %statistics.1.rest_8_.rest_0_.rest_4_, f32[4,8,2,512]{3,2,1,0:T(2,128)} %copy-done.15, f32[4,8,2,512]{3,2,1,0:T(2,128)} %copy-done.16, ...), custom_call_target="tpu_custom_call" | custom-call | flops 5000000000 | bytes 5000000 | tf_op jit(solution)/shard_map/combine/pallas_call | solution.py:660
  201.6 3.5 %all-to-all-start.5 = ((bf16[4,256,256]{2,1,0:T(8,128)(2,1)}), bf16[4,256,256]{2,1,0:T(8,128)(2,1)S(1)}, u32[]{:S(2)}, u32[]{:S(2)}) async-start(bf16[4,256,256]{2,1,0:T(8,128)(2,1)} %bitcast.14), calls=%async_computation.5 | async-start | bytes 1048576 | tf_op jit(solution)/shard_map/all_to_all | solution.py:509
  206.6 2.6 collective-permute-start.18
  209.2 3.0 %attention.1 = (bf16[1024,256]{1,0:T(8,128)(2,1)}, bf16[256,1024]{1,0:T(8,128)(2,1)}) custom-call(f32[4]{0:T(128)} %add_divide_fusion.gate, f32[8,256,128]{2,1,0:T(8,128)} %get-tuple-element.58.local_ref, bf16[8,256,128]{2,1,0:T(8,128)(2,1)} %get-tuple-element.73.rest_0_, bf16[8,256,128]{2,1,0:T(8,128)(2,1)} %copy-done.6, bf16[8,256,128]{2,1,0:T(8,128)(2,1)} %copy-done.7, ...), custom_call_target="tpu_custom_call" | custom-call | flops 3000000000 | bytes 3000000 | tf_op jit(solution)/shard_map/attention/pallas_call | solution.py:693
  212.2 1.6 all-to-all-done.5
  213.8 3.5 %all-to-all-start.3 = ((bf16[4,256,256]{2,1,0:T(8,128)(2,1)}), bf16[4,256,256]{2,1,0:T(8,128)(2,1)S(1)}, u32[]{:S(2)}, u32[]{:S(2)}) async-start(bf16[4,256,256]{2,1,0:T(8,128)(2,1)} %bitcast.63), calls=%async_computation.3 | async-start | bytes 1048576 | tf_op jit(solution)/shard_map/all_to_all | solution.py:509
  217.3 5.8 %weight_grad.1 = (bf16[4,256,256]{2,1,0:T(8,128)(2,1)}, bf16[4,256,256]{2,1,0:T(8,128)(2,1)}) custom-call(s32[4]{0:T(128)} %iota_xor_fusion.order, s32[5]{0:T(128)} %pad_add_fusion.dests, bf16[256,1024]{1,0:T(8,128)(2,1)} %get-tuple-element.90.attention_ref, bf16[256,2048]{1,0:T(8,128)(2,1)} %rest_0_.1, bf16[256,2048]{1,0:T(8,128)(2,1)} %copy-done.1, ...), custom_call_target="tpu_custom_call" | custom-call | flops 5000000000 | bytes 5000000 | tf_op jit(solution)/shard_map/weight_grad/pallas_call | solution.py:708
  223.1 1.5 collective-permute-start.20
  224.6 1.5 all-to-all-done.3
  226.1 3.5 %all-to-all-start.6 = ((bf16[4,256,256]{2,1,0:T(8,128)(2,1)}), bf16[4,256,256]{2,1,0:T(8,128)(2,1)S(1)}, u32[]{:S(2)}, u32[]{:S(2)}) async-start(bf16[4,256,256]{2,1,0:T(8,128)(2,1)} %bitcast.16), calls=%async_computation.6 | async-start | bytes 1048576 | tf_op jit(solution)/shard_map/all_to_all | solution.py:509
  229.6 4.4 %fusion = bf16[256,2048]{1,0:T(8,128)(2,1)} fusion(bf16[4,256,256]{2,1,0:T(8,128)(2,1)S(1)} %all-to-all-done.3, bf16[4,256,2048]{2,1,0:T(8,128)(2,1)} %bitcast.67), kind=kOutput, calls=%fused_computation.2 | convolution fusion | flops 1074266112 | bytes 5767168 | tf_op jit(solution)/shard_map/stc,scd->td/dot_general | solution.py:729
  234.1 21.3 %collective-permute-done.18.rest_2_ = bf16[8,256,128]{2,1,0:T(8,128)(2,1)S(1)} collective-permute-done((bf16[8,256,128]{2,1,0:T(8,128)(2,1)}, bf16[8,256,128]{2,1,0:T(8,128)(2,1)S(1)}, u32[]{:S(2)}, u32[]{:S(2)}) %collective-permute-start.18) | collective-permute-done | bytes 524320 | tf_op jit(solution)/shard_map/ppermute | solution.py:506
  256.1 2.8 query_grad.1
  259.0 3.5 %all-to-all-start.4 = ((bf16[4,256,256]{2,1,0:T(8,128)(2,1)}), bf16[4,256,256]{2,1,0:T(8,128)(2,1)S(1)}, u32[]{:S(2)}, u32[]{:S(2)}) async-start(bf16[4,256,256]{2,1,0:T(8,128)(2,1)} %bitcast.60), calls=%async_computation.4 | async-start | bytes 1048576 | tf_op jit(solution)/shard_map/all_to_all | solution.py:509
  262.7 1.9 collective-permute-start.23
  264.7 0.9 copy.45
  266.4 3.3 %collective-permute-done.21 = bf16[256,256]{1,0:T(8,128)(2,1)S(1)} collective-permute-done((bf16[256,256]{1,0:T(8,128)(2,1)S(1)}, bf16[256,256]{1,0:T(8,128)(2,1)S(1)}, u32[]{:S(2)}, u32[]{:S(2)}) %collective-permute-start.21) | collective-permute-done | bytes 131104 | tf_op jit(solution)/shard_map/ppermute | solution.py:506
  269.7 5.5 %collective-permute-done.22 = bf16[256,256]{1,0:T(8,128)(2,1)S(1)} collective-permute-done((bf16[256,256]{1,0:T(8,128)(2,1)S(1)}, bf16[256,256]{1,0:T(8,128)(2,1)S(1)}, u32[]{:S(2)}, u32[]{:S(2)}) %collective-permute-start.22) | collective-permute-done | bytes 131104 | tf_op jit(solution)/shard_map/ppermute | solution.py:506
  275.9 0.9 copy.44
  (97 shorter events, 13.9 us)
Async XLA Ops:
  7.2 56.8 %copy-start.3 = (bf16[256,1024]{1,0:T(8,128)(2,1)S(1)}, bf16[256,1024]{1,0:T(8,128)(2,1)}, u32[]{:S(2)}) copy-start(bf16[256,1024]{1,0:T(8,128)(2,1)} %param.10) | copy-start | bytes 1572868
  7.2 63.9 %copy-start.18 = (f32[16]{0:T(128)S(1)}, f32[16]{0:T(128)}, u32[]{:S(2)}) copy-start(f32[16]{0:T(128)} %param.15) | copy-start | bytes 196
  21.4 61.3 %copy-start.4 = (bf16[4,256,256]{2,1,0:T(8,128)(2,1)}, bf16[4,256,256]{2,1,0:T(8,128)(2,1)S(1)}, u32[]{:S(2)}) copy-start(bf16[4,256,256]{2,1,0:T(8,128)(2,1)S(1)} %all_to_all.35.q_ref.rest_0_) | copy-start | bytes 1572868
  21.4 24.7 %collective-permute-start.4 = (bf16[256,2048]{1,0:T(8,128)(2,1)}, bf16[256,2048]{1,0:T(8,128)(2,1)S(1)}, u32[]{:S(2)}, u32[]{:S(2)}) collective-permute-start(bf16[256,2048]{1,0:T(8,128)(2,1)} %rest_0_.1), channel_id=1, source_target_pairs={{0,2},{1,3},{2,0},{3,1},{4,6},{5,7},{6,4},{7,5},{8,10},{9,11},{10,... | collective-permute-start | bytes 3145736 | tf_op jit(solution)/shard_map/ppermute | solution.py:456
  21.8 78.6 %collective-permute-start.6 = (bf16[4096,256]{1,0:T(8,128)(2,1)}, bf16[4096,256]{1,0:T(8,128)(2,1)}, u32[]{:S(2)}, u32[]{:S(2)}) collective-permute-start(bf16[4096,256]{1,0:T(8,128)(2,1)} %k_own.3), channel_id=1, source_target_pairs={{0,4},{4,0},{8,12},{12,8},{16,20},{20,16},{24,28},{28,24},{1,5},{5... | collective-permute-start | bytes 6291464 | tf_op jit(solution)/shard_map/ppermute | solution.py:515
  23.3 90.9 %collective-permute-start.7 = (bf16[4096,256]{1,0:T(8,128)(2,1)}, bf16[4096,256]{1,0:T(8,128)(2,1)}, u32[]{:S(2)}, u32[]{:S(2)}) collective-permute-start(bf16[4096,256]{1,0:T(8,128)(2,1)} %v_own.3), channel_id=1, source_target_pairs={{0,4},{4,0},{8,12},{12,8},{16,20},{20,16},{24,28},{28,24},{1,5},{5... | collective-permute-start | bytes 6291464 | tf_op jit(solution)/shard_map/ppermute | solution.py:516
  24.9 16.9 %collective-permute-start = (bf16[4,256,256]{2,1,0:T(8,128)(2,1)S(1)}, bf16[4,256,256]{2,1,0:T(8,128)(2,1)}, u32[]{:S(2)}, u32[]{:S(2)}) collective-permute-start(bf16[4,256,256]{2,1,0:T(8,128)(2,1)S(1)} %all_to_all.35.q_ref.rest_0_), channel_id=1, source_target_pairs={{0,8},{4,12},{8,16},{12,20},{16,24},{20,28},{24,0},{28,4},{1,9},{5... | collective-permute-start | bytes 1572872 | tf_op jit(solution)/shard_map/ppermute | solution.py:506
  27.2 35.1 %collective-permute-start.1 = (bf16[4,256,256]{2,1,0:T(8,128)(2,1)S(1)}, bf16[4,256,256]{2,1,0:T(8,128)(2,1)}, u32[]{:S(2)}, u32[]{:S(2)}) collective-permute-start(bf16[4,256,256]{2,1,0:T(8,128)(2,1)S(1)} %all_to_all.35.q_ref.rest_0_), channel_id=1, source_target_pairs={{0,16},{4,20},{8,24},{12,28},{16,0},{20,4},{24,8},{28,12},{1,17},{... | collective-permute-start | bytes 1572872 | tf_op jit(solution)/shard_map/ppermute | solution.py:506
  41.8 35.3 %collective-permute-start.3 = (bf16[256,2048]{1,0:T(8,128)(2,1)}, bf16[256,2048]{1,0:T(8,128)(2,1)S(1)}, u32[]{:S(2)}, u32[]{:S(2)}) collective-permute-start(bf16[256,2048]{1,0:T(8,128)(2,1)} %rest_0_.1), channel_id=1, source_target_pairs={{0,1},{1,0},{2,3},{3,2},{4,5},{5,4},{6,7},{7,6},{8,9},{9,8},{10,11... | collective-permute-start | bytes 3145736 | tf_op jit(solution)/shard_map/ppermute | solution.py:457
  46.2 31.0 %copy-start = (bf16[256,2048]{1,0:T(8,128)(2,1)}, bf16[256,2048]{1,0:T(8,128)(2,1)S(1)}, u32[]{:S(2)}) copy-start(bf16[256,2048]{1,0:T(8,128)(2,1)S(1)} %collective-permute-done.4.rest_2_) | copy-start | bytes 3145732
  46.2 30.9 %collective-permute-start.5 = (bf16[256,2048]{1,0:T(8,128)(2,1)S(1)}, bf16[256,2048]{1,0:T(8,128)(2,1)}, u32[]{:S(2)}, u32[]{:S(2)}) collective-permute-start(bf16[256,2048]{1,0:T(8,128)(2,1)S(1)} %collective-permute-done.4.rest_2_), channel_id=1, source_target_pairs={{0,1},{1,0},{2,3},{3,2},{4,5},{5,4},{6,7},{7,6},{8,9},{9,8},{10,11... | collective-permute-start | bytes 3145736 | tf_op jit(solution)/shard_map/ppermute | solution.py:458
  48.4 16.4 %all-to-all-start.2 = ((bf16[4,256,256]{2,1,0:T(8,128)(2,1)}), bf16[4,256,256]{2,1,0:T(8,128)(2,1)}, u32[]{:S(2)}, u32[]{:S(2)}) async-start(bf16[4,256,256]{2,1,0:T(8,128)(2,1)} %bitcast.50), calls=%async_computation.2 | async-start | bytes 1048576 | tf_op jit(solution)/shard_map/all_to_all | solution.py:509
  62.3 14.8 %collective-permute-start.2 = (bf16[4,256,256]{2,1,0:T(8,128)(2,1)S(1)}, bf16[4,256,256]{2,1,0:T(8,128)(2,1)}, u32[]{:S(2)}, u32[]{:S(2)}) collective-permute-start(bf16[4,256,256]{2,1,0:T(8,128)(2,1)S(1)} %all_to_all.35.q_ref.rest_0_), channel_id=1, source_target_pairs={{0,24},{4,28},{8,0},{12,4},{16,8},{20,12},{24,16},{28,20},{1,25},{... | collective-permute-start | bytes 1572872 | tf_op jit(solution)/shard_map/ppermute | solution.py:506
  64.8 12.3 %all-to-all-start.1 = ((bf16[4,256,256]{2,1,0:T(8,128)(2,1)}), bf16[4,256,256]{2,1,0:T(8,128)(2,1)S(1)}, u32[]{:S(2)}, u32[]{:S(2)}) async-start(bf16[4,256,256]{2,1,0:T(8,128)(2,1)} %bitcast.52), calls=%async_computation.1 | async-start | bytes 1048576 | tf_op jit(solution)/shard_map/all_to_all | solution.py:509
  68.3 161.3 %all-gather.2.cloned.1.call-start = ((), (), s32[]{:S(2)}) async-start(), calls=%async_computation.7 | async-start | bytes 5242880 | tf_op jit(solution)/shard_map/all_gather | solution.py:541
  77.1 12.8 %copy-start.5 = (bf16[4,256,256]{2,1,0:T(8,128)(2,1)}, bf16[4,256,256]{2,1,0:T(8,128)(2,1)S(1)}, u32[]{:S(2)}) copy-start(bf16[4,256,256]{2,1,0:T(8,128)(2,1)S(1)} %all-to-all-done.1) | copy-start | bytes 1572868
  77.1 1.0 copy-start.1
  82.8 58.8 %collective-permute-start.10 = (bf16[4,256,256]{2,1,0:T(8,128)(2,1)}, bf16[4,256,256]{2,1,0:T(8,128)(2,1)S(1)}, u32[]{:S(2)}, u32[]{:S(2)}) collective-permute-start(bf16[4,256,256]{2,1,0:T(8,128)(2,1)} %attention_grad.1.rest_0_.rest_4_), channel_id=1, source_target_pairs={{0,24},{4,28},{8,0},{12,4},{16,8},{20,12},{24,16},{28,20},{1,25},{... | collective-permute-start | bytes 1572872 | tf_op jit(solution)/shard_map/ppermute | solution.py:506
  83.9 57.6 %collective-permute-start.8 = (bf16[4,256,256]{2,1,0:T(8,128)(2,1)}, bf16[4,256,256]{2,1,0:T(8,128)(2,1)S(1)}, u32[]{:S(2)}, u32[]{:S(2)}) collective-permute-start(bf16[4,256,256]{2,1,0:T(8,128)(2,1)} %attention_grad.1.rest_0_.rest_4_), channel_id=1, source_target_pairs={{0,8},{4,12},{8,16},{12,20},{16,24},{20,28},{24,0},{28,4},{1,9},{5... | collective-permute-start | bytes 1572872 | tf_op jit(solution)/shard_map/ppermute | solution.py:506
  85.7 55.9 %collective-permute-start.9 = (bf16[4,256,256]{2,1,0:T(8,128)(2,1)}, bf16[4,256,256]{2,1,0:T(8,128)(2,1)S(1)}, u32[]{:S(2)}, u32[]{:S(2)}) collective-permute-start(bf16[4,256,256]{2,1,0:T(8,128)(2,1)} %attention_grad.1.rest_0_.rest_4_), channel_id=1, source_target_pairs={{0,16},{4,20},{8,24},{12,28},{16,0},{20,4},{24,8},{28,12},{1,17},{... | collective-permute-start | bytes 1572872 | tf_op jit(solution)/shard_map/ppermute | solution.py:506
  132.7 73.0 %collective-permute-start.14 = (bf16[8,256,128]{2,1,0:T(8,128)(2,1)}, bf16[8,256,128]{2,1,0:T(8,128)(2,1)S(1)}, u32[]{:S(2)}, u32[]{:S(2)}) collective-permute-start(bf16[8,256,128]{2,1,0:T(8,128)(2,1)} %get-tuple-element.70), channel_id=1, source_target_pairs={{0,24},{4,28},{8,0},{12,4},{16,8},{20,12},{24,16},{28,20},{1,25},{... | collective-permute-start | bytes 1572872 | tf_op jit(solution)/shard_map/ppermute | solution.py:506
  135.8 69.9 %collective-permute-start.15 = (bf16[8,256,128]{2,1,0:T(8,128)(2,1)}, bf16[8,256,128]{2,1,0:T(8,128)(2,1)S(1)}, u32[]{:S(2)}, u32[]{:S(2)}) collective-permute-start(bf16[8,256,128]{2,1,0:T(8,128)(2,1)} %get-tuple-element.71), channel_id=1, source_target_pairs={{0,16},{4,20},{8,24},{12,28},{16,0},{20,4},{24,8},{28,12},{1,17},{... | collective-permute-start | bytes 1572872 | tf_op jit(solution)/shard_map/ppermute | solution.py:506
  141.5 0.8 copy-start.11
  141.6 1.0 copy-start.12
  141.6 1.1 copy-start.13
  146.5 29.6 %copy-start.8 = (bf16[8,256,128]{2,1,0:T(8,128)(2,1)S(1)}, bf16[8,256,128]{2,1,0:T(8,128)(2,1)}, u32[]{:S(2)}) copy-start(bf16[8,256,128]{2,1,0:T(8,128)(2,1)} %get-tuple-element.72) | copy-start | bytes 1572868
  146.5 29.5 %collective-permute-start.11 = (f32[4,8,2,512]{3,2,1,0:T(2,128)}, f32[4,8,2,512]{3,2,1,0:T(2,128)S(1)}, u32[]{:S(2)}, u32[]{:S(2)}) collective-permute-start(f32[4,8,2,512]{3,2,1,0:T(2,128)} %statistics.1.rest_8_.rest_0_.rest_4_), channel_id=1, source_target_pairs={{0,8},{4,12},{8,16},{12,20},{16,24},{20,28},{24,0},{28,4},{1,9},{5... | collective-permute-start | bytes 393224 | tf_op jit(solution)/shard_map/ppermute | solution.py:506
  146.5 49.3 %collective-permute-start.12 = (f32[4,8,2,512]{3,2,1,0:T(2,128)}, f32[4,8,2,512]{3,2,1,0:T(2,128)S(1)}, u32[]{:S(2)}, u32[]{:S(2)}) collective-permute-start(f32[4,8,2,512]{3,2,1,0:T(2,128)} %statistics.1.rest_8_.rest_0_.rest_4_), channel_id=1, source_target_pairs={{0,16},{4,20},{8,24},{12,28},{16,0},{20,4},{24,8},{28,12},{1,17},{... | collective-permute-start | bytes 393224 | tf_op jit(solution)/shard_map/ppermute | solution.py:506
  148.0 47.8 %collective-permute-start.13 = (f32[4,8,2,512]{3,2,1,0:T(2,128)}, f32[4,8,2,512]{3,2,1,0:T(2,128)S(1)}, u32[]{:S(2)}, u32[]{:S(2)}) collective-permute-start(f32[4,8,2,512]{3,2,1,0:T(2,128)} %statistics.1.rest_8_.rest_0_.rest_4_), channel_id=1, source_target_pairs={{0,24},{4,28},{8,0},{12,4},{16,8},{20,12},{24,16},{28,20},{1,25},{... | collective-permute-start | bytes 393224 | tf_op jit(solution)/shard_map/ppermute | solution.py:506
  176.1 19.8 %copy-start.15 = (f32[4,8,2,512]{3,2,1,0:T(2,128)}, f32[4,8,2,512]{3,2,1,0:T(2,128)S(1)}, u32[]{:S(2)}) copy-start(f32[4,8,2,512]{3,2,1,0:T(2,128)S(1)} %collective-permute-done.11.rest_1_.rest_7_) | copy-start | bytes 393220
  176.1 29.6 %collective-permute-start.16 = (bf16[8,256,128]{2,1,0:T(8,128)(2,1)S(1)}, bf16[8,256,128]{2,1,0:T(8,128)(2,1)S(1)}, u32[]{:S(2)}, u32[]{:S(2)}) collective-permute-start(bf16[8,256,128]{2,1,0:T(8,128)(2,1)S(1)} %copy-done.8), channel_id=1, source_target_pairs={{0,8},{4,12},{8,16},{12,20},{16,24},{20,28},{24,0},{28,4},{1,9},{5... | collective-permute-start | bytes 1572872 | tf_op jit(solution)/shard_map/ppermute | solution.py:506
  201.6 12.3 %all-to-all-start.5 = ((bf16[4,256,256]{2,1,0:T(8,128)(2,1)}), bf16[4,256,256]{2,1,0:T(8,128)(2,1)S(1)}, u32[]{:S(2)}, u32[]{:S(2)}) async-start(bf16[4,256,256]{2,1,0:T(8,128)(2,1)} %bitcast.14), calls=%async_computation.5 | async-start | bytes 1048576 | tf_op jit(solution)/shard_map/all_to_all | solution.py:509
  205.7 3.5 %copy-start.6 = (bf16[8,256,128]{2,1,0:T(8,128)(2,1)}, bf16[8,256,128]{2,1,0:T(8,128)(2,1)S(1)}, u32[]{:S(2)}) copy-start(bf16[8,256,128]{2,1,0:T(8,128)(2,1)S(1)} %collective-permute-done.14.rest_1_) | copy-start | bytes 1572868
  205.7 3.5 %copy-start.7 = (bf16[8,256,128]{2,1,0:T(8,128)(2,1)}, bf16[8,256,128]{2,1,0:T(8,128)(2,1)S(1)}, u32[]{:S(2)}) copy-start(bf16[8,256,128]{2,1,0:T(8,128)(2,1)S(1)} %collective-permute-done.15.rest_2_) | copy-start | bytes 1572868
  205.7 0.9 copy-start.14
  205.7 28.3 %collective-permute-start.17 = (bf16[8,256,128]{2,1,0:T(8,128)(2,1)}, bf16[8,256,128]{2,1,0:T(8,128)(2,1)S(1)}, u32[]{:S(2)}, u32[]{:S(2)}) collective-permute-start(bf16[8,256,128]{2,1,0:T(8,128)(2,1)} %get-tuple-element.80), channel_id=1, source_target_pairs={{0,24},{4,28},{8,0},{12,4},{16,8},{20,12},{24,16},{28,20},{1,25},{... | collective-permute-start | bytes 1572872 | tf_op jit(solution)/shard_map/ppermute | solution.py:506
  206.6 48.8 %collective-permute-start.18 = (bf16[8,256,128]{2,1,0:T(8,128)(2,1)}, bf16[8,256,128]{2,1,0:T(8,128)(2,1)S(1)}, u32[]{:S(2)}, u32[]{:S(2)}) collective-permute-start(bf16[8,256,128]{2,1,0:T(8,128)(2,1)} %get-tuple-element.81), channel_id=1, source_target_pairs={{0,16},{4,20},{8,24},{12,28},{16,0},{20,4},{24,8},{28,12},{1,17},{... | collective-permute-start | bytes 1572872 | tf_op jit(solution)/shard_map/ppermute | solution.py:506
  209.2 46.2 %collective-permute-start.19 = (bf16[8,256,128]{2,1,0:T(8,128)(2,1)}, bf16[8,256,128]{2,1,0:T(8,128)(2,1)}, u32[]{:S(2)}, u32[]{:S(2)}) collective-permute-start(bf16[8,256,128]{2,1,0:T(8,128)(2,1)} %get-tuple-element.82), channel_id=1, source_target_pairs={{0,8},{4,12},{8,16},{12,20},{16,24},{20,28},{24,0},{28,4},{1,9},{5... | collective-permute-start | bytes 1572872 | tf_op jit(solution)/shard_map/ppermute | solution.py:506
  213.8 12.3 %all-to-all-start.3 = ((bf16[4,256,256]{2,1,0:T(8,128)(2,1)}), bf16[4,256,256]{2,1,0:T(8,128)(2,1)S(1)}, u32[]{:S(2)}, u32[]{:S(2)}) async-start(bf16[4,256,256]{2,1,0:T(8,128)(2,1)} %bitcast.63), calls=%async_computation.3 | async-start | bytes 1048576 | tf_op jit(solution)/shard_map/all_to_all | solution.py:509
  223.1 39.3 %collective-permute-start.20 = (bf16[4,256,256]{2,1,0:T(8,128)(2,1)}, bf16[4,256,256]{2,1,0:T(8,128)(2,1)S(1)}, u32[]{:S(2)}, u32[]{:S(2)}) collective-permute-start(bf16[4,256,256]{2,1,0:T(8,128)(2,1)} %get-tuple-element.92), channel_id=1, source_target_pairs={{0,4},{4,0},{8,12},{12,8},{16,20},{20,16},{24,28},{28,24},{1,5},{5... | collective-permute-start | bytes 1572872 | tf_op jit(solution)/shard_map/ppermute | solution.py:722
  226.1 32.8 %all-to-all-start.6 = ((bf16[4,256,256]{2,1,0:T(8,128)(2,1)}), bf16[4,256,256]{2,1,0:T(8,128)(2,1)S(1)}, u32[]{:S(2)}, u32[]{:S(2)}) async-start(bf16[4,256,256]{2,1,0:T(8,128)(2,1)} %bitcast.16), calls=%async_computation.6 | async-start | bytes 1048576 | tf_op jit(solution)/shard_map/all_to_all | solution.py:509
  234.1 22.1 %copy-start.9 = (bf16[8,256,128]{2,1,0:T(8,128)(2,1)}, bf16[8,256,128]{2,1,0:T(8,128)(2,1)S(1)}, u32[]{:S(2)}) copy-start(bf16[8,256,128]{2,1,0:T(8,128)(2,1)S(1)} %collective-permute-done.17.rest_1_) | copy-start | bytes 1572868
  255.3 0.8 copy-start.10
  256.1 6.3 %copy-start.2 = (bf16[4,256,256]{2,1,0:T(8,128)(2,1)S(1)}, bf16[4,256,256]{2,1,0:T(8,128)(2,1)}, u32[]{:S(2)}) copy-start(bf16[4,256,256]{2,1,0:T(8,128)(2,1)} %get-tuple-element.91) | copy-start | bytes 1572868
  259.0 17.0 %all-to-all-start.4 = ((bf16[4,256,256]{2,1,0:T(8,128)(2,1)}), bf16[4,256,256]{2,1,0:T(8,128)(2,1)S(1)}, u32[]{:S(2)}, u32[]{:S(2)}) async-start(bf16[4,256,256]{2,1,0:T(8,128)(2,1)} %bitcast.60), calls=%async_computation.4 | async-start | bytes 1048576 | tf_op jit(solution)/shard_map/all_to_all | solution.py:509
  262.6 7.1 %collective-permute-start.21 = (bf16[256,256]{1,0:T(8,128)(2,1)S(1)}, bf16[256,256]{1,0:T(8,128)(2,1)S(1)}, u32[]{:S(2)}, u32[]{:S(2)}) collective-permute-start(bf16[256,256]{1,0:T(8,128)(2,1)S(1)} %get-tuple-element.94), channel_id=1, source_target_pairs={{0,24},{4,28},{8,0},{12,4},{16,8},{20,12},{24,16},{28,20},{1,25},{... | collective-permute-start | bytes 393224 | tf_op jit(solution)/shard_map/ppermute | solution.py:506
  262.7 12.5 %collective-permute-start.22 = (bf16[256,256]{1,0:T(8,128)(2,1)S(1)}, bf16[256,256]{1,0:T(8,128)(2,1)S(1)}, u32[]{:S(2)}, u32[]{:S(2)}) collective-permute-start(bf16[256,256]{1,0:T(8,128)(2,1)S(1)} %get-tuple-element.95), channel_id=1, source_target_pairs={{0,16},{4,20},{8,24},{12,28},{16,0},{20,4},{24,8},{28,12},{1,17},{... | collective-permute-start | bytes 393224 | tf_op jit(solution)/shard_map/ppermute | solution.py:506
  262.7 12.4 %collective-permute-start.23 = (bf16[256,256]{1,0:T(8,128)(2,1)S(1)}, bf16[256,256]{1,0:T(8,128)(2,1)S(1)}, u32[]{:S(2)}, u32[]{:S(2)}) collective-permute-start(bf16[256,256]{1,0:T(8,128)(2,1)S(1)} %get-tuple-element.96), channel_id=1, source_target_pairs={{0,8},{4,12},{8,16},{12,20},{16,24},{20,28},{24,0},{28,4},{1,9},{5... | collective-permute-start | bytes 393224 | tf_op jit(solution)/shard_map/ppermute | solution.py:506
  (2 other events, 1.4 us)
Sparse Core Ops, SparseCore 0:
  71.9 37.1 all-gather.1
